TPU v7x, 32 devices: a whole 2x2x4 slice. The times are simulated.
32 devices in a mesh: row: 4 (over x, core), col: 8 (over z, y).
Axes of the slice: x: 2, y: 2, z: 4, core: 2. Of those that a mesh axis runs over, the one named last changes fastest.
Arguments:
- inverse_first: float32 [6144, 6144], P('col', 'row'), as said below
- inverse_second: float32 [5120, 5120], P('col', 'row'), as said below
- inverse_third: float32 [4096, 4096], P('col', 'row'), as said below
- inverse_fourth: float32 [3072, 3072], P('col', 'row'), as said below
- coupling_first: float32 [1024, 6144], P('row', 'col'), may hold values from -0.078125 to 0.078125
- coupling_second: float32 [1024, 5120], P('row', 'col'), may hold values from -0.078125 to 0.078125
- coupling_third: float32 [1024, 4096], P('row', 'col'), may hold values from -0.09375 to 0.09375
- coupling_fourth: float32 [1024, 3072], P('row', 'col'), may hold values from -0.109375 to 0.109375
- inverse_root: float32 [16384, 16384], P('col', 'row'), as said below
- loads_first: float32 [6144, 512], P('row'), may hold values from -6 to 6
- loads_second: float32 [5120, 512], P('row'), may hold values from -6 to 6
- loads_third: float32 [4096, 512], P('row'), may hold values from -6 to 6
- loads_fourth: float32 [3072, 512], P('row'), may hold values from -6 to 6
- loads_root: float32 [16384, 512], P('row'), may hold values from -6 to 6
- target_blocks: int32 [4, 8], replicated, may hold values from 0 to 127, as said below
Outputs:
- solved_first: float32 [6144, 512], P(('row', 'col'))
- solved_second: float32 [5120, 512], P(('row', 'col'))
- solved_third: float32 [4096, 512], P(('row', 'col'))
- solved_fourth: float32 [3072, 512], P(('row', 'col'))
- solved_root: float32 [16384, 512], P('col')
Inputs may be any that keep to these rules, and one draw needn't show every extreme that they name: `target_blocks`: within each row the entries are distinct; entry [k, j] is the root block of 128 rows that receives block j of the k-th child's coupling rows. Different children may share root blocks. `inverse_first`: lower triangular with a positive diagonal. `inverse_second`: lower triangular with a positive diagonal. `inverse_third`: lower triangular with a positive diagonal. `inverse_fourth`: lower triangular with a positive diagonal. `inverse_root`: Symmetric.
All inputs are finite; a program needn't handle non-finite values.
Results may differ from a plain program's by a relative error of at most 0.0001.
Values sent between devices are 32-bit elements; how exact they have to be, the bound alone decides.
No kernel may reach another device: no remote copies, remote signals or barrier semaphores. Data moves between devices by JAX's collectives and lax.ppermute only.
A program may use at most 192 MiB of HBM per device.

v0:
```python
import jax
import jax.numpy as jnp
from jax import lax
from jax.sharding import PartitionSpec as P

BLOCK = 128


def product(matrix, vector):
    return jnp.dot(
        matrix, vector, precision=lax.Precision.HIGHEST, preferred_element_type=jnp.float32
    )


def transposed(matrix, vector):
    return lax.dot_general(
        matrix,
        vector,
        (((0,), (0,)), ((), ())),
        precision=lax.Precision.HIGHEST,
        preferred_element_type=jnp.float32,
    )


def local(
    inverse_first,
    inverse_second,
    inverse_third,
    inverse_fourth,
    coupling_first,
    coupling_second,
    coupling_third,
    coupling_fourth,
    inverse_root,
    loads_first,
    loads_second,
    loads_third,
    loads_fourth,
    loads_root,
    target_blocks,
):
    inverses = [inverse_first, inverse_second, inverse_third, inverse_fourth]
    couplings = [coupling_first, coupling_second, coupling_third, coupling_fourth]
    sources = [loads_first, loads_second, loads_third, loads_fourth]
    first_terms = [product(weight, source) for weight, source in zip(inverses, sources)]
    forward = lax.psum((first_terms[0], first_terms[1], first_terms[2], first_terms[3]), "row")
    partial_value = jnp.stack(
        [product(weight, solved) for weight, solved in zip(couplings, forward)]
    )
    columns = loads_root.shape[1]
    count = target_blocks.shape[1]
    root_rows = loads_root.shape[0]
    owned_count = root_rows // BLOCK
    owned_ids = lax.axis_index("row") * owned_count + jnp.arange(owned_count, dtype=jnp.int32)
    spread_map = (target_blocks[:, None, :] == owned_ids[None, :, None]).astype(jnp.float32)
    summed = lax.psum(partial_value, "col")
    blocks = lax.all_gather(summed, "row", axis=1, tiled=True).reshape(4, count, BLOCK * columns)
    placed = jnp.einsum(
        "kij,kjm->im",
        spread_map,
        blocks,
        precision=lax.Precision.HIGHEST,
        preferred_element_type=jnp.float32,
    )
    update = placed.reshape(root_rows, columns)
    shifted = loads_root - update
    solved_root = lax.psum(product(inverse_root, shifted), "row")
    local_blocks = solved_root.shape[0] // BLOCK
    held_ids = lax.axis_index("col") * local_blocks + jnp.arange(local_blocks, dtype=jnp.int32)
    per_row = partial_value.shape[1] // BLOCK
    wanted = lax.dynamic_slice_in_dim(target_blocks, lax.axis_index("row") * per_row, per_row, 1)
    pick_map = (wanted[:, :, None] == held_ids[None, None, :]).astype(jnp.float32)
    picked = jnp.einsum(
        "kji,im->kjm",
        pick_map,
        solved_root.reshape(local_blocks, BLOCK * columns),
        precision=lax.Precision.HIGHEST,
        preferred_element_type=jnp.float32,
    )
    picked = lax.psum(picked.reshape(4, per_row * BLOCK, columns), "col")
    back_terms = [transposed(couplings[child], picked[child]) for child in range(4)]
    corrections = lax.psum((back_terms[0], back_terms[1], back_terms[2], back_terms[3]), "row")
    finals = [
        transposed(weight, solved - fixed)
        for weight, solved, fixed in zip(inverses, forward, corrections)
    ]
    solved = (
        lax.psum_scatter(finals[0], "col", scatter_dimension=0, tiled=True),
        lax.psum_scatter(finals[1], "col", scatter_dimension=0, tiled=True),
        lax.psum_scatter(finals[2], "col", scatter_dimension=0, tiled=True),
        lax.psum_scatter(finals[3], "col", scatter_dimension=0, tiled=True),
    )
    return (solved[0], solved[1], solved[2], solved[3], solved_root)


def solution(mesh):
    placed = (
        P("col", "row"),
        P("col", "row"),
        P("col", "row"),
        P("col", "row"),
        P("row", "col"),
        P("row", "col"),
        P("row", "col"),
        P("row", "col"),
        P("col", "row"),
        P("row", None),
        P("row", None),
        P("row", None),
        P("row", None),
        P("row", None),
        P(),
    )
    return jax.shard_map(
        local,
        mesh=mesh,
        in_specs=placed,
        out_specs=(
            P(("row", "col"), None),
            P(("row", "col"), None),
            P(("row", "col"), None),
            P(("row", "col"), None),
            P("col", None),
        ),
        check_vma=False,
    )
```

profile of v0, /device:TPU:0, one launch (start us, length us, event | category | flops | bytes accessed | tf_op | source)
XLA Modules:
  0.0 1064.5 jit_solution(3771818948653831838)
XLA Ops:
  12.1 6.9 fusion.16
  19.0 6.4 fusion.15
  25.4 9.1 fusion.14
  34.6 97.4 %all-reduce.16.cloned.1.call-done = (f32[768,512]{1,0:T(8,128)}, f32[384,512]{1,0:T(8,128)}, f32[512,512]{1,0:T(8,128)}, f32[640,512]{1,0:T(8,128)}) async-done(((f32[768,512]{1,0:T(8,128)}, f32[384,512]{1,0:T(8,128)}, f32[512,512]{1,0:T(8,128)}, f32[640,512]{1,0:T(8,128)}), (f32[768,512]{1,0:T(8,128)}, f32[384,512]{1,0:T(8,128)}, f32[512,512]{1,0:T(8,128)}, ...) | async-done | bytes 4718608 | tf_op jit(solution)/shard_map/psum | solution.py:46
  143.5 102.1 %all-reduce.8.cloned.1.call-done = f32[4,256,512]{1,2,0:T(8,128)} async-done(((f32[4,256,512]{1,2,0:T(8,128)}), f32[4,256,512]{1,2,0:T(8,128)}) %all-reduce.8.cloned.1.call-update) | async-done | bytes 2097168 | tf_op jit(solution)/shard_map/psum | solution.py:56
  245.7 59.5 %all-gather.2.cloned.1.call-done = f32[4,1024,512]{1,2,0:T(8,128)} async-done(((f32[4,256,512]{1,2,0:T(8,128)}), f32[4,1024,512]{1,2,0:T(8,128)}) %all-gather.2.cloned.1.call-update) | async-done | bytes 8388624 | tf_op jit(solution)/shard_map/all_gather | solution.py:57
  305.2 8.7 copy.36
  313.9 7.5 reshape.32
  321.5 8.5 convolution_bitcast_fusion
  330.0 7.5 reshape.33
  337.5 111.1 %fusion.2 = f32[2048,512]{0,1:T(8,128)} fusion(f32[2048,4096]{1,0:T(8,128)} %param.23, f32[4096,512]{1,0:T(8,128)} %param.28, f32[4096,512]{1,0:T(8,128)} %reshape.33), kind=kOutput, calls=%fused_computation.4 | convolution fusion | flops 51541704704 | bytes 54525952 | tf_op jit(solution)/shard_map/dot_general | solution.py:10
  449.0 85.4 %all-reduce.10.cloned.1.call-done = f32[2048,512]{0,1:T(8,128)} async-done(((f32[2048,512]{0,1:T(8,128)}), f32[2048,512]{0,1:T(8,128)}) %all-reduce.10.cloned.1.call-update) | async-done | bytes 4194320 | tf_op jit(solution)/shard_map/psum | solution.py:67
  534.4 5.3 copy.37
  543.6 6.7 fusion.12
  555.0 102.1 %all-reduce.12.cloned.1.call-done = f32[4,256,512]{2,1,0:T(8,128)} async-done(((f32[4,256,512]{2,1,0:T(8,128)}), f32[4,256,512]{2,1,0:T(8,128)}) %all-reduce.12.cloned.1.call-update) | async-done | bytes 2097168 | tf_op jit(solution)/shard_map/psum | solution.py:80
  668.9 94.0 %all-reduce.14.cloned.1.call-done = (f32[768,512]{1,0:T(8,128)}, f32[640,512]{1,0:T(8,128)}, f32[512,512]{1,0:T(8,128)}, f32[384,512]{1,0:T(8,128)}) async-done(((f32[768,512]{1,0:T(8,128)}, f32[640,512]{1,0:T(8,128)}, f32[512,512]{1,0:T(8,128)}, f32[384,512]{1,0:T(8,128)}), (f32[768,512]{1,0:T(8,128)}, f32[640,512]{1,0:T(8,128)}, f32[512,512]{1,0:T(8,128)}, ...) | async-done | bytes 4718608 | tf_op jit(solution)/shard_map/psum | solution.py:82
  762.9 7.1 convolution_bitcast_fusion.3
  770.1 5.7 convolution_bitcast_fusion.5
  778.9 9.1 convolution_bitcast_fusion.1
  791.5 12.2 %convolution_bitcast_fusion.2 = f32[1536,512]{0,1:T(8,128)} fusion(f32[768,1536]{1,0:T(8,128)} %param.15, f32[768,512]{1,0:T(8,128)} %get-tuple-element.24, f32[768,512]{1,0:T(8,128)} %get-tuple-element.20), kind=kOutput, calls=%fused_computation.5 | convolution fusion | flops 7248150528 | bytes 11010048 | tf_op jit(solution)/shard_map/dot_general | solution.py:16
  807.3 31.5 %reduce-scatter.11.cloned.1.call-done = f32[128,512]{0,1:T(8,128)} async-done(((f32[1024,512]{0,1:T(8,128)}), f32[128,512]{0,1:T(8,128)}) %reduce-scatter.11.cloned.1.call-update) | async-done | bytes 262160 | tf_op jit(solution)/shard_map/reduce_scatter | solution.py:90
  840.6 66.5 %reduce-scatter.17.cloned.1.call-done = f32[96,512]{1,0:T(8,128)} async-done(((f32[768,512]{1,0:T(8,128)}), f32[96,512]{1,0:T(8,128)}) %reduce-scatter.17.cloned.1.call-update) | async-done | bytes 196624
  907.1 73.2 %reduce-scatter.15.cloned.1.call-done = f32[160,512]{1,0:T(8,128)} async-done(((f32[1280,512]{1,0:T(8,128)}), f32[160,512]{1,0:T(8,128)}) %reduce-scatter.15.cloned.1.call-update) | async-done | bytes 327696
  980.3 77.2 %reduce-scatter.13.cloned.1.call-done = f32[192,512]{1,0:T(8,128)} async-done(((f32[1536,512]{1,0:T(8,128)}), f32[192,512]{1,0:T(8,128)}) %reduce-scatter.13.cloned.1.call-update) | async-done | bytes 393232
  (72 shorter events, 49.2 us)
Async XLA Ops:
  7.2 11.8 %copy-start = (f32[640,1280]{1,0:T(8,128)S(1)}, f32[640,1280]{1,0:T(8,128)}, u32[]{:S(2)}) copy-start(f32[640,1280]{1,0:T(8,128)} %param.16) | copy-start | bytes 9830404
  7.2 124.8 %all-reduce.16.cloned.1.call-start = ((), (), s32[]{:S(2)}) async-start(), calls=%async_computation.13 | async-start | bytes 9437184 | tf_op jit(solution)/shard_map/psum | solution.py:46
  7.2 18.2 %slice-start = ((s8[4718592]{0:T(1024)(128)(4,1)}), s8[4194304]{0:T(1024)(128)(4,1)S(1)}, s32[]{:S(2)}) async-start(s8[4718592]{0:T(1024)(128)(4,1)} %bitcast.80), calls=%async_computation.14 | async-start | bytes 8388608
  12.1 6.9 copy-start.6
  12.1 13.3 %slice-start.1 = ((s8[4718592]{0:T(1024)(128)(4,1)}), s8[524288]{0:T(1024)(128)(4,1)S(1)}, s32[]{:S(2)}) async-start(s8[4718592]{0:T(1024)(128)(4,1)} %bitcast.80), calls=%async_computation.15 | async-start | bytes 1048576
  19.0 6.4 copy-start.3
  34.6 211.0 %all-reduce.8.cloned.1.call-start = ((), (), s32[]{:S(2)}) async-start(), calls=%async_computation.4 | async-start | bytes 4194304 | tf_op jit(solution)/shard_map/psum | solution.py:56
  132.0 4.4 copy-start.5
  132.0 4.4 copy-start.11
  132.0 5.9 copy-start.2
  132.0 5.9 copy-start.10
  136.4 3.3 copy-start.1
  143.5 161.8 %all-gather.2.cloned.1.call-start = ((), (), s32[]{:S(2)}) async-start(), calls=%async_computation.5 | async-start | bytes 10485760 | tf_op jit(solution)/shard_map/all_gather | solution.py:57
  245.7 288.7 %all-reduce.10.cloned.1.call-start = ((), (), s32[]{:S(2)}) async-start(), calls=%async_computation.6 | async-start | bytes 8388608 | tf_op jit(solution)/shard_map/psum | solution.py:67
  313.9 7.5 copy-start.12
  448.7 208.5 %all-reduce.12.cloned.1.call-start = ((), (), s32[]{:S(2)}) async-start(), calls=%async_computation.7 | async-start | bytes 4194304 | tf_op jit(solution)/shard_map/psum | solution.py:80
  555.0 208.0 %all-reduce.14.cloned.1.call-start = ((), (), s32[]{:S(2)}) async-start(), calls=%async_computation.12 | async-start | bytes 9437184 | tf_op jit(solution)/shard_map/psum | solution.py:82
  657.1 6.3 copy-start.8
  657.1 6.3 copy-start.9
  660.2 5.6 copy-start.4
  668.5 170.3 %reduce-scatter.11.cloned.1.call-start = ((), (), s32[]{:S(2)}) async-start(), calls=%async_computation.8 | async-start | bytes 2359296 | tf_op jit(solution)/shard_map/reduce_scatter | solution.py:90
  770.0 137.1 %reduce-scatter.17.cloned.1.call-start = ((), (), s32[]{:S(2)}) async-start(), calls=%async_computation.11 | async-start | bytes 1769472
  778.8 201.5 %reduce-scatter.15.cloned.1.call-start = ((), (), s32[]{:S(2)}) async-start(), calls=%async_computation.10 | async-start | bytes 2949120
  791.3 266.2 %reduce-scatter.13.cloned.1.call-start = ((), (), s32[]{:S(2)}) async-start(), calls=%async_computation.9 | async-start | bytes 3538944
  (1 other events, 3.3 us)
Sparse Core Ops, SparseCore 0:
  34.7 97.2 all-reduce.15
  143.6 101.9 all-reduce.7
  247.2 58.0 all-gather.1
  448.8 85.5 all-reduce.9
  555.1 102.0 all-reduce.11
  668.6 94.2 all-reduce.13
  770.2 68.5 reduce-scatter.10
  843.2 63.8 reduce-scatter.16
  911.2 69.0 reduce-scatter.14
  984.3 73.1 reduce-scatter.12
where the time goes:
time: 1070 us; the launch traced here: 1060 us
  waiting for transfers between devices  789 us (74%)
  matrix products  209 us (20%)
  local copies, waits for them, and re-layouts  49.5 us (5%)
  between operations  14.5 us (1%)
    unnamed x13, waiting for transfers between devices  217 us
    dot_general x9, matrix products, product(): jnp.dot(matrix, vector, precision=lax.Precision.HIGHEST, preferred_elemen...  148 us
    psum x1, waiting for transfers between devices, local(): picked = lax.psum(picked.reshape(4, per_row * BLOCK, columns), 'col')  102 us
    psum x1, waiting for transfers between devices, local(): summed = lax.psum(partial_value, 'col')  102 us
    psum x1, waiting for transfers between devices, local(): lax.psum((first_terms[0], first_terms[1], first_terms[2], first_terms[3])...  97.4 us
    psum x1, waiting for transfers between devices, local(): lax.psum((back_terms[0], back_terms[1], back_terms[2], back_terms[3]), 'r...  94 us
    psum x1, waiting for transfers between devices, local(): solved_root = lax.psum(product(inverse_root, shifted), 'row')  85.4 us
    all_gather x1, waiting for transfers between devices, local(): lax.all_gather(summed, 'row', axis=1, tiled=True)  59.5 us
  transfers between devices with their start and end apart: 10, of which 10 were waited for; matrix products, arithmetic and copies ran while one was open for 4% of the time, Pallas kernels for 0%

commit v1 on v0

v1 whole, which is shorter than its diff:
```python
import jax
import jax.numpy as jnp
from jax import lax
from jax.experimental import pallas as pl
from jax.experimental.pallas import tpu as pltpu
from jax.sharding import PartitionSpec as P

BLOCK = 128
AXES = ("row", "col")
PARTS = 2


def product(matrix, vector):
    return jnp.dot(
        matrix, vector, precision=lax.Precision.HIGH, preferred_element_type=jnp.float32
    )


def transposed(matrix, vector):
    return lax.dot_general(
        matrix,
        vector,
        (((0,), (0,)), ((), ())),
        precision=lax.Precision.HIGH,
        preferred_element_type=jnp.float32,
    )


def pick(array, index, axis):
    return lax.dynamic_index_in_dim(array, index, axis, keepdims=False)


class Group:
    def __init__(self, rows, cols, axis, stride, size):
        self.size = size
        self.place = lax.rem(lax.axis_index(axis) // stride, size)
        self.pairs = []
        for step in range(1, size):
            listed = []
            for r in range(rows):
                for c in range(cols):
                    old = r if axis == "row" else c
                    digit = old // stride % size
                    new = old + ((digit + step) % size - digit) * stride
                    there = (new, c) if axis == "row" else (r, new)
                    listed.append((r * cols + c, there[0] * cols + there[1]))
            self.pairs.append(listed)

    def scatter_sum(self, array, axis):
        total = pick(array, self.place, axis)
        for step in range(1, self.size):
            sent = pick(array, lax.rem(self.place + step, self.size), axis)
            total = total + lax.ppermute(sent, AXES, self.pairs[step - 1])
        return total

    def gather(self, array, axis):
        if self.size == 1:
            return jnp.expand_dims(array, axis)
        held = [array]
        for step in range(1, self.size):
            held.append(lax.ppermute(array, AXES, self.pairs[step - 1]))
        if self.size == 2:
            first = self.place == 0
            return jnp.stack(
                [jnp.where(first, held[0], held[1]), jnp.where(first, held[1], held[0])], axis
            )
        shape = array.shape[:axis] + (self.size,) + array.shape[axis:]
        out = jnp.zeros(shape, array.dtype)
        for step, value in enumerate(held):
            source = lax.rem(self.place + self.size - step, self.size)
            out = lax.dynamic_update_index_in_dim(out, value, source, axis)
        return out

    def total(self, array):
        if self.size == 2:
            return array + lax.ppermute(array, AXES, self.pairs[0])
        if self.size == 1:
            return array
        pieces = array.reshape((self.size, array.shape[0] // self.size) + array.shape[1:])
        return self.gather(self.scatter_sum(pieces, 0), 0).reshape(array.shape)


class Links:
    def __init__(self, rows, cols):
        cores = 2 if rows % 2 == 0 else 1
        near = 1
        while cols % (near * 2) == 0 and near * near * 8 <= cols * 2:
            near *= 2
        self.core = Group(rows, cols, "row", 1, cores)
        self.x = Group(rows, cols, "row", cores, rows // cores)
        self.y = Group(rows, cols, "col", 1, near)
        self.z = Group(rows, cols, "col", near, cols // near)

    def row_total(self, array):
        pieces = array.reshape((self.core.size, array.shape[0] // self.core.size, array.shape[1]))
        part = self.x.total(self.core.scatter_sum(pieces, 0))
        return self.core.gather(part, 0).reshape(array.shape)

    def col_scatter(self, array):
        size = array.shape[0] // (self.z.size * self.y.size)
        pieces = array.reshape(self.z.size, self.y.size, size, array.shape[1])
        return self.z.scatter_sum(self.y.scatter_sum(pieces, 1), 0)

    def col_gather(self, array):
        whole = self.y.gather(self.z.gather(array, 0), 1)
        return whole.reshape(-1, array.shape[-1])


def place_kernel(count, map_ref, loads_ref, blocks_ref, out_ref):
    here = pl.program_id(0)
    out_ref[...] = loads_ref[...]
    for child in range(map_ref.shape[0]):
        source = map_ref[child, here]

        @pl.when(source < count)
        def _():
            out_ref[...] -= blocks_ref[child, source]


def place(loads, blocks, slots, part, parts):
    children, count, size, width = blocks.shape
    owned = slots.shape[1]
    return pl.pallas_call(
        lambda *refs: place_kernel(count, *refs),
        grid_spec=pltpu.PrefetchScalarGridSpec(
            num_scalar_prefetch=1,
            grid=(owned,),
            in_specs=[
                pl.BlockSpec((size, width), lambda i, slots: (i, part)),
                pl.BlockSpec((children, count, size, width), lambda i, slots: (0, 0, 0, 0)),
            ],
            out_specs=pl.BlockSpec((size, width), lambda i, slots: (i, 0)),
        ),
        out_shape=jax.ShapeDtypeStruct((owned * size, width), jnp.float32),
        compiler_params=pltpu.CompilerParams(vmem_limit_bytes=40 * 2**20),
    )(slots, loads, blocks)


def take_kernel(count, ids_ref, held_ref, out_ref):
    source = ids_ref[pl.program_id(0)]
    inside = jnp.logical_and(source >= 0, source < count)

    @pl.when(inside)
    def _():
        out_ref[...] = held_ref[...]

    @pl.when(jnp.logical_not(inside))
    def _():
        out_ref[...] = jnp.zeros_like(out_ref)


def take(held, ids):
    rows, width = held.shape
    count = rows // BLOCK
    wanted = ids.shape[0]
    return pl.pallas_call(
        lambda *refs: take_kernel(count, *refs),
        grid_spec=pltpu.PrefetchScalarGridSpec(
            num_scalar_prefetch=1,
            grid=(wanted,),
            in_specs=[
                pl.BlockSpec(
                    (BLOCK, width), lambda i, ids: (jnp.clip(ids[i], 0, count - 1), 0)
                ),
            ],
            out_specs=pl.BlockSpec((BLOCK, width), lambda i, ids: (i, 0)),
        ),
        out_shape=jax.ShapeDtypeStruct((wanted * BLOCK, width), jnp.float32),
    )(ids, held)


def local(rows, cols, *arguments):
    inverses = arguments[0:4]
    couplings = arguments[4:8]
    inverse_root = arguments[8]
    sources = arguments[9:13]
    loads_root = arguments[13]
    target_blocks = arguments[14]
    links = Links(rows, cols)
    columns = loads_root.shape[1]
    parts = PARTS if columns % (PARTS * 128) == 0 else 1
    width = columns // parts
    children, count = target_blocks.shape
    per_row = couplings[0].shape[0] // BLOCK
    owned = loads_root.shape[0] // BLOCK
    held = inverse_root.shape[0] // BLOCK

    owned_ids = lax.axis_index("row") * owned + jnp.arange(owned, dtype=jnp.int32)
    same = target_blocks[:, :, None] == owned_ids[None, None, :]
    numbers = jnp.arange(count, dtype=jnp.int32)[None, :, None]
    slots = jnp.min(jnp.where(same, numbers, count), axis=1)
    mine = lax.dynamic_slice_in_dim(target_blocks, lax.axis_index("row") * per_row, per_row, 1)
    wanted = (mine - lax.axis_index("col") * held).reshape(-1)

    answers = []
    for part in range(parts):
        span = slice(part * width, (part + 1) * width)
        forward = [
            links.row_total(product(weight, source[:, span]))
            for weight, source in zip(inverses, sources)
        ]
        partial_value = jnp.concatenate(
            [product(weight, solved) for weight, solved in zip(couplings, forward)]
        )
        summed = links.col_scatter(partial_value)
        spread = links.core.gather(links.x.gather(links.col_gather(summed), 0), 1)
        blocks = spread.reshape(rows, children, per_row, BLOCK, width)
        blocks = blocks.transpose(1, 0, 2, 3, 4).reshape(children, count, BLOCK, width)
        shifted = place(loads_root, blocks, slots, part, parts)
        solved_root = links.row_total(product(inverse_root, shifted))
        picked = links.col_gather(links.col_scatter(take(solved_root, wanted)))
        picked = picked.reshape(children, per_row * BLOCK, width)
        finals = []
        for child in range(4):
            correction = links.row_total(transposed(couplings[child], picked[child]))
            final = transposed(inverses[child], forward[child] - correction)
            finals.append(links.col_scatter(final))
        answers.append(finals + [solved_root])
    return tuple(jnp.concatenate(list(pieces), axis=1) for pieces in zip(*answers))


def solution(mesh):
    rows, cols = mesh.shape["row"], mesh.shape["col"]
    matrices = [P("col", "row")] * 4 + [P("row", "col")] * 4 + [P("col", "row")]
    vectors = [P("row", None)] * 5
    return jax.shard_map(
        lambda *arguments: local(rows, cols, *arguments),
        mesh=mesh,
        in_specs=tuple(matrices + vectors + [P()]),
        out_specs=(P(AXES, None),) * 4 + (P("col", None),),
        check_vma=False,
    )
```

time: 1070 us -> 798 us (0.75)
  waiting for transfers between devices: 789 us -> 241 us
  starting transfers between devices: 0.99 us -> 139 us
  local copies, waits for them, and re-layouts: 49.5 us -> 145 us
  other arithmetic: 1.56 us -> 85.5 us
  matrix products: 209 us -> 128 us
  Pallas kernels: 0 us -> 41.3 us
  between operations: 14.5 us -> 2.71 us
    psum x5 -> x0, waiting for transfers between devices: 481 us -> none  [the longest x1 102 us: local(): picked = lax.psum(picked.reshape(4, per_row * BLOCK, columns), 'col')]
    ppermute x0 -> x122, waiting for transfers between devices: none -> 241 us  [the longest x66 98.2 us: scatter_sum(): total = total + lax.ppermute(sent, AXES, self.pairs[step - 1])]
    unnamed x13 -> x0, waiting for transfers between devices: 217 us -> none
    ppermute x0 -> x122, starting transfers between devices: none -> 139 us  [the longest x66 75.7 us: scatter_sum(): total = total + lax.ppermute(sent, AXES, self.pairs[step - 1])]
    dot_general x11 -> x18, matrix products: 164 us -> 85.7 us  [product(): jnp.dot(matrix, vector, precision=lax.Precision.HIGH, preferred_element_t...]
    all_gather x1 -> x0, waiting for transfers between devices: 59.5 us -> none  [local(): lax.all_gather(summed, 'row', axis=1, tiled=True)]
    add x2 -> x57, other arithmetic: 0.01 us -> 42.1 us  [the longest x38 29.7 us: scatter_sum(): total = total + lax.ppermute(sent, AXES, self.pairs[step - 1])]
    pallas_call x0 -> x4, Pallas kernels: none -> 41.3 us  [the longest x2 32.7 us: place(): pl.pallas_call(lambda *refs: place_kernel(count, *refs), grid_spec=pltpu....]
  transfers between devices with their start and end apart: 10 -> 122, of which waited for: 10 -> 46; matrix products, arithmetic and copies ran while one was open for 4% -> 43% of each run, Pallas kernels for 0% -> 5%
where the time goes in v1:
time: 798 us; the launch traced here: 784 us
  waiting for transfers between devices  241 us (30%)
  local copies, waits for them, and re-layouts  145 us (18%)
  starting transfers between devices  139 us (17%)
  matrix products  128 us (16%)
  other arithmetic  85.5 us (11%)
  Pallas kernels  41.3 us (5%)
    ppermute x66, waiting for transfers between devices, scatter_sum(): total = total + lax.ppermute(sent, AXES, self.pairs[step - 1])  98.2 us
    dot_general x18, matrix products, product(): jnp.dot(matrix, vector, precision=lax.Precision.HIGH, preferred_element_t...  85.7 us
    ppermute x18, waiting for transfers between devices, total(): return array + lax.ppermute(array, AXES, self.pairs[0])  79.2 us
    ppermute x66, starting transfers between devices, scatter_sum(): total = total + lax.ppermute(sent, AXES, self.pairs[step - 1])  75.7 us
    ppermute x38, waiting for transfers between devices, gather(): held.append(lax.ppermute(array, AXES, self.pairs[step - 1]))  63.8 us
    dot_general x16, matrix products, transposed(): lax.dot_general(matrix, vector, (((0,), (0,)), ((), ())), precision=lax.P...  42.6 us
    ppermute x38, starting transfers between devices, gather(): held.append(lax.ppermute(array, AXES, self.pairs[step - 1]))  37.9 us
    squeeze x38, local copies, waits for them, and re-layouts, pick(): return lax.dynamic_index_in_dim(array, index, axis, keepdims=False)  34.2 us
  transfers between devices with their start and end apart: 122, of which 46 were waited for; matrix products, arithmetic and copies ran while one was open for 43% of the time, Pallas kernels for 5%

profile of v1, /device:TPU:0, one launch (start us, length us, event | category | flops | bytes accessed | tf_op | source)
XLA Modules:
  0.0 783.8 jit_solution(15277051601175068397)
XLA Ops:
  63.7 7.0 collective-permute-done.44
  72.7 6.4 collective-permute-done.1
  79.3 8.0 %collective-permute-done.41 = f32[384,256]{1,0:T(8,128)S(1)} collective-permute-done((f32[384,256]{1,0:T(8,128)S(1)}, f32[384,256]{1,0:T(8,128)S(1)}, u32[]{:S(2)}, u32[]{:S(2)}) %collective-permute-start.41) | collective-permute-done | bytes 393248 | tf_op jit(solution)/shard_map/ppermute | solution.py:76
  93.4 11.9 %collective-permute-done.12 = f32[4,128,256]{2,1,0:T(8,128)S(1)} collective-permute-done((f32[4,128,256]{2,1,0:T(8,128)S(1)}, f32[4,128,256]{2,1,0:T(8,128)S(1)}, u32[]{:S(2)}, u32[]{:S(2)}) %collective-permute-start.12) | collective-permute-done | bytes 524320 | tf_op jit(solution)/shard_map/ppermute | solution.py:53
  144.1 6.2 collective-permute-done.19
  170.4 6.7 collective-permute-done.20
  186.2 23.2 %collective-permute-done.60 = f32[1024,256]{1,0:T(8,128)} collective-permute-done((f32[1024,256]{1,0:T(8,128)}, f32[1024,256]{1,0:T(8,128)}, u32[]{:S(2)}, u32[]{:S(2)}) %collective-permute-start.60) | collective-permute-done | bytes 1048608 | tf_op jit(solution)/shard_map/ppermute | solution.py:61
  217.3 16.5 %shard_map.182 = f32[4096,256]{1,0:T(8,128)S(1)} custom-call(s32[4,32]{1,0:T(4,128)S(1)} %select_reduce_fusion.refs_0_, f32[4096,512]{1,0:T(8,128)} %refs_1_.3, f32[4,8,128,256]{3,2,1,0:T(8,128)S(1)} %bitcast.605), custom_call_target="tpu_custom_call" | custom-call | tf_op jit(solution)/shard_map/pallas_call | solution.py:123
  235.8 32.3 %convolution_bitcast_fusion.3 = f32[2048,256]{0,1:T(8,128)} fusion(f32[4096,256]{1,0:T(8,128)} %copy-done.2, f32[2048,4096]{1,0:T(8,128)} %param.23), kind=kOutput, calls=%fused_computation.6 | convolution fusion | flops 12884901888 | bytes 39845888 | tf_op jit(solution)/shard_map/dot_general | solution.py:14
  272.1 5.8 constant_dynamic-slice_fusion.7
  285.2 16.1 %shard_map.184 = f32[4096,256]{1,0:T(8,128)S(1)} custom-call(s32[4,32]{1,0:T(4,128)S(1)} %select_reduce_fusion.refs_0_, f32[4096,512]{1,0:T(8,128)} %refs_1_.3, f32[4,8,128,256]{3,2,1,0:T(8,128)S(1)} %bitcast.604), custom_call_target="tpu_custom_call" | custom-call | tf_op jit(solution)/shard_map/pallas_call | solution.py:123
  303.4 32.4 %convolution_bitcast_fusion.2 = f32[2048,256]{0,1:T(8,128)} fusion(f32[4096,256]{1,0:T(8,128)} %copy-done.1, f32[2048,4096]{1,0:T(8,128)} %param.23), kind=kOutput, calls=%fused_computation.5 | convolution fusion | flops 12884901888 | bytes 39845888 | tf_op jit(solution)/shard_map/dot_general | solution.py:14
  339.8 5.7 constant_dynamic-slice_fusion.5
  363.2 19.0 %collective-permute-done.23 = f32[1024,256]{1,0:T(8,128)} collective-permute-done((f32[1024,256]{1,0:T(8,128)}, f32[1024,256]{1,0:T(8,128)}, u32[]{:S(2)}, u32[]{:S(2)}) %collective-permute-start.23) | collective-permute-done | bytes 1048608 | tf_op jit(solution)/shard_map/ppermute | solution.py:76
  384.8 18.8 %collective-permute-done.63 = f32[1024,256]{1,0:T(8,128)S(1)} collective-permute-done((f32[1024,256]{1,0:T(8,128)S(1)}, f32[1024,256]{1,0:T(8,128)S(1)}, u32[]{:S(2)}, u32[]{:S(2)}) %collective-permute-start.63) | collective-permute-done | bytes 1048608 | tf_op jit(solution)/shard_map/ppermute | solution.py:76
  447.6 8.5 %collective-permute-start.29 = (f32[128,256]{1,0:T(8,128)S(1)}, f32[128,256]{1,0:T(8,128)S(1)}, u32[]{:S(2)}, u32[]{:S(2)}) collective-permute-start(f32[128,256]{1,0:T(8,128)S(1)} %get-tuple-element.6), channel_id=1, source_target_pairs={{0,2},{1,3},{2,4},{3,5},{4,6},{5,7},{6,0},{7,1},{8,10},{9,11},{10,... | collective-permute-start | bytes 393224 | tf_op jit(solution)/shard_map/ppermute | solution.py:61
  622.8 7.4 collective-permute-start.112
  665.6 5.7 convolution_bitcast_fusion.1
  675.8 5.9 convolution_bitcast_fusion
  701.1 8.7 %collective-permute-done.99 = f32[128,256]{1,0:T(8,128)S(1)} collective-permute-done((f32[128,256]{1,0:T(8,128)S(1)}, f32[128,256]{1,0:T(8,128)S(1)}, u32[]{:S(2)}, u32[]{:S(2)}) %collective-permute-start.99) | collective-permute-done | bytes 131104 | tf_op jit(solution)/shard_map/ppermute | solution.py:53
  725.8 6.0 collective-permute-done.85
  734.6 9.5 %collective-permute-done.92 = f32[160,256]{1,0:T(8,128)S(1)} collective-permute-done((f32[160,256]{1,0:T(8,128)S(1)}, f32[160,256]{1,0:T(8,128)S(1)}, u32[]{:S(2)}, u32[]{:S(2)}) %collective-permute-start.92) | collective-permute-done | bytes 163872 | tf_op jit(solution)/shard_map/ppermute | solution.py:53
  758.2 15.2 %collective-permute-done.38 = f32[192,256]{1,0:T(8,128)S(1)} collective-permute-done((f32[192,256]{1,0:T(8,128)S(1)}, f32[192,256]{1,0:T(8,128)S(1)}, u32[]{:S(2)}, u32[]{:S(2)}) %collective-permute-start.38) | collective-permute-done | bytes 196640 | tf_op jit(solution)/shard_map/ppermute | solution.py:53
  773.5 9.2 %collective-permute-done.78 = f32[192,256]{1,0:T(8,128)S(1)} collective-permute-done((f32[192,256]{1,0:T(8,128)S(1)}, f32[192,256]{1,0:T(8,128)S(1)}, u32[]{:S(2)}, u32[]{:S(2)}) %collective-permute-start.78) | collective-permute-done | bytes 196640 | tf_op jit(solution)/shard_map/ppermute | solution.py:53
  (640 shorter events, 488.9 us)
Async XLA Ops:
  7.4 31.5 %collective-permute-start = (f32[384,256]{1,0:T(8,128)}, f32[384,256]{1,0:T(8,128)}, u32[]{:S(2)}, u32[]{:S(2)}) collective-permute-start(f32[384,256]{1,0:T(8,128)} %dynamic-slice_bitcast_fusion.13), channel_id=1, source_target_pairs={{0,8},{1,9},{2,10},{3,11},{4,12},{5,13},{6,14},{7,15},{8,0},{9,1},... | collective-permute-start | bytes 1179656 | tf_op jit(solution)/shard_map/ppermute | solution.py:53
  17.3 30.2 %collective-permute-start.40 = (f32[384,256]{1,0:T(8,128)}, f32[384,256]{1,0:T(8,128)}, u32[]{:S(2)}, u32[]{:S(2)}) collective-permute-start(f32[384,256]{1,0:T(8,128)} %dynamic-slice_bitcast_fusion.11), channel_id=1, source_target_pairs={{0,8},{1,9},{2,10},{3,11},{4,12},{5,13},{6,14},{7,15},{8,0},{9,1},... | collective-permute-start | bytes 1179656 | tf_op jit(solution)/shard_map/ppermute | solution.py:53
  56.7 30.6 %collective-permute-start.41 = (f32[384,256]{1,0:T(8,128)S(1)}, f32[384,256]{1,0:T(8,128)S(1)}, u32[]{:S(2)}, u32[]{:S(2)}) collective-permute-start(f32[384,256]{1,0:T(8,128)S(1)} %bitcast_add_fusion.15), channel_id=1, source_target_pairs={{0,16},{1,17},{2,18},{3,19},{4,20},{5,21},{6,22},{7,23},{8,24},{9,... | collective-permute-start | bytes 1179656 | tf_op jit(solution)/shard_map/ppermute | solution.py:76
  180.8 32.3 %collective-permute-start.21 = (f32[2,1024,256]{2,1,0:T(8,128)}, f32[2,1024,256]{2,1,0:T(8,128)}, u32[]{:S(2)}, u32[]{:S(2)}) collective-permute-start(f32[2,1024,256]{2,1,0:T(8,128)} %pad_maximum_fusion.3), channel_id=1, source_target_pairs={{0,8},{1,9},{2,10},{3,11},{4,12},{5,13},{6,14},{7,15},{8,0},{9,1},... | collective-permute-start | bytes 6291464 | tf_op jit(solution)/shard_map/ppermute | solution.py:61
  213.2 68.3 %collective-permute-start.61 = (f32[2,1024,256]{2,1,0:T(8,128)}, f32[2,1024,256]{2,1,0:T(8,128)}, u32[]{:S(2)}, u32[]{:S(2)}) collective-permute-start(f32[2,1024,256]{2,1,0:T(8,128)} %pad_maximum_fusion.5), channel_id=1, source_target_pairs={{0,8},{1,9},{2,10},{3,11},{4,12},{5,13},{6,14},{7,15},{8,0},{9,1},... | collective-permute-start | bytes 6291464 | tf_op jit(solution)/shard_map/ppermute | solution.py:61
  281.5 71.7 %collective-permute-start.22 = (f32[1024,256]{1,0:T(8,128)}, f32[1024,256]{1,0:T(8,128)}, u32[]{:S(2)}, u32[]{:S(2)}) collective-permute-start(f32[1024,256]{1,0:T(8,128)} %bitcast.674), channel_id=1, source_target_pairs={{0,8},{1,9},{2,10},{3,11},{4,12},{5,13},{6,14},{7,15},{8,0},{9,1},... | collective-permute-start | bytes 3145736 | tf_op jit(solution)/shard_map/ppermute | solution.py:53
  362.3 41.3 %collective-permute-start.63 = (f32[1024,256]{1,0:T(8,128)S(1)}, f32[1024,256]{1,0:T(8,128)S(1)}, u32[]{:S(2)}, u32[]{:S(2)}) collective-permute-start(f32[1024,256]{1,0:T(8,128)S(1)} %bitcast_add_fusion), channel_id=1, source_target_pairs={{0,16},{1,17},{2,18},{3,19},{4,20},{5,21},{6,22},{7,23},{8,24},{9,... | collective-permute-start | bytes 3145736 | tf_op jit(solution)/shard_map/ppermute | solution.py:76
  489.7 50.6 %collective-permute-start.108 = (f32[192,256]{1,0:T(8,128)}, f32[192,256]{1,0:T(8,128)}, u32[]{:S(2)}, u32[]{:S(2)}) collective-permute-start(f32[192,256]{1,0:T(8,128)} %dynamic-slice_bitcast_fusion.23), channel_id=1, source_target_pairs={{0,8},{1,9},{2,10},{3,11},{4,12},{5,13},{6,14},{7,15},{8,0},{9,1},... | collective-permute-start | bytes 589832 | tf_op jit(solution)/shard_map/ppermute | solution.py:53
  502.2 39.3 %collective-permute-start.115 = (f32[192,256]{1,0:T(8,128)}, f32[192,256]{1,0:T(8,128)}, u32[]{:S(2)}, u32[]{:S(2)}) collective-permute-start(f32[192,256]{1,0:T(8,128)} %dynamic-slice_bitcast_fusion.22), channel_id=1, source_target_pairs={{0,8},{1,9},{2,10},{3,11},{4,12},{5,13},{6,14},{7,15},{8,0},{9,1},... | collective-permute-start | bytes 589832 | tf_op jit(solution)/shard_map/ppermute | solution.py:53
  508.2 34.8 %collective-permute-start.94 = (f32[256,256]{1,0:T(8,128)}, f32[256,256]{1,0:T(8,128)}, u32[]{:S(2)}, u32[]{:S(2)}) collective-permute-start(f32[256,256]{1,0:T(8,128)} %dynamic-slice_bitcast_fusion.19), channel_id=1, source_target_pairs={{0,8},{1,9},{2,10},{3,11},{4,12},{5,13},{6,14},{7,15},{8,0},{9,1},... | collective-permute-start | bytes 786440 | tf_op jit(solution)/shard_map/ppermute | solution.py:53
  514.8 29.3 %collective-permute-start.101 = (f32[256,256]{1,0:T(8,128)}, f32[256,256]{1,0:T(8,128)}, u32[]{:S(2)}, u32[]{:S(2)}) collective-permute-start(f32[256,256]{1,0:T(8,128)} %dynamic-slice_bitcast_fusion.18), channel_id=1, source_target_pairs={{0,8},{1,9},{2,10},{3,11},{4,12},{5,13},{6,14},{7,15},{8,0},{9,1},... | collective-permute-start | bytes 786440 | tf_op jit(solution)/shard_map/ppermute | solution.py:53
  552.8 28.8 %collective-permute-start.81 = (f32[320,256]{1,0:T(8,128)}, f32[320,256]{1,0:T(8,128)}, u32[]{:S(2)}, u32[]{:S(2)}) collective-permute-start(f32[320,256]{1,0:T(8,128)} %bitcast_add_fusion.19), channel_id=1, source_target_pairs={{0,16},{1,17},{2,18},{3,19},{4,20},{5,21},{6,22},{7,23},{8,24},{9,... | collective-permute-start | bytes 983048 | tf_op jit(solution)/shard_map/ppermute | solution.py:76
  567.5 47.7 %collective-permute-start.34 = (f32[384,256]{1,0:T(8,128)}, f32[384,256]{1,0:T(8,128)}, u32[]{:S(2)}, u32[]{:S(2)}) collective-permute-start(f32[384,256]{1,0:T(8,128)} %bitcast_add_fusion.16), channel_id=1, source_target_pairs={{0,16},{1,17},{2,18},{3,19},{4,20},{5,21},{6,22},{7,23},{8,24},{9,... | collective-permute-start | bytes 1179656 | tf_op jit(solution)/shard_map/ppermute | solution.py:76
  569.5 48.0 %collective-permute-start.74 = (f32[384,256]{1,0:T(8,128)}, f32[384,256]{1,0:T(8,128)}, u32[]{:S(2)}, u32[]{:S(2)}) collective-permute-start(f32[384,256]{1,0:T(8,128)} %bitcast_add_fusion.14), channel_id=1, source_target_pairs={{0,16},{1,17},{2,18},{3,19},{4,20},{5,21},{6,22},{7,23},{8,24},{9,... | collective-permute-start | bytes 1179656 | tf_op jit(solution)/shard_map/ppermute | solution.py:76
  584.0 36.8 %collective-permute-start.111 = (f32[4,96,256]{2,1,0:T(8,128)}, f32[4,96,256]{2,1,0:T(8,128)}, u32[]{:S(2)}, u32[]{:S(2)}) collective-permute-start(f32[4,96,256]{2,1,0:T(8,128)} %dynamic-slice_bitcast_fusion.9), channel_id=1, source_target_pairs={{0,1},{1,0},{2,3},{3,2},{4,5},{5,4},{6,7},{7,6},{8,9},{9,8},{10,11... | collective-permute-start | bytes 1179656 | tf_op jit(solution)/shard_map/ppermute | solution.py:53
  587.4 60.8 %collective-permute-start.118 = (f32[4,96,256]{2,1,0:T(8,128)}, f32[4,96,256]{2,1,0:T(8,128)}, u32[]{:S(2)}, u32[]{:S(2)}) collective-permute-start(f32[4,96,256]{2,1,0:T(8,128)} %dynamic-slice_bitcast_fusion.8), channel_id=1, source_target_pairs={{0,1},{1,0},{2,3},{3,2},{4,5},{5,4},{6,7},{7,6},{8,9},{9,8},{10,11... | collective-permute-start | bytes 1179656 | tf_op jit(solution)/shard_map/ppermute | solution.py:53
  617.5 69.5 %collective-permute-start.97 = (f32[4,128,256]{2,1,0:T(8,128)}, f32[4,128,256]{2,1,0:T(8,128)}, u32[]{:S(2)}, u32[]{:S(2)}) collective-permute-start(f32[4,128,256]{2,1,0:T(8,128)} %bitcast.684), channel_id=1, source_target_pairs={{0,1},{1,0},{2,3},{3,2},{4,5},{5,4},{6,7},{7,6},{8,9},{9,8},{10,11... | collective-permute-start | bytes 1572872 | tf_op jit(solution)/shard_map/ppermute | solution.py:53
  620.8 42.1 %collective-permute-start.35 = (f32[384,256]{1,0:T(8,128)}, f32[384,256]{1,0:T(8,128)}, u32[]{:S(2)}, u32[]{:S(2)}) collective-permute-start(f32[384,256]{1,0:T(8,128)} %add.562), channel_id=1, source_target_pairs={{0,8},{1,9},{2,10},{3,11},{4,12},{5,13},{6,14},{7,15},{8,0},{9,1},... | collective-permute-start | bytes 1179656 | tf_op jit(solution)/shard_map/ppermute | solution.py:61
  658.3 33.3 %collective-permute-start.104 = (f32[4,128,256]{2,1,0:T(8,128)}, f32[4,128,256]{2,1,0:T(8,128)}, u32[]{:S(2)}, u32[]{:S(2)}) collective-permute-start(f32[4,128,256]{2,1,0:T(8,128)} %bitcast.222), channel_id=1, source_target_pairs={{0,1},{1,0},{2,3},{3,2},{4,5},{5,4},{6,7},{7,6},{8,9},{9,8},{10,11... | collective-permute-start | bytes 1572872 | tf_op jit(solution)/shard_map/ppermute | solution.py:53
  661.5 54.0 %collective-permute-start.83 = (f32[4,160,256]{2,1,0:T(8,128)}, f32[4,160,256]{2,1,0:T(8,128)}, u32[]{:S(2)}, u32[]{:S(2)}) collective-permute-start(f32[4,160,256]{2,1,0:T(8,128)} %dynamic-slice_bitcast_fusion.3), channel_id=1, source_target_pairs={{0,1},{1,0},{2,3},{3,2},{4,5},{5,4},{6,7},{7,6},{8,9},{9,8},{10,11... | collective-permute-start | bytes 1966088 | tf_op jit(solution)/shard_map/ppermute | solution.py:53
  662.9 57.4 %collective-permute-start.90 = (f32[4,160,256]{2,1,0:T(8,128)}, f32[4,160,256]{2,1,0:T(8,128)}, u32[]{:S(2)}, u32[]{:S(2)}) collective-permute-start(f32[4,160,256]{2,1,0:T(8,128)} %dynamic-slice_bitcast_fusion.2), channel_id=1, source_target_pairs={{0,1},{1,0},{2,3},{3,2},{4,5},{5,4},{6,7},{7,6},{8,9},{9,8},{10,11... | collective-permute-start | bytes 1966088 | tf_op jit(solution)/shard_map/ppermute | solution.py:53
  709.9 38.4 %collective-permute-start.36 = (f32[4,192,256]{2,1,0:T(8,128)S(1)}, f32[4,192,256]{2,1,0:T(8,128)S(1)}, u32[]{:S(2)}, u32[]{:S(2)}) collective-permute-start(f32[4,192,256]{2,1,0:T(8,128)S(1)} %copy-done.76), channel_id=1, source_target_pairs={{0,1},{1,0},{2,3},{3,2},{4,5},{5,4},{6,7},{7,6},{8,9},{9,8},{10,11... | collective-permute-start | bytes 2359304 | tf_op jit(solution)/shard_map/ppermute | solution.py:53
  712.6 39.7 %collective-permute-start.76 = (f32[4,192,256]{2,1,0:T(8,128)S(1)}, f32[4,192,256]{2,1,0:T(8,128)S(1)}, u32[]{:S(2)}, u32[]{:S(2)}) collective-permute-start(f32[4,192,256]{2,1,0:T(8,128)S(1)} %dynamic-slice_bitcast_fusion), channel_id=1, source_target_pairs={{0,1},{1,0},{2,3},{3,2},{4,5},{5,4},{6,7},{7,6},{8,9},{9,8},{10,11... | collective-permute-start | bytes 2359304 | tf_op jit(solution)/shard_map/ppermute | solution.py:53
  753.1 29.5 %collective-permute-start.78 = (f32[192,256]{1,0:T(8,128)S(1)}, f32[192,256]{1,0:T(8,128)S(1)}, u32[]{:S(2)}, u32[]{:S(2)}) collective-permute-start(f32[192,256]{1,0:T(8,128)S(1)} %get-tuple-element.58), channel_id=1, source_target_pairs={{0,4},{1,5},{2,6},{3,7},{4,0},{5,1},{6,2},{7,3},{8,12},{9,13},{10,... | collective-permute-start | bytes 589832 | tf_op jit(solution)/shard_map/ppermute | solution.py:53
  (179 other events, 1861.3 us)

commit v2 on v1

--- a/solution.py
+++ b/solution.py
@@ -1,3 +1,5 @@
+import functools
+
 import jax
 import jax.numpy as jnp
 from jax import lax
@@ -7,7 +9,7 @@
 
 BLOCK = 128
 AXES = ("row", "col")
-PARTS = 2
+LIMIT = 56 * 2**20
 
 
 def product(matrix, vector):
@@ -169,7 +171,7 @@
     )(ids, held)
 
 
-def local(rows, cols, *arguments):
+def general(rows, cols, *arguments):
     inverses = arguments[0:4]
     couplings = arguments[4:8]
     inverse_root = arguments[8]
@@ -178,8 +180,7 @@
     target_blocks = arguments[14]
     links = Links(rows, cols)
     columns = loads_root.shape[1]
-    parts = PARTS if columns % (PARTS * 128) == 0 else 1
-    width = columns // parts
+    parts, width = 1, columns
     children, count = target_blocks.shape
     per_row = couplings[0].shape[0] // BLOCK
     owned = loads_root.shape[0] // BLOCK
@@ -219,6 +220,400 @@
     return tuple(jnp.concatenate(list(pieces), axis=1) for pieces in zip(*answers))
 
 
+def split(value):
+    high = value.astype(jnp.bfloat16)
+    return high, (value - high.astype(jnp.float32)).astype(jnp.bfloat16)
+
+
+def dot(first, second, flip=False):
+    dims = (((0 if flip else 1,), (0,)), ((), ()))
+
+    def one(a, b):
+        return lax.dot_general(a, b, dims, preferred_element_type=jnp.float32)
+
+    return one(first[0], second[0]) + (one(first[0], second[1]) + one(first[1], second[0]))
+
+
+def call(kernel, me, inputs, outputs, scratch, macs):
+    size = sum(a.size * 4 for a in inputs) + sum(4 * a.size for a in outputs)
+    whole = pl.BlockSpec(memory_space=pltpu.VMEM)
+    return pl.pallas_call(
+        kernel,
+        in_specs=[pl.BlockSpec(memory_space=pltpu.SMEM)] + [whole] * len(inputs),
+        out_specs=[whole] * len(outputs),
+        out_shape=outputs,
+        scratch_shapes=scratch,
+        cost_estimate=pl.CostEstimate(flops=6 * macs, bytes_accessed=size, transcendentals=0),
+        compiler_params=pltpu.CompilerParams(vmem_limit_bytes=LIMIT),
+    )(me, *inputs)
+
+
+def shape(*extent):
+    return jax.ShapeDtypeStruct(extent, jnp.float32)
+
+
+def forward_kernel(me, first, second, first_loads, second_loads, own, other):
+    width = own.shape[1]
+    start = 0
+    for weight, loads in ((first, first_loads), (second, second_loads)):
+        rows = weight.shape[0]
+        held = split(weight[...])
+        for out, half in ((own, me[0]), (other, 1 - me[0])):
+            part = loads[:, pl.ds(pl.multiple_of(half * width, width), width)]
+            out[start : start + rows] = dot(held, split(part))
+        start += rows
+
+
+def couple_kernel(me, first, second, own, other, keep, send):
+    y, z = me[1], me[2]
+    count = keep.shape[0]
+    start = 0
+    for child, weight in enumerate((first, second)):
+        rows = weight.shape[1]
+        blocks = weight.shape[0] // BLOCK
+        held = split(weight[...])
+        mine, theirs = own[start : start + rows], other[start : start + rows]
+        start += rows
+        for out, half in ((send, 1 - y), (keep, y)):
+            value = dot(held, split(jnp.where(half == 0, mine, theirs)))
+            for block in range(blocks):
+                place = lax.rem(child * blocks + block + count - z, count)
+                out[place] = value[block * BLOCK : (block + 1) * BLOCK]
+
+
+def base_kernel(me, weight, loads, own, other, high, low):
+    width = own.shape[1]
+
+    @pl.when(pl.program_id(0) == 0)
+    def _():
+        high[...], low[...] = split(loads[...])
+
+    held = split(weight[...])
+    for out, half in ((own, me[0]), (other, 1 - me[0])):
+        span = pl.ds(pl.multiple_of(half * width, width), width)
+        out[...] = dot(held, (high[:, span], low[:, span]))
+
+
+def base(me, weight, loads):
+    rows, depth = weight.shape
+    columns = loads.shape[1]
+    tile = rows // 8
+    return pl.pallas_call(
+        base_kernel,
+        grid_spec=pltpu.PrefetchScalarGridSpec(
+            num_scalar_prefetch=1,
+            grid=(rows // tile,),
+            in_specs=[
+                pl.BlockSpec((tile, depth), lambda i, me: (i, 0)),
+                pl.BlockSpec(memory_space=pltpu.VMEM),
+            ],
+            out_specs=[pl.BlockSpec((tile, columns // 2), lambda i, me: (i, 0))] * 2,
+            scratch_shapes=[pltpu.VMEM((depth, columns), jnp.bfloat16)] * 2,
+        ),
+        out_shape=[shape(rows, columns // 2)] * 2,
+        cost_estimate=pl.CostEstimate(
+            flops=6 * rows * depth * columns,
+            bytes_accessed=4 * (rows * depth + depth * columns + rows * columns),
+            transcendentals=0,
+        ),
+        compiler_params=pltpu.CompilerParams(vmem_limit_bytes=LIMIT),
+    )(me, weight, loads)
+
+
+def root_kernel(list_ref, left, right, base_own, base_other, *refs):
+    sources, outs, (moved,) = refs[:-5], refs[-5:-1], refs[-1:]
+    step = pl.program_id(0)
+    width = base_own.shape[1]
+    rows = outs[0].shape[0]
+
+    @pl.when(step == 0)
+    def _():
+        for piece in range(2):
+            span = slice(piece * rows, (piece + 1) * rows)
+            outs[piece][...] = base_own[span]
+            outs[2 + piece][...] = base_other[span]
+
+    @pl.when(2 * step < list_ref[4, 0])
+    def _():
+        for entry in range(2):
+            span = slice(entry * BLOCK, (entry + 1) * BLOCK)
+            which = list_ref[1, 2 * step + entry]
+
+            @pl.when(which < 0)
+            def _():
+                moved[span] = jnp.zeros((BLOCK, 2 * width), jnp.float32)
+
+            for number, source in enumerate(sources):
+
+                @pl.when(which == number)
+                def _():
+                    moved[span, :width] = source[list_ref[2, 2 * step + entry]]
+                    moved[span, width:] = source[list_ref[3, 2 * step + entry]]
+
+        held = split(moved[...])
+        tile = rows // 4
+        for piece in range(2):
+            for start in range(0, rows, tile):
+                span = slice(piece * rows + start, piece * rows + start + tile)
+                weight = split(jnp.concatenate([left[span], right[span]], axis=1))
+                value = dot(weight, held)
+                outs[piece][start : start + tile] -= value[:, :width]
+                outs[2 + piece][start : start + tile] -= value[:, width:]
+
+
+def root(listed, weight, bases, sources):
+    rows = weight.shape[0]
+    width = bases[0].shape[1]
+    whole = pl.BlockSpec(memory_space=pltpu.VMEM)
+    return pl.pallas_call(
+        root_kernel,
+        grid_spec=pltpu.PrefetchScalarGridSpec(
+            num_scalar_prefetch=1,
+            grid=(listed.shape[1] // 2,),
+            in_specs=[
+                pl.BlockSpec((rows, BLOCK), lambda i, listed: (0, listed[0, 2 * i])),
+                pl.BlockSpec((rows, BLOCK), lambda i, listed: (0, listed[0, 2 * i + 1])),
+            ]
+            + [whole] * (2 + len(sources)),
+            out_specs=[whole] * 4,
+            scratch_shapes=[pltpu.VMEM((2 * BLOCK, 2 * width), jnp.float32)],
+        ),
+        out_shape=[shape(rows // 2, width)] * 4,
+        cost_estimate=pl.CostEstimate(
+            flops=6 * rows * 1024 * 2 * width,
+            bytes_accessed=4 * (rows * 1024 + rows * width * 8),
+            transcendentals=0,
+        ),
+        compiler_params=pltpu.CompilerParams(vmem_limit_bytes=LIMIT),
+    )(listed, weight, weight, *bases, *sources)
+
+
+def pick_kernel(me, first, second, keep, send):
+    y, z = me[1], me[2]
+    count = first.shape[0] // BLOCK
+    children = keep.shape[0]
+    for out, block in ((send, 1 - y), (keep, y)):
+        for child in range(children):
+            place = lax.rem(child + children - z, children)
+            source = me[3 + 2 * child + block]
+            inside = jnp.logical_and(source >= 0, source < 2 * count)
+
+            @pl.when(jnp.logical_and(inside, source < count))
+            def _():
+                out[place] = first[pl.ds(pl.multiple_of(source * BLOCK, BLOCK), BLOCK)]
+
+            @pl.when(jnp.logical_and(inside, source >= count))
+            def _():
+                start = pl.multiple_of((source - count) * BLOCK, BLOCK)
+                out[place] = second[pl.ds(start, BLOCK)]
+
+            @pl.when(jnp.logical_not(inside))
+            def _():
+                out[place] = jnp.zeros((BLOCK, first.shape[1]), jnp.float32)
+
+
+def correct_kernel(pair, me, first, second, own_near, own_far, other_near, other_far, own, other, rows_ref):
+    y, z = me[1], me[2]
+    children = own_near.shape[0]
+    near = pl.ds(pl.multiple_of(y * BLOCK, BLOCK), BLOCK)
+    far = pl.ds(pl.multiple_of((1 - y) * BLOCK, BLOCK), BLOCK)
+    start = 0
+    for child, weight in zip(pair, (first, second)):
+        rows = weight.shape[1]
+        held = split(weight[...])
+        place = lax.rem(z + children - child, children)
+        for out, here, there in ((other, other_near, other_far), (own, own_near, own_far)):
+            rows_ref[near] = here[place]
+            rows_ref[far] = there[place]
+            out[start : start + rows] = dot(held, split(rows_ref[...]), True)
+        start += rows
+
+
+def final_kernel(me, first, second, own, other, keep, send, whole):
+    y, z = me[1], me[2]
+    count = keep.shape[0]
+    width = own.shape[1]
+    start, place = 0, 0
+    for weight in (first, second):
+        rows, total = weight.shape
+        size = total // (2 * count)
+        held = split(weight[...])
+        for half, vector in ((me[0], own), (1 - me[0], other)):
+            columns = pl.ds(pl.multiple_of(half * width, width), width)
+            whole[:total] = dot(held, split(vector[start : start + rows]), True)
+            for out, side in ((send, 1 - y), (keep, y)):
+                for owner in range(count):
+                    taken = pl.ds(pl.multiple_of((2 * owner + side) * size, 8), size)
+                    there = lax.rem(owner + count - z, count)
+                    out[there, place : place + size, columns] = whole[taken]
+        start += rows
+        place += size
+
+
+def fast(rows, cols, *arguments):
+    inverses = arguments[0:4]
+    couplings = arguments[4:8]
+    inverse_root = arguments[8]
+    sources = arguments[9:13]
+    loads_root = arguments[13]
+    target_blocks = arguments[14]
+    links = Links(rows, cols)
+    core, x, y, z = links.core, links.x, links.y, links.z
+    width = loads_root.shape[1] // 2
+    children, count = target_blocks.shape
+    per_row = count // rows
+    owned = loads_root.shape[0] // BLOCK
+    held = inverse_root.shape[0] // BLOCK
+    row = lax.axis_index("row")
+    pairs = ((0, 3), (1, 2))
+
+    def send(array, group, step=1):
+        return lax.ppermute(array, AXES, group.pairs[step - 1])
+
+    mine = lax.dynamic_slice_in_dim(target_blocks, row * per_row, per_row, 1)
+    wanted = (mine - lax.axis_index("col") * held).reshape(-1)
+    me = jnp.concatenate([jnp.stack([core.place, y.place, z.place]).astype(jnp.int32), wanted])
+
+    child = jnp.arange(children, dtype=jnp.int32)[:, None] + jnp.zeros((1, count), jnp.int32)
+    block = jnp.arange(count, dtype=jnp.int32)[None, :] + jnp.zeros((children, 1), jnp.int32)
+    group = jnp.where((child == 0) | (child == 3), 0, 1)
+    inner = jnp.where(child >= 2, 1, 0)
+    from_row = block // per_row
+    owner = inner * per_row + block % per_row
+    away_x = jnp.where(from_row // 2 == x.place, 0, 1)
+    away_core = jnp.where(from_row % 2 == core.place, 0, 1)
+    array = group * 4 + away_core * 2 + away_x
+    place = (z.place + z.size - owner) % z.size
+    first = (away_core + y.place) % 2 * z.size + place
+    second = (away_core + y.place + 1) % 2 * z.size + place
+    local_block = target_blocks - row * owned
+    inside = ((local_block >= 0) & (local_block < owned)).reshape(-1)
+    rank = jnp.cumsum(inside.astype(jnp.int32)) - 1
+    chosen = inside[None, :] & (rank[None, :] == jnp.arange(inside.shape[0])[:, None])
+    table = jnp.stack([local_block, array + 1, first, second]).reshape(4, -1)
+    listed = jnp.sum(jnp.where(chosen[None], table[:, None, :], 0), axis=2)
+    listed = listed - jnp.array([[0], [1], [0], [0]], jnp.int32)
+    found = jnp.sum(inside.astype(jnp.int32))
+    entries = jnp.arange(inside.shape[0], dtype=jnp.int32)
+    last = jnp.sum(jnp.where(entries == found - 1, listed[0], 0))
+    listed = listed.at[0].set(jnp.where(entries < found, listed[0], last))
+    listed = jnp.concatenate([listed, jnp.full((1, entries.size), found, jnp.int32)])
+
+    forward, spread = [], []
+    started = []
+    for a, b in pairs:
+        n = inverses[a].shape[0] + inverses[b].shape[0]
+        macs = inverses[a].size + inverses[b].size
+        started.append(
+            call(
+                forward_kernel,
+                me,
+                [inverses[a], inverses[b], sources[a], sources[b]],
+                [shape(n, width)] * 2,
+                [],
+                macs * 2 * width,
+            )
+        )
+    bases = base(me, inverse_root, loads_root)
+    for (a, b), (own, other) in zip(pairs, started):
+        own = own + send(other, core)
+        own = own + send(own, x)
+        other = send(own, core)
+        forward.append((own, other))
+        piece = shape(z.size, BLOCK, width)
+        macs = couplings[a].size + couplings[b].size
+        keep, sent = call(
+            couple_kernel, me, [couplings[a], couplings[b], own, other], [piece] * 2, [], macs * 2 * width
+        )
+        part = keep + send(sent, y)
+        total = part[0]
+        for step in range(1, z.size):
+            total = total + send(part[step], z, step)
+        near = jnp.stack([total] + [send(total, z, step) for step in range(1, z.size)])
+        near = jnp.concatenate([near, send(near, y)])
+        far = send(near, x)
+        spread += [near, far, send(near, core), send(far, core)]
+
+    own0, own1, other0, other1 = root(listed, inverse_root, bases, spread)
+    own0 = own0 + send(other0, core)
+    own1 = own1 + send(other1, core)
+    own0 = own0 + send(own0, x)
+    own1 = own1 + send(own1, x)
+    other0 = send(own0, core)
+    other1 = send(own1, core)
+    picked = []
+    for pieces in ((own0, own1), (other0, other1)):
+        piece = shape(children, BLOCK, width)
+        keep, sent = call(pick_kernel, me, list(pieces), [piece] * 2, [], 0)
+        part = keep + send(sent, y)
+        total = part[0]
+        for step in range(1, z.size):
+            total = total + send(part[step], z, step)
+        near = jnp.stack([total] + [send(total, z, step) for step in range(1, z.size)])
+        picked += [near, send(near, y)]
+
+    solved = [None] * 4
+    for (a, b), (own, other) in zip(pairs, forward):
+        macs = couplings[a].size + couplings[b].size
+        fix_own, fix_other = call(
+            functools.partial(correct_kernel, (a, b)),
+            me,
+            [couplings[a], couplings[b]] + picked,
+            [shape(*own.shape)] * 2,
+            [pltpu.VMEM((per_row * BLOCK, width), jnp.float32)],
+            macs * 2 * width,
+        )
+        fix_own = fix_own + send(fix_other, core)
+        own = own - fix_own - send(fix_own, x)
+        other = send(own, core)
+        sizes = [inverses[k].shape[1] // cols for k in (a, b)]
+        piece = shape(z.size, sum(sizes), 2 * width)
+        macs = inverses[a].size + inverses[b].size
+        keep, sent = call(
+            final_kernel,
+            me,
+            [inverses[a], inverses[b], own, other],
+            [piece] * 2,
+            [pltpu.VMEM((max(inverses[k].shape[1] for k in (a, b)), width), jnp.float32)],
+            macs * 2 * width,
+        )
+        arrived = send(sent, y)
+        total = keep[0] + arrived[0]
+        for step in range(1, z.size):
+            total = total + send(keep[step] + arrived[step], z, step)
+        solved[a] = total[: sizes[0]]
+        solved[b] = total[sizes[0] :]
+
+    left = jnp.concatenate([own0, own1])
+    right = jnp.concatenate([other0, other1])
+    first = core.place == 0
+    solved_root = jnp.concatenate(
+        [jnp.where(first, left, right), jnp.where(first, right, left)], axis=1
+    )
+    return tuple(solved) + (solved_root,)
+
+
+def local(rows, cols, *arguments):
+    links = Links(rows, cols)
+    children, count = arguments[14].shape
+    columns = arguments[13].shape[1]
+    sizes = [arguments[k].shape[1] for k in range(4)]
+    fits = (
+        links.core.size == 2
+        and links.x.size == 2
+        and links.y.size == 2
+        and children == 4
+        and links.z.size == 4
+        and count == 2 * rows
+        and arguments[4].shape[0] == 2 * BLOCK
+        and columns % 256 == 0
+        and arguments[8].shape[0] % (16 * BLOCK) == 0
+        and all(size % (cols * 16) == 0 for size in sizes)
+        and all(arguments[k].shape[0] % 16 == 0 for k in range(4))
+    )
+    return (fast if fits else general)(rows, cols, *arguments)
+
+
 def solution(mesh):
     rows, cols = mesh.shape["row"], mesh.shape["col"]
     matrices = [P("col", "row")] * 4 + [P("row", "col")] * 4 + [P("col", "row")]

time: 798 us -> 641 us (0.80)
  waiting for transfers between devices: 241 us -> 399 us
  local copies, waits for them, and re-layouts: 145 us -> 13.4 us
  matrix products: 128 us -> 0 us
  Pallas kernels: 41.3 us -> 122 us
  other arithmetic: 85.5 us -> 17.5 us
  starting transfers between devices: 139 us -> 79.8 us
    ppermute x122 -> x64, waiting for transfers between devices: 241 us -> 399 us  [send(): return lax.ppermute(array, AXES, group.pairs[step - 1])]
    dot_general x34 -> x0, matrix products: 128 us -> none  [the longest x18 85.7 us: product(): jnp.dot(matrix, vector, precision=lax.Precision.HIGH, preferred_element_t...]
    pallas_call x4 -> x12, Pallas kernels: 41.3 us -> 122 us  [the longest x10 65.3 us: call(): pl.pallas_call(kernel, in_specs=[pl.BlockSpec(memory_space=pltpu.SMEM)] +...]
    ppermute x122 -> x64, starting transfers between devices: 139 us -> 79.8 us  [send(): return lax.ppermute(array, AXES, group.pairs[step - 1])]
    squeeze x38 -> x4, local copies, waits for them, and re-layouts: 34.2 us -> 0.11 us  [fast(): total = total + send(part[step], z, step)]
    add x57 -> x23, other arithmetic: 42.1 us -> 9.63 us  [the longest x4 6.57 us: fast(): total = total + send(keep[step] + arrived[step], z, step)]
    another operation x52 -> x6, other arithmetic: 31.6 us -> 0.2 us  [the longest x4 0.14 us: fast(): jnp.stack([total] + [send(total, z, step) for step in range(1, z.size)])]
    dynamic_slice x7 -> x0, local copies, waits for them, and re-layouts: 31.2 us -> none  [pick(): return lax.dynamic_index_in_dim(array, index, axis, keepdims=False)]
  transfers between devices with their start and end apart: 122 -> 64, of which waited for: 46 -> 33; matrix products, arithmetic and copies ran while one was open for 43% -> 3% of each run, Pallas kernels for 5% -> 14%
where the time goes in v2:
time: 641 us; the launch traced here: 634 us
  waiting for transfers between devices  399 us (62%)
  Pallas kernels  122 us (19%)
  starting transfers between devices  79.8 us (12%)
  other arithmetic  17.5 us (3%)
  local copies, waits for them, and re-layouts  13.4 us (2%)
    ppermute x64, waiting for transfers between devices, send(): return lax.ppermute(array, AXES, group.pairs[step - 1])  399 us
    ppermute x64, starting transfers between devices, send(): return lax.ppermute(array, AXES, group.pairs[step - 1])  79.8 us
    pallas_call x10, Pallas kernels, call(): pl.pallas_call(kernel, in_specs=[pl.BlockSpec(memory_space=pltpu.SMEM)] +...  65.3 us
    pallas_call x1, Pallas kernels, base(): pl.pallas_call(base_kernel, grid_spec=pltpu.PrefetchScalarGridSpec(num_sc...  35.9 us
    pallas_call x1, Pallas kernels, root(): pl.pallas_call(root_kernel, grid_spec=pltpu.PrefetchScalarGridSpec(num_sc...  21.1 us
  transfers between devices with their start and end apart: 64, of which 33 were waited for; matrix products, arithmetic and copies ran while one was open for 3% of the time, Pallas kernels for 14%

profile of v2, /device:TPU:0, one launch (start us, length us, event | category | flops | bytes accessed | tf_op | source)
XLA Modules:
  0.0 634.0 jit_solution(9670047017775964318)
XLA Ops:
  2.1 9.8 %shard_map.194 = (f32[1152,256]{1,0:T(8,128)}, f32[1152,256]{1,0:T(8,128)}) custom-call(s32[11]{0:T(128)} %pad_add_fusion.1.me, f32[640,1280]{1,0:T(8,128)} %first.15, f32[512,1024]{1,0:T(8,128)} %second.15, f32[1280,512]{1,0:T(8,128)} %first_loads.3, f32[1024,512]{1,0:T(8,128)} %second_loads.3), custom_call_target="tpu_custom_call" | custom-call | flops 4127195136 | bytes 12451840 | tf_op jit(solution)/shard_map/pallas_call | solution.py:240
  12.3 10.3 %shard_map.191 = (f32[1152,256]{1,0:T(8,128)}, f32[1152,256]{1,0:T(8,128)}) custom-call(s32[11]{0:T(128)} %pad_add_fusion.1.me, f32[768,1536]{1,0:T(8,128)} %first.13, f32[384,768]{1,0:T(8,128)} %second.13, f32[1536,512]{1,0:T(8,128)} %first_loads.2, f32[768,512]{1,0:T(8,128)} %second_loads.2), custom_call_target="tpu_custom_call" | custom-call | flops 4529848320 | bytes 12976128 | tf_op jit(solution)/shard_map/pallas_call | solution.py:240
  28.5 24.1 %collective-permute-done.15 = f32[1152,256]{1,0:T(8,128)S(1)} collective-permute-done((f32[1152,256]{1,0:T(8,128)S(1)}, f32[1152,256]{1,0:T(8,128)S(1)}, u32[]{:S(2)}, u32[]{:S(2)}) %collective-permute-start.15) | collective-permute-done | bytes 1179680 | tf_op jit(solution)/shard_map/ppermute | solution.py:471
  52.9 24.4 %collective-permute-done.1 = f32[1152,256]{1,0:T(8,128)S(1)} collective-permute-done((f32[1152,256]{1,0:T(8,128)S(1)}, f32[1152,256]{1,0:T(8,128)S(1)}, u32[]{:S(2)}, u32[]{:S(2)}) %collective-permute-start.1) | collective-permute-done | bytes 1179680 | tf_op jit(solution)/shard_map/ppermute | solution.py:471
  77.5 35.9 %shard_map.192 = (f32[2048,256]{1,0:T(8,128)}, f32[2048,256]{1,0:T(8,128)}) custom-call(s32[11]{0:T(128)} %pad_add_fusion.1.me, f32[2048,4096]{1,0:T(8,128)} %right.1, f32[4096,512]{1,0:T(8,128)} %loads.1), custom_call_target="tpu_custom_call" | custom-call | flops 25769803776 | bytes 46137344 | tf_op jit(solution)/shard_map/pallas_call | solution.py:301
  152.7 10.2 %collective-permute-start.21 = (f32[128,256]{1,0:T(8,128)S(1)}, f32[128,256]{1,0:T(8,128)S(1)}, u32[]{:S(2)}, u32[]{:S(2)}) collective-permute-start(f32[128,256]{1,0:T(8,128)S(1)} %get-tuple-element.70), channel_id=1, source_target_pairs={{0,2},{1,3},{2,4},{3,5},{4,6},{5,7},{6,0},{7,1},{8,10},{9,11},{10,... | collective-permute-start | bytes 393224 | tf_op jit(solution)/shard_map/ppermute | solution.py:471
  169.5 7.7 %collective-permute-done.22 = f32[128,256]{1,0:T(8,128)S(1)} collective-permute-done((f32[128,256]{1,0:T(8,128)S(1)}, f32[128,256]{1,0:T(8,128)S(1)}, u32[]{:S(2)}, u32[]{:S(2)}) %collective-permute-start.22) | collective-permute-done | bytes 131104 | tf_op jit(solution)/shard_map/ppermute | solution.py:471
  184.0 8.1 %collective-permute-done.24 = f32[4,128,256]{2,1,0:T(8,128)S(1)} collective-permute-done((f32[4,128,256]{2,1,0:T(8,128)S(1)}, f32[4,128,256]{2,1,0:T(8,128)S(1)}, u32[]{:S(2)}, u32[]{:S(2)}) %collective-permute-start.24) | collective-permute-done | bytes 524320 | tf_op jit(solution)/shard_map/ppermute | solution.py:471
  192.2 9.2 %collective-permute-done.10 = f32[4,128,256]{2,1,0:T(8,128)S(1)} collective-permute-done((f32[4,128,256]{2,1,0:T(8,128)S(1)}, f32[4,128,256]{2,1,0:T(8,128)S(1)}, u32[]{:S(2)}, u32[]{:S(2)}) %collective-permute-start.10) | collective-permute-done | bytes 524320 | tf_op jit(solution)/shard_map/ppermute | solution.py:471
  203.4 14.9 %collective-permute-done.25.refs_5_ = f32[8,128,256]{2,1,0:T(8,128)S(1)} collective-permute-done((f32[8,128,256]{2,1,0:T(8,128)S(1)}, f32[8,128,256]{2,1,0:T(8,128)S(1)}, u32[]{:S(2)}, u32[]{:S(2)}) %collective-permute-start.25) | collective-permute-done | bytes 1048608 | tf_op jit(solution)/shard_map/ppermute | solution.py:471
  218.3 17.9 %collective-permute-done.11.refs_1_ = f32[8,128,256]{2,1,0:T(8,128)} collective-permute-done((f32[8,128,256]{2,1,0:T(8,128)S(1)}, f32[8,128,256]{2,1,0:T(8,128)}, u32[]{:S(2)}, u32[]{:S(2)}) %collective-permute-start.11) | collective-permute-done | bytes 1048608 | tf_op jit(solution)/shard_map/ppermute | solution.py:471
  240.7 21.1 %shard_map.196 = (f32[1024,256]{1,0:T(8,128)}, f32[1024,256]{1,0:T(8,128)}, f32[1024,256]{1,0:T(8,128)}, f32[1024,256]{1,0:T(8,128)}) custom-call(s32[5,32]{1,0:T(8,128)} %concatenate.27.list_ref, f32[2048,4096]{1,0:T(8,128)} %right.1, f32[2048,4096]{1,0:T(8,128)} %right.1, f32[2048,256]{1,0:T(8,128)} %get-tuple-element.45.base_own, ...), custom_call_target="tpu_custom_call" | custom-call | flops 6442450944 | bytes 25165824 | tf_op jit(solution)/shard_map/pallas_call | solution.py:368
  268.4 23.8 %collective-permute-done.29 = f32[1024,256]{1,0:T(8,128)S(1)} collective-permute-done((f32[1024,256]{1,0:T(8,128)S(1)}, f32[1024,256]{1,0:T(8,128)S(1)}, u32[]{:S(2)}, u32[]{:S(2)}) %collective-permute-start.29) | collective-permute-done | bytes 1048608 | tf_op jit(solution)/shard_map/ppermute | solution.py:471
  292.4 21.4 %collective-permute-done.31 = f32[1024,256]{1,0:T(8,128)S(1)} collective-permute-done((f32[1024,256]{1,0:T(8,128)S(1)}, f32[1024,256]{1,0:T(8,128)S(1)}, u32[]{:S(2)}, u32[]{:S(2)}) %collective-permute-start.31) | collective-permute-done | bytes 1048608 | tf_op jit(solution)/shard_map/ppermute | solution.py:471
  324.4 8.3 %collective-permute-done.32 = f32[4,128,256]{2,1,0:T(8,128)S(1)} collective-permute-done((f32[4,128,256]{2,1,0:T(8,128)}, f32[4,128,256]{2,1,0:T(8,128)S(1)}, u32[]{:S(2)}, u32[]{:S(2)}) %collective-permute-start.32) | collective-permute-done | bytes 524320 | tf_op jit(solution)/shard_map/ppermute | solution.py:471
  384.1 9.2 %collective-permute-done.49.other_far = f32[4,128,256]{2,1,0:T(8,128)S(1)} collective-permute-done((f32[4,128,256]{2,1,0:T(8,128)S(1)}, f32[4,128,256]{2,1,0:T(8,128)S(1)}, u32[]{:S(2)}, u32[]{:S(2)}) %collective-permute-start.49) | collective-permute-done | bytes 524320 | tf_op jit(solution)/shard_map/ppermute | solution.py:471
  406.8 25.8 %collective-permute-done.51 = f32[1152,256]{1,0:T(8,128)S(1)} collective-permute-done((f32[1152,256]{1,0:T(8,128)S(1)}, f32[1152,256]{1,0:T(8,128)S(1)}, u32[]{:S(2)}, u32[]{:S(2)}) %collective-permute-start.51) | collective-permute-done | bytes 1179680 | tf_op jit(solution)/shard_map/ppermute | solution.py:471
  432.9 24.1 %collective-permute-done.58 = f32[1152,256]{1,0:T(8,128)S(1)} collective-permute-done((f32[1152,256]{1,0:T(8,128)S(1)}, f32[1152,256]{1,0:T(8,128)S(1)}, u32[]{:S(2)}, u32[]{:S(2)}) %collective-permute-start.58) | collective-permute-done | bytes 1179680 | tf_op jit(solution)/shard_map/ppermute | solution.py:471
  458.4 11.2 %shard_map.200 = (f32[4,288,512]{2,1,0:T(8,128)}, f32[4,288,512]{2,1,0:T(8,128)}) custom-call(s32[11]{0:T(128)} %pad_add_fusion.1.me, f32[768,1536]{1,0:T(8,128)} %first.13, f32[384,768]{1,0:T(8,128)} %second.13, f32[1152,256]{1,0:T(8,128)} %copy-done.23, f32[1152,256]{1,0:T(8,128)} %copy-done.35), custom_call_target="tpu_custom_call" | custom-call | flops 4529848320 | bytes 12976128 | tf_op jit(solution)/shard_map/pallas_call | solution.py:240
  471.2 11.1 %shard_map.202 = (f32[4,288,512]{2,1,0:T(8,128)}, f32[4,288,512]{2,1,0:T(8,128)}) custom-call(s32[11]{0:T(128)} %pad_add_fusion.1.me, f32[640,1280]{1,0:T(8,128)} %first.15, f32[512,1024]{1,0:T(8,128)} %second.15, f32[1152,256]{1,0:T(8,128)} %copy-done.21, f32[1152,256]{1,0:T(8,128)} %copy-done.34), custom_call_target="tpu_custom_call" | custom-call | flops 4127195136 | bytes 12451840 | tf_op jit(solution)/shard_map/pallas_call | solution.py:240
  484.0 40.0 %collective-permute-done.53 = f32[4,288,512]{2,1,0:T(8,128)} collective-permute-done((f32[4,288,512]{2,1,0:T(8,128)}, f32[4,288,512]{2,1,0:T(8,128)}, u32[]{:S(2)}, u32[]{:S(2)}) %collective-permute-start.53) | collective-permute-done | bytes 2359328 | tf_op jit(solution)/shard_map/ppermute | solution.py:471
  532.2 41.8 %collective-permute-done.60 = f32[4,288,512]{2,1,0:T(8,128)} collective-permute-done((f32[4,288,512]{2,1,0:T(8,128)}, f32[4,288,512]{2,1,0:T(8,128)}, u32[]{:S(2)}, u32[]{:S(2)}) %collective-permute-start.60) | collective-permute-done | bytes 2359328 | tf_op jit(solution)/shard_map/ppermute | solution.py:471
  594.5 10.9 %collective-permute-done.63 = f32[288,512]{1,0:T(8,128)S(1)} collective-permute-done((f32[288,512]{1,0:T(8,128)S(1)}, f32[288,512]{1,0:T(8,128)S(1)}, u32[]{:S(2)}, u32[]{:S(2)}) %collective-permute-start.63) | collective-permute-done | bytes 589856 | tf_op jit(solution)/shard_map/ppermute | solution.py:471
  605.4 25.3 %collective-permute-done.62 = f32[288,512]{1,0:T(8,128)S(1)} collective-permute-done((f32[288,512]{1,0:T(8,128)S(1)}, f32[288,512]{1,0:T(8,128)S(1)}, u32[]{:S(2)}, u32[]{:S(2)}) %collective-permute-start.62) | collective-permute-done | bytes 589856 | tf_op jit(solution)/shard_map/ppermute | solution.py:471
  (275 shorter events, 185.2 us)
Async XLA Ops:
  22.9 29.7 %collective-permute-start.15 = (f32[1152,256]{1,0:T(8,128)S(1)}, f32[1152,256]{1,0:T(8,128)S(1)}, u32[]{:S(2)}, u32[]{:S(2)}) collective-permute-start(f32[1152,256]{1,0:T(8,128)S(1)} %add.407), channel_id=1, source_target_pairs={{0,16},{1,17},{2,18},{3,19},{4,20},{5,21},{6,22},{7,23},{8,24},{9,... | collective-permute-start | bytes 3538952 | tf_op jit(solution)/shard_map/ppermute | solution.py:471
  26.0 51.3 %collective-permute-start.1 = (f32[1152,256]{1,0:T(8,128)S(1)}, f32[1152,256]{1,0:T(8,128)S(1)}, u32[]{:S(2)}, u32[]{:S(2)}) collective-permute-start(f32[1152,256]{1,0:T(8,128)S(1)} %add.378), channel_id=1, source_target_pairs={{0,16},{1,17},{2,18},{3,19},{4,20},{5,21},{6,22},{7,23},{8,24},{9,... | collective-permute-start | bytes 3538952 | tf_op jit(solution)/shard_map/ppermute | solution.py:471
  52.8 60.7 %collective-permute-start.16 = (f32[1152,256]{1,0:T(8,128)S(1)}, f32[1152,256]{1,0:T(8,128)S(1)}, u32[]{:S(2)}, u32[]{:S(2)}) collective-permute-start(f32[1152,256]{1,0:T(8,128)S(1)} %add.408.own), channel_id=1, source_target_pairs={{0,8},{1,9},{2,10},{3,11},{4,12},{5,13},{6,14},{7,15},{8,0},{9,1},... | collective-permute-start | bytes 3538952 | tf_op jit(solution)/shard_map/ppermute | solution.py:471
  77.5 43.1 %collective-permute-start.2 = (f32[1152,256]{1,0:T(8,128)S(1)}, f32[1152,256]{1,0:T(8,128)S(1)}, u32[]{:S(2)}, u32[]{:S(2)}) collective-permute-start(f32[1152,256]{1,0:T(8,128)S(1)} %add.379.own), channel_id=1, source_target_pairs={{0,8},{1,9},{2,10},{3,11},{4,12},{5,13},{6,14},{7,15},{8,0},{9,1},... | collective-permute-start | bytes 3538952 | tf_op jit(solution)/shard_map/ppermute | solution.py:471
  151.4 25.7 %collective-permute-start.22 = (f32[128,256]{1,0:T(8,128)S(1)}, f32[128,256]{1,0:T(8,128)S(1)}, u32[]{:S(2)}, u32[]{:S(2)}) collective-permute-start(f32[128,256]{1,0:T(8,128)S(1)} %get-tuple-element.70), channel_id=1, source_target_pairs={{0,4},{1,5},{2,6},{3,7},{4,0},{5,1},{6,2},{7,3},{8,12},{9,13},{10,... | collective-permute-start | bytes 393224 | tf_op jit(solution)/shard_map/ppermute | solution.py:471
  152.7 24.5 %collective-permute-start.21 = (f32[128,256]{1,0:T(8,128)S(1)}, f32[128,256]{1,0:T(8,128)S(1)}, u32[]{:S(2)}, u32[]{:S(2)}) collective-permute-start(f32[128,256]{1,0:T(8,128)S(1)} %get-tuple-element.70), channel_id=1, source_target_pairs={{0,2},{1,3},{2,4},{3,5},{4,6},{5,7},{6,0},{7,1},{8,10},{9,11},{10,... | collective-permute-start | bytes 393224 | tf_op jit(solution)/shard_map/ppermute | solution.py:471
  192.2 26.2 %collective-permute-start.25 = (f32[8,128,256]{2,1,0:T(8,128)S(1)}, f32[8,128,256]{2,1,0:T(8,128)S(1)}, u32[]{:S(2)}, u32[]{:S(2)}) collective-permute-start(f32[8,128,256]{2,1,0:T(8,128)S(1)} %constant_dynamic-update-slice_fusion.5.refs_4_), channel_id=1, source_target_pairs={{0,16},{1,17},{2,18},{3,19},{4,20},{5,21},{6,22},{7,23},{8,24},{9,... | collective-permute-start | bytes 3145736 | tf_op jit(solution)/shard_map/ppermute | solution.py:471
  201.5 34.7 %collective-permute-start.11 = (f32[8,128,256]{2,1,0:T(8,128)S(1)}, f32[8,128,256]{2,1,0:T(8,128)}, u32[]{:S(2)}, u32[]{:S(2)}) collective-permute-start(f32[8,128,256]{2,1,0:T(8,128)S(1)} %constant_dynamic-update-slice_fusion.refs_0_), channel_id=1, source_target_pairs={{0,16},{1,17},{2,18},{3,19},{4,20},{5,21},{6,22},{7,23},{8,24},{9,... | collective-permute-start | bytes 3145736 | tf_op jit(solution)/shard_map/ppermute | solution.py:471
  202.9 37.8 %collective-permute-start.26 = (f32[8,128,256]{2,1,0:T(8,128)S(1)}, f32[8,128,256]{2,1,0:T(8,128)}, u32[]{:S(2)}, u32[]{:S(2)}) collective-permute-start(f32[8,128,256]{2,1,0:T(8,128)S(1)} %constant_dynamic-update-slice_fusion.5.refs_4_), channel_id=1, source_target_pairs={{0,8},{1,9},{2,10},{3,11},{4,12},{5,13},{6,14},{7,15},{8,0},{9,1},... | collective-permute-start | bytes 3145736 | tf_op jit(solution)/shard_map/ppermute | solution.py:471
  202.9 37.7 %collective-permute-start.12 = (f32[8,128,256]{2,1,0:T(8,128)S(1)}, f32[8,128,256]{2,1,0:T(8,128)}, u32[]{:S(2)}, u32[]{:S(2)}) collective-permute-start(f32[8,128,256]{2,1,0:T(8,128)S(1)} %constant_dynamic-update-slice_fusion.refs_0_), channel_id=1, source_target_pairs={{0,8},{1,9},{2,10},{3,11},{4,12},{5,13},{6,14},{7,15},{8,0},{9,1},... | collective-permute-start | bytes 3145736 | tf_op jit(solution)/shard_map/ppermute | solution.py:471
  266.1 26.1 %collective-permute-start.29 = (f32[1024,256]{1,0:T(8,128)S(1)}, f32[1024,256]{1,0:T(8,128)S(1)}, u32[]{:S(2)}, u32[]{:S(2)}) collective-permute-start(f32[1024,256]{1,0:T(8,128)S(1)} %add.413), channel_id=1, source_target_pairs={{0,16},{1,17},{2,18},{3,19},{4,20},{5,21},{6,22},{7,23},{8,24},{9,... | collective-permute-start | bytes 3145736 | tf_op jit(solution)/shard_map/ppermute | solution.py:471
  266.3 47.5 %collective-permute-start.31 = (f32[1024,256]{1,0:T(8,128)S(1)}, f32[1024,256]{1,0:T(8,128)S(1)}, u32[]{:S(2)}, u32[]{:S(2)}) collective-permute-start(f32[1024,256]{1,0:T(8,128)S(1)} %add.415), channel_id=1, source_target_pairs={{0,16},{1,17},{2,18},{3,19},{4,20},{5,21},{6,22},{7,23},{8,24},{9,... | collective-permute-start | bytes 3145736 | tf_op jit(solution)/shard_map/ppermute | solution.py:471
  292.3 25.4 %collective-permute-start.40 = (f32[1024,256]{1,0:T(8,128)S(1)}, f32[1024,256]{1,0:T(8,128)S(1)}, u32[]{:S(2)}, u32[]{:S(2)}) collective-permute-start(f32[1024,256]{1,0:T(8,128)S(1)} %add.414.first), channel_id=1, source_target_pairs={{0,8},{1,9},{2,10},{3,11},{4,12},{5,13},{6,14},{7,15},{8,0},{9,1},... | collective-permute-start | bytes 3145736 | tf_op jit(solution)/shard_map/ppermute | solution.py:471
  347.8 24.9 %collective-permute-start.37 = (f32[128,256]{1,0:T(8,128)S(1)}, f32[128,256]{1,0:T(8,128)S(1)}, u32[]{:S(2)}, u32[]{:S(2)}) collective-permute-start(f32[128,256]{1,0:T(8,128)S(1)} %fusion.21), channel_id=1, source_target_pairs={{0,4},{1,5},{2,6},{3,7},{4,0},{5,1},{6,2},{7,3},{8,12},{9,13},{10,... | collective-permute-start | bytes 393224 | tf_op jit(solution)/shard_map/ppermute | solution.py:471
  403.7 28.9 %collective-permute-start.51 = (f32[1152,256]{1,0:T(8,128)S(1)}, f32[1152,256]{1,0:T(8,128)S(1)}, u32[]{:S(2)}, u32[]{:S(2)}) collective-permute-start(f32[1152,256]{1,0:T(8,128)S(1)} %add.425), channel_id=1, source_target_pairs={{0,16},{1,17},{2,18},{3,19},{4,20},{5,21},{6,22},{7,23},{8,24},{9,... | collective-permute-start | bytes 3538952 | tf_op jit(solution)/shard_map/ppermute | solution.py:471
  406.3 50.6 %collective-permute-start.58 = (f32[1152,256]{1,0:T(8,128)S(1)}, f32[1152,256]{1,0:T(8,128)S(1)}, u32[]{:S(2)}, u32[]{:S(2)}) collective-permute-start(f32[1152,256]{1,0:T(8,128)S(1)} %add.437), channel_id=1, source_target_pairs={{0,16},{1,17},{2,18},{3,19},{4,20},{5,21},{6,22},{7,23},{8,24},{9,... | collective-permute-start | bytes 3538952 | tf_op jit(solution)/shard_map/ppermute | solution.py:471
  432.8 24.5 %collective-permute-start.52 = (f32[1152,256]{1,0:T(8,128)S(1)}, f32[1152,256]{1,0:T(8,128)S(1)}, u32[]{:S(2)}, u32[]{:S(2)}) collective-permute-start(f32[1152,256]{1,0:T(8,128)S(1)} %subtract_subtract_fusion.1.own), channel_id=1, source_target_pairs={{0,8},{1,9},{2,10},{3,11},{4,12},{5,13},{6,14},{7,15},{8,0},{9,1},... | collective-permute-start | bytes 3538952 | tf_op jit(solution)/shard_map/ppermute | solution.py:471
  469.6 54.4 %collective-permute-start.53 = (f32[4,288,512]{2,1,0:T(8,128)}, f32[4,288,512]{2,1,0:T(8,128)}, u32[]{:S(2)}, u32[]{:S(2)}) collective-permute-start(f32[4,288,512]{2,1,0:T(8,128)} %get-tuple-element.64), channel_id=1, source_target_pairs={{0,1},{1,0},{2,3},{3,2},{4,5},{5,4},{6,7},{7,6},{8,9},{9,8},{10,11... | collective-permute-start | bytes 7077896 | tf_op jit(solution)/shard_map/ppermute | solution.py:471
  482.3 91.7 %collective-permute-start.60 = (f32[4,288,512]{2,1,0:T(8,128)}, f32[4,288,512]{2,1,0:T(8,128)}, u32[]{:S(2)}, u32[]{:S(2)}) collective-permute-start(f32[4,288,512]{2,1,0:T(8,128)} %get-tuple-element.68), channel_id=1, source_target_pairs={{0,1},{1,0},{2,3},{3,2},{4,5},{5,4},{6,7},{7,6},{8,9},{9,8},{10,11... | collective-permute-start | bytes 7077896 | tf_op jit(solution)/shard_map/ppermute | solution.py:471
  525.9 53.8 %collective-permute-start.54 = (f32[288,512]{1,0:T(8,128)S(1)}, f32[288,512]{1,0:T(8,128)S(1)}, u32[]{:S(2)}, u32[]{:S(2)}) collective-permute-start(f32[288,512]{1,0:T(8,128)S(1)} %get-tuple-element.83), channel_id=1, source_target_pairs={{0,2},{1,3},{2,4},{3,5},{4,6},{5,7},{6,0},{7,1},{8,10},{9,11},{10,... | collective-permute-start | bytes 1769480 | tf_op jit(solution)/shard_map/ppermute | solution.py:471
  527.7 56.6 %collective-permute-start.56 = (f32[288,512]{1,0:T(8,128)S(1)}, f32[288,512]{1,0:T(8,128)S(1)}, u32[]{:S(2)}, u32[]{:S(2)}) collective-permute-start(f32[288,512]{1,0:T(8,128)S(1)} %get-tuple-element.84), channel_id=1, source_target_pairs={{0,6},{1,7},{2,0},{3,1},{4,2},{5,3},{6,4},{7,5},{8,14},{9,15},{10,... | collective-permute-start | bytes 1769480 | tf_op jit(solution)/shard_map/ppermute | solution.py:471
  530.2 61.5 %collective-permute-start.55 = (f32[288,512]{1,0:T(8,128)S(1)}, f32[288,512]{1,0:T(8,128)S(1)}, u32[]{:S(2)}, u32[]{:S(2)}) collective-permute-start(f32[288,512]{1,0:T(8,128)S(1)} %get-tuple-element.85), channel_id=1, source_target_pairs={{0,4},{1,5},{2,6},{3,7},{4,0},{5,1},{6,2},{7,3},{8,12},{9,13},{10,... | collective-permute-start | bytes 1769480 | tf_op jit(solution)/shard_map/ppermute | solution.py:471
  577.4 28.0 %collective-permute-start.63 = (f32[288,512]{1,0:T(8,128)S(1)}, f32[288,512]{1,0:T(8,128)S(1)}, u32[]{:S(2)}, u32[]{:S(2)}) collective-permute-start(f32[288,512]{1,0:T(8,128)S(1)} %get-tuple-element.81), channel_id=1, source_target_pairs={{0,6},{1,7},{2,0},{3,1},{4,2},{5,3},{6,4},{7,5},{8,14},{9,15},{10,... | collective-permute-start | bytes 1769480 | tf_op jit(solution)/shard_map/ppermute | solution.py:471
  579.8 51.0 %collective-permute-start.62 = (f32[288,512]{1,0:T(8,128)S(1)}, f32[288,512]{1,0:T(8,128)S(1)}, u32[]{:S(2)}, u32[]{:S(2)}) collective-permute-start(f32[288,512]{1,0:T(8,128)S(1)} %get-tuple-element.82), channel_id=1, source_target_pairs={{0,4},{1,5},{2,6},{3,7},{4,0},{5,1},{6,2},{7,3},{8,12},{9,13},{10,... | collective-permute-start | bytes 1769480 | tf_op jit(solution)/shard_map/ppermute | solution.py:471
  (78 other events, 1191.8 us)

commit v3 on v1

--- a/solution.py
+++ b/solution.py
@@ -1,3 +1,5 @@
+import functools
+
 import jax
 import jax.numpy as jnp
 from jax import lax
@@ -7,7 +9,7 @@
 
 BLOCK = 128
 AXES = ("row", "col")
-PARTS = 2
+COST = pl.CostEstimate(flops=1, bytes_accessed=1, transcendentals=0)
 
 
 def product(matrix, vector):
@@ -169,7 +171,7 @@
     )(ids, held)
 
 
-def local(rows, cols, *arguments):
+def general(rows, cols, *arguments):
     inverses = arguments[0:4]
     couplings = arguments[4:8]
     inverse_root = arguments[8]
@@ -178,8 +180,7 @@
     target_blocks = arguments[14]
     links = Links(rows, cols)
     columns = loads_root.shape[1]
-    parts = PARTS if columns % (PARTS * 128) == 0 else 1
-    width = columns // parts
+    parts, width = 1, columns
     children, count = target_blocks.shape
     per_row = couplings[0].shape[0] // BLOCK
     owned = loads_root.shape[0] // BLOCK
@@ -219,6 +220,636 @@
     return tuple(jnp.concatenate(list(pieces), axis=1) for pieces in zip(*answers))
 
 
+def split(value):
+    high = value.astype(jnp.bfloat16)
+    return high, (value - high.astype(jnp.float32)).astype(jnp.bfloat16)
+
+
+def dot(first, second, flip=False):
+    dims = (((0 if flip else 1,), (0,)), ((), ()))
+
+    def one(a, b):
+        return lax.dot_general(a, b, dims, preferred_element_type=jnp.float32)
+
+    return one(first[0], second[0]) + (one(first[0], second[1]) + one(first[1], second[0]))
+
+
+class Sequence:
+    def __init__(self, me):
+        self.me = me
+        self.last = me
+
+    def __call__(self, kernel, inputs, outputs, scratch=(), limit=24):
+        whole = pl.BlockSpec(memory_space=pltpu.VMEM)
+        count = len(inputs)
+        results = pl.pallas_call(
+            lambda *refs: kernel(*refs[: count + 1], *refs[count + 2 :]),
+            in_specs=[pl.BlockSpec(memory_space=pltpu.SMEM)]
+            + [whole] * count
+            + [pl.BlockSpec(memory_space=pl.ANY)],
+            out_specs=[whole] * len(outputs),
+            out_shape=list(outputs),
+            scratch_shapes=list(scratch),
+            cost_estimate=COST,
+            compiler_params=pltpu.CompilerParams(vmem_limit_bytes=limit * 2**20),
+        )(self.me, *inputs, self.last)
+        self.last = results[0]
+        return results
+
+    def merge(self, inputs, signs=None):
+        signs = signs or (1,) * len(inputs)
+
+        def kernel(me, *refs):
+            refs[-1][...] = total([ref[...] for ref in refs[:-1]], signs)
+
+        return self(kernel, inputs, [shape(*inputs[0].shape)])[0]
+
+    def merge_split(self, inputs):
+        count = inputs[0].shape[0]
+
+        def kernel(me, *refs):
+            sources, outs = refs[: len(inputs)], refs[len(inputs) :]
+            for place in range(count):
+                outs[place][...] = total([ref[place] for ref in sources], (1,) * len(inputs))
+
+        return self(kernel, inputs, [shape(*inputs[0].shape[1:])] * count)
+
+    def stack(self, inputs):
+        def kernel(me, *refs):
+            for place, ref in enumerate(refs[:-1]):
+                refs[-1][place] = ref[...]
+
+        return self(kernel, inputs, [shape(len(inputs), *inputs[0].shape)])[0]
+
+    def join(self, inputs):
+        rows = [a.shape[0] for a in inputs]
+
+        def kernel(me, *refs):
+            start = 0
+            for ref, count in zip(refs[:-1], rows):
+                refs[-1][start : start + count] = ref[...]
+                start += count
+
+        return self(kernel, inputs, [shape(sum(rows), *inputs[0].shape[1:])])[0]
+
+
+def total(values, signs):
+    result = values[0]
+    for value, sign in zip(values[1:], signs[1:]):
+        result = result + value if sign > 0 else result - value
+    return result
+
+
+def shape(*extent):
+    return jax.ShapeDtypeStruct(extent, jnp.float32)
+
+
+def part_of(half, part, width):
+    parts = 2
+    return pl.ds(pl.multiple_of((half * parts + part) * width, width), width)
+
+
+def forward_kernel(parts, me, *refs):
+    count = (len(refs) - 2 * len(parts)) // 2
+    outs = refs[2 * count :]
+    width = outs[0].shape[1]
+    start = 0
+    for weight, loads in zip(refs[:count], refs[count : 2 * count]):
+        rows = weight.shape[0]
+        pieces = [
+            loads[:, part_of(half, part, width)] for part in parts for half in (me[0], 1 - me[0])
+        ]
+        value = dot(split(weight[...]), split(jnp.concatenate(pieces, axis=1)))
+        for place, out in enumerate(outs):
+            out[start : start + rows] = value[:, place * width : (place + 1) * width]
+        start += rows
+
+
+def couple_kernel(me, *refs):
+    y, z = me[1], me[2]
+    keep, send = refs[-2:]
+    count = keep.shape[0]
+    for child in range(count):
+        weight, (own, other, start) = refs[child], refs[count + child]
+        rows = weight.shape[1]
+        span = slice(start, start + rows)
+        held = jnp.concatenate([own[span], other[span]], axis=1)
+        value = dot(split(weight[...]), split(held))
+        place = lax.rem(child + count - z, count)
+
+        @pl.when(y == 0)
+        def _():
+            keep[place] = value[:BLOCK]
+            send[place] = value[BLOCK:]
+
+        @pl.when(y != 0)
+        def _():
+            keep[place] = value[BLOCK:]
+            send[place] = value[:BLOCK]
+
+
+def base_kernel(me, weight, mine, theirs, last, out, high, low):
+    @pl.when(pl.program_id(0) == 0)
+    def _():
+        high[...], low[...] = split(jnp.concatenate([mine[...], theirs[...]], axis=1))
+
+    out[...] = dot(split(weight[...]), (high[...], low[...]))
+
+
+def base(sequence, part, piece, width, weight, loads):
+    rows, depth = weight.shape[0] // 2, weight.shape[1]
+    steps = 4
+    tile = rows // steps
+    parts = 2
+    result = pl.pallas_call(
+        base_kernel,
+        grid_spec=pltpu.PrefetchScalarGridSpec(
+            num_scalar_prefetch=1,
+            grid=(steps,),
+            in_specs=[
+                pl.BlockSpec((tile, depth), lambda i, me: (piece * steps + i, 0)),
+                pl.BlockSpec((depth, width), lambda i, me: (0, me[0] * parts + part)),
+                pl.BlockSpec((depth, width), lambda i, me: (0, (1 - me[0]) * parts + part)),
+                pl.BlockSpec(memory_space=pl.ANY),
+            ],
+            out_specs=pl.BlockSpec((tile, 2 * width), lambda i, me: (i, 0)),
+            scratch_shapes=[pltpu.VMEM((depth, 2 * width), jnp.bfloat16)] * 2,
+        ),
+        out_shape=shape(rows, 2 * width),
+        cost_estimate=COST,
+        compiler_params=pltpu.CompilerParams(vmem_limit_bytes=40 * 2**20),
+    )(sequence.me, weight, loads, loads, sequence.last)
+    sequence.last = result
+    return result
+
+
+def root_kernel(list_ref, left, right, upper, lower, *refs):
+    sources, (own, other, moved) = refs[:-4], refs[-3:]
+    step = pl.program_id(0)
+    width = own.shape[1]
+    rows = own.shape[0]
+
+    @pl.when(step == 0)
+    def _():
+        for start, ref in ((0, upper), (rows // 2, lower)):
+            own[start : start + rows // 2] = ref[:, :width]
+            other[start : start + rows // 2] = ref[:, width:]
+
+    @pl.when(2 * step < list_ref[3, 0])
+    def _():
+        for entry in range(2):
+            span = slice(entry * BLOCK, (entry + 1) * BLOCK)
+            which = list_ref[1, 2 * step + entry]
+            place = list_ref[2, 2 * step + entry]
+
+            @pl.when(which < 0)
+            def _():
+                moved[span] = jnp.zeros((BLOCK, 2 * width), jnp.float32)
+
+            for number, source in enumerate(sources):
+
+                @pl.when(which == number)
+                def _():
+                    if number < 2:
+                        moved[span] = source[place]
+                    else:
+                        moved[span, :width] = source[place, :, width:]
+                        moved[span, width:] = source[place, :, :width]
+
+        held = split(moved[...])
+        tile = rows // 4
+        for start in range(0, rows, tile):
+            span = slice(start, start + tile)
+            weight = split(jnp.concatenate([left[span], right[span]], axis=1))
+            value = dot(weight, held)
+            own[span] -= value[:, :width]
+            other[span] -= value[:, width:]
+
+
+def root(sequence, listed, weight, starts, sources):
+    rows = weight.shape[0]
+    width = starts[0].shape[1] // 2
+    whole = pl.BlockSpec(memory_space=pltpu.VMEM)
+    results = pl.pallas_call(
+        root_kernel,
+        grid_spec=pltpu.PrefetchScalarGridSpec(
+            num_scalar_prefetch=1,
+            grid=(listed.shape[1] // 2,),
+            in_specs=[
+                pl.BlockSpec((rows, BLOCK), lambda i, listed: (0, listed[0, 2 * i])),
+                pl.BlockSpec((rows, BLOCK), lambda i, listed: (0, listed[0, 2 * i + 1])),
+            ]
+            + [whole] * (2 + len(sources))
+            + [pl.BlockSpec(memory_space=pl.ANY)],
+            out_specs=[whole] * 2,
+            scratch_shapes=[pltpu.VMEM((2 * BLOCK, 2 * width), jnp.float32)],
+        ),
+        out_shape=[shape(rows, width)] * 2,
+        cost_estimate=COST,
+        compiler_params=pltpu.CompilerParams(vmem_limit_bytes=40 * 2**20),
+    )(listed, weight, weight, *starts, *sources, sequence.last)
+    sequence.last = results[0]
+    return results
+
+
+def pick_kernel(me, own, other, keep, send):
+    y, z = me[1], me[2]
+    count = own.shape[0] // BLOCK
+    width = own.shape[1]
+    children = keep.shape[0]
+    for out, block in ((send, 1 - y), (keep, y)):
+        for child in range(children):
+            place = lax.rem(child + children - z, children)
+            source = me[3 + 2 * child + block]
+            inside = jnp.logical_and(source >= 0, source < count)
+
+            @pl.when(inside)
+            def _():
+                span = pl.ds(pl.multiple_of(source * BLOCK, BLOCK), BLOCK)
+                out[place, :, :width] = own[span]
+                out[place, :, width:] = other[span]
+
+            @pl.when(jnp.logical_not(inside))
+            def _():
+                out[place] = jnp.zeros((BLOCK, 2 * width), jnp.float32)
+
+
+def correct_kernel(pair, me, first, second, near, far, own, other, rows_ref):
+    y, z = me[1], me[2]
+    width = own.shape[1]
+    children = near.shape[0]
+    start = 0
+    for child, weight in zip(pair, (first, second)):
+        rows = weight.shape[1]
+        place = lax.rem(z + children - child, children)
+        rows_ref[pl.ds(pl.multiple_of(y * BLOCK, BLOCK), BLOCK)] = near[place]
+        rows_ref[pl.ds(pl.multiple_of((1 - y) * BLOCK, BLOCK), BLOCK)] = far[place]
+        value = dot(split(weight[...]), split(rows_ref[...]), True)
+        own[start : start + rows] = value[:, :width]
+        other[start : start + rows] = value[:, width:]
+        start += rows
+
+
+def final_kernel(me, first, second, own, other, keep, send, whole):
+    y, z = me[1], me[2]
+    count = keep.shape[0]
+    width = own.shape[1]
+    start, place = 0, 0
+    for weight in (first, second):
+        rows, columns = weight.shape
+        size = columns // (2 * count)
+        span = slice(start, start + rows)
+        held = jnp.concatenate([own[span], other[span]], axis=1)
+        value = dot(split(weight[...]), split(held), True)
+        whole[:columns, pl.ds(pl.multiple_of(me[0] * width, width), width)] = value[:, :width]
+        whole[:columns, pl.ds(pl.multiple_of((1 - me[0]) * width, width), width)] = value[:, width:]
+        for out, side in ((send, 1 - y), (keep, y)):
+            for owner in range(count):
+                taken = pl.ds(pl.multiple_of((2 * owner + side) * size, 8), size)
+                out[jnp.bitwise_xor(owner, z), place : place + size] = whole[taken]
+        start += rows
+        place += size
+
+
+def halve_kernel(me, keep, arrived, send, held):
+    for place in range(keep.shape[0]):
+        out = send if place % 2 else held
+        out[place // 2] = keep[place] + arrived[place]
+
+
+def finish_kernel(terms, me, *refs):
+    parts = len(terms)
+    held = iter(refs[:-2])
+    first, second = refs[-2:]
+    rows = first.shape[0]
+    width = first.shape[1] // (2 * parts)
+    for part in range(parts):
+        value = total([next(held)[...] for _ in range(terms[part])], (1,) * terms[part])
+        for half in range(2):
+            there = slice((half * parts + part) * width, (half * parts + part + 1) * width)
+            here = slice(half * width, (half + 1) * width)
+            first[:, there] = value[:rows, here]
+            second[:, there] = value[rows:, here]
+
+
+def whole_kernel(me, *refs):
+    out = refs[-1]
+    width = refs[0].shape[1]
+    for part in range(2):
+        out[:, part_of(me[0], part, width)] = refs[2 * part][...]
+        out[:, part_of(1 - me[0], part, width)] = refs[2 * part + 1][...]
+
+
+def fast(rows, cols, *arguments):
+    inverses = arguments[0:4]
+    couplings = arguments[4:8]
+    inverse_root = arguments[8]
+    sources = arguments[9:13]
+    loads_root = arguments[13]
+    target_blocks = arguments[14]
+    links = Links(rows, cols)
+    core, x, y, z = links.core, links.x, links.y, links.z
+    width = loads_root.shape[1] // 4
+    children, count = target_blocks.shape
+    per_row = count // rows
+    owned = loads_root.shape[0] // BLOCK
+    held = inverse_root.shape[0] // BLOCK
+    row = lax.axis_index("row")
+    pairs = ((0, 3), (1, 2))
+
+    def send(array, group, step=1):
+        return lax.ppermute(array, AXES, group.pairs[step - 1])
+
+    def spread(array, group):
+        return [send(array, group, step) for step in range(1, group.size)]
+
+    def deal(arrays, group):
+        return [send(arrays[step], group, step) for step in range(1, group.size)]
+
+    mine = lax.dynamic_slice_in_dim(target_blocks, row * per_row, per_row, 1)
+    wanted = (mine - lax.axis_index("col") * held).reshape(-1)
+    me = jnp.concatenate([jnp.stack([core.place, y.place, z.place]).astype(jnp.int32), wanted])
+
+    child = jnp.arange(children, dtype=jnp.int32)[:, None] + jnp.zeros((1, count), jnp.int32)
+    block = jnp.arange(count, dtype=jnp.int32)[None, :] + jnp.zeros((children, 1), jnp.int32)
+    from_row = block // per_row
+    away_x = jnp.where(from_row // 2 == x.place, 0, 1)
+    away_core = jnp.where(from_row % 2 == core.place, 0, 1)
+    away_y = jnp.where(block % per_row == y.place, 0, 1)
+    place = (z.place + z.size - child) % z.size
+    local_block = target_blocks - row * owned
+    inside = ((local_block >= 0) & (local_block < owned)).reshape(-1)
+    rank = jnp.cumsum(inside.astype(jnp.int32)) - 1
+    entries = jnp.arange(inside.shape[0], dtype=jnp.int32)
+    chosen = inside[None, :] & (rank[None, :] == entries[:, None])
+    tables = (
+        (local_block, away_core * 2 + away_x + 1, away_y * z.size + place),
+        (local_block, away_core * 2 + away_y + 1, place * x.size + away_x),
+    )
+    found = jnp.sum(inside.astype(jnp.int32))
+    listed = []
+    for table in tables:
+        rows_of = jnp.stack(table).reshape(3, -1)
+        held_rows = jnp.sum(jnp.where(chosen[None], rows_of[:, None, :], 0), axis=2)
+        last = jnp.sum(jnp.where(entries == found - 1, held_rows[0], 0))
+        listed.append(
+            jnp.stack(
+                [
+                    jnp.where(entries < found, held_rows[0], last),
+                    held_rows[1] - 1,
+                    held_rows[2],
+                    jnp.zeros_like(entries) + found,
+                ]
+            )
+        )
+
+    run = Sequence(me)
+    parts = range(2)
+    state = [dict() for _ in parts]
+
+    def forward_start(pair, chosen):
+        weights = [inverses[k] for k in pair]
+        loads = [sources[k] for k in pair]
+        n = sum(weight.shape[0] for weight in weights)
+        outs = run(
+            functools.partial(forward_kernel, chosen),
+            weights + loads,
+            [shape(n, width)] * (2 * len(chosen)),
+            limit=56,
+        )
+        return [(own, send(other, core)) for own, other in zip(outs[::2], outs[1::2])]
+
+    def forward_cross(own, arrived):
+        own = run.merge([own, arrived])
+        return own, send(own, x)
+
+    def forward_end(own, arrived):
+        own = run.merge([own, arrived])
+        return own, send(own, core)
+
+    def couple(part, arrays):
+        flat = [a for own, other, _ in arrays for a in (own, other)]
+        firsts = [start for _, _, start in arrays]
+
+        def kernel(me, *refs):
+            held = refs[children : 3 * children]
+            triples = [(held[2 * k], held[2 * k + 1], firsts[k]) for k in range(children)]
+            couple_kernel(me, *refs[:children], *triples, *refs[3 * children :])
+
+        piece = shape(z.size, BLOCK, 2 * width)
+        keep, sent = run(kernel, list(couplings) + flat, [piece] * 2, limit=40)
+        state[part]["keep"], state[part]["arrived"] = keep, send(sent, y)
+
+    def sum_y(part):
+        split_up = run.merge_split([state[part]["keep"], state[part]["arrived"]])
+        state[part]["terms"] = [split_up[0]] + deal(split_up, z)
+
+    def sum_z(part):
+        value = run.merge(state[part]["terms"])
+        state[part]["pieces"] = [value] + spread(value, z)
+
+    def gather_z(part):
+        near = run.stack(state[part]["pieces"])
+        state[part]["near"], state[part]["far"] = near, send(near, y)
+
+    def gather_y(part):
+        near = run.join([state[part]["near"], state[part]["far"]])
+        far = send(near, x)
+        state[part]["blocks"] = [near, far, send(near, core), send(far, core)]
+
+    def gather_x(part):
+        value = run.merge(state[part]["terms"])
+        state[part]["pieces"] = [value, send(value, x)]
+
+    def spread_z(part):
+        both = run.stack(state[part]["pieces"])
+        state[part]["pieces"] = [both] + spread(both, z)
+
+    def join_z(part):
+        near = run.join(state[part]["pieces"])
+        far = send(near, y)
+        state[part]["blocks"] = [near, far, send(near, core), send(far, core)]
+
+    def solve_root(part):
+        own, other = root(run, listed[part], inverse_root, state[part]["base"], state[part]["blocks"])
+        state[part]["root"] = own, send(other, core)
+
+    def cross_root(part):
+        own = run.merge(list(state[part]["root"]))
+        state[part]["root"] = own, send(own, x)
+
+    def end_root(part):
+        own = run.merge(list(state[part]["root"]))
+        state[part]["root"] = own, send(own, core)
+
+    def pick_root(part):
+        piece = shape(children, BLOCK, 2 * width)
+        keep, sent = run(pick_kernel, list(state[part]["root"]), [piece] * 2)
+        state[part]["keep"], state[part]["arrived"] = keep, send(sent, y)
+
+    def correct(part, group):
+        pair = pairs[group]
+        weights = [couplings[k] for k in pair]
+        own, other = run(
+            functools.partial(correct_kernel, pair),
+            weights + [state[part]["near"], state[part]["far"]],
+            [shape(sum(weight.shape[1] for weight in weights), width)] * 2,
+            [pltpu.VMEM((per_row * BLOCK, 2 * width), jnp.float32)],
+        )
+        state[part][group] = own, send(other, core)
+
+    def correct_cross(part, group):
+        own = run.merge(list(state[part][group]))
+        state[part][group] = own, send(own, x)
+
+    def reduce(part, group):
+        first = forward[part][group][0]
+        own = run.merge([first] + list(state[part][group]), (1, -1, -1))
+        state[part][group] = own, send(own, core)
+
+    def final(part, group):
+        weights = [inverses[k] for k in pairs[group]]
+        size = sum(weight.shape[1] for weight in weights) // cols
+        keep, sent = run(
+            final_kernel,
+            weights + list(state[part][group]),
+            [shape(z.size, size, 2 * width)] * 2,
+            [pltpu.VMEM((max(weight.shape[1] for weight in weights), 2 * width), jnp.float32)],
+            limit=40,
+        )
+        state[part][group] = keep, send(sent, y)
+
+    def exchange(array, mask):
+        flip = mask * y.size
+        listed = [(r * cols + c, r * cols + (c ^ flip)) for r in range(rows) for c in range(cols)]
+        return lax.ppermute(array, AXES, listed)
+
+    def final_y(part, group):
+        keep, arrived = state[part][group]
+        half = shape(z.size // 2, *keep.shape[1:])
+        sent, held = run(halve_kernel, [keep, arrived], [half] * 2)
+        state[part][group] = held, exchange(sent, 1)
+
+    def final_z(part, group):
+        held, away = run.merge_split(list(state[part][group]))
+        state[part][group] = [held, exchange(away, 2)]
+
+    def finish(group):
+        sizes = [inverses[k].shape[1] // cols for k in pairs[group]]
+        outs = [shape(size, 4 * width) for size in sizes]
+        terms = [len(state[part][group]) for part in parts]
+        inputs = [a for part in parts for a in state[part][group]]
+        return run(functools.partial(finish_kernel, terms), inputs, outs)
+
+    def final_last(part, group):
+        state[part][group] = [run.merge(state[part][group])]
+
+    def by_child(part):
+        arrays = [None] * children
+        for (a, b), (own, other) in zip(pairs, forward[part]):
+            arrays[a] = own, other, 0
+            arrays[b] = own, other, couplings[a].shape[1]
+        return arrays
+
+    def start_root(part, piece):
+        held = base(run, part, piece, width, inverse_root, loads_root)
+        state[part].setdefault("base", []).append(held)
+
+    def forward_begin(chosen):
+        begun = [forward_start(pair, chosen) for pair in pairs]
+        return [[forward_cross(*pieces[k]) for pieces in begun] for k in range(len(chosen))]
+
+    crossed = forward_begin((0, 1))
+    start_root(0, 0)
+    start_root(0, 1)
+    forward = [None, None]
+    forward[0] = [forward_end(*piece) for piece in crossed[0]]
+    couple(0, by_child(0))
+    start_root(1, 0)
+    sum_y(0)
+    start_root(1, 1)
+    sum_z(0)
+    forward[1] = [forward_end(*piece) for piece in crossed[1]]
+    couple(1, by_child(1))
+    gather_z(0)
+    sum_y(1)
+    gather_y(0)
+    gather_x(1)
+    spread_z(1)
+    solve_root(0)
+    join_z(1)
+    cross_root(0)
+    end_root(0)
+    solve_root(1)
+    pick_root(0)
+    cross_root(1)
+    sum_y(0)
+    end_root(1)
+    sum_z(0)
+    pick_root(1)
+    gather_z(0)
+    sum_y(1)
+    (solved_root,) = run(
+        whole_kernel,
+        [a for part in parts for a in state[part]["root"]],
+        [shape(inverse_root.shape[0], 4 * width)],
+    )
+    correct(0, 0)
+    correct(0, 1)
+    correct_cross(0, 0)
+    correct_cross(0, 1)
+    sum_z(1)
+    reduce(0, 0)
+    gather_z(1)
+    final(0, 0)
+    reduce(0, 1)
+    correct(1, 0)
+    correct(1, 1)
+    final(0, 1)
+    correct_cross(1, 0)
+    correct_cross(1, 1)
+    final_y(0, 0)
+    reduce(1, 0)
+    final_z(0, 0)
+    final(1, 0)
+    reduce(1, 1)
+    final_y(0, 1)
+    final(1, 1)
+    final_last(0, 0)
+    final_z(0, 1)
+    final_y(1, 0)
+    final_last(0, 1)
+    final_z(1, 0)
+    final_y(1, 1)
+    final_last(1, 0)
+    final_z(1, 1)
+    solved = [None] * 4
+    for group, (a, b) in enumerate(pairs):
+        solved[a], solved[b] = finish(group)
+    return tuple(solved) + (solved_root,)
+
+
+def local(rows, cols, *arguments):
+    links = Links(rows, cols)
+    children, count = arguments[14].shape
+    columns = arguments[13].shape[1]
+    sizes = [arguments[k].shape[1] for k in range(4)]
+    fits = (
+        links.core.size == 2
+        and links.x.size == 2
+        and links.y.size == 2
+        and children == 4
+        and links.z.size == 4
+        and count == 2 * rows
+        and arguments[4].shape[0] == 2 * BLOCK
+        and columns % 512 == 0
+        and arguments[8].shape[0] % (16 * BLOCK) == 0
+        and all(size % (cols * 16) == 0 for size in sizes)
+        and all(arguments[k].shape[0] % 16 == 0 for k in range(4))
+    )
+    return (fast if fits else general)(rows, cols, *arguments)
+
+
 def solution(mesh):
     rows, cols = mesh.shape["row"], mesh.shape["col"]
     matrices = [P("col", "row")] * 4 + [P("row", "col")] * 4 + [P("col", "row")]

time: 798 us -> 525 us (0.66)
  matrix products: 128 us -> 0 us
  local copies, waits for them, and re-layouts: 145 us -> 17 us
  Pallas kernels: 41.3 us -> 155 us
  other arithmetic: 85.5 us -> 14.7 us
  starting transfers between devices: 139 us -> 103 us
  waiting for transfers between devices: 241 us -> 226 us
    dot_general x34 -> x0, matrix products: 128 us -> none  [the longest x18 85.7 us: product(): jnp.dot(matrix, vector, precision=lax.Precision.HIGH, preferred_element_t...]
    pallas_call x4 -> x68, Pallas kernels: 41.3 us -> 155 us  [the longest x62 87.7 us: __call__(): pl.pallas_call(lambda *refs: kernel(*refs[:count + 1], *refs[count + 2:])...]
    add x57 -> x4, other arithmetic: 42.1 us -> 3.61 us  [the longest x1 1.27 us: fast(): away_core * 2 + away_x + 1]
    ppermute x122 -> x80, starting transfers between devices: 139 us -> 103 us  [the longest x72 80 us: send(): return lax.ppermute(array, AXES, group.pairs[step - 1])]
    squeeze x38 -> x0, local copies, waits for them, and re-layouts: 34.2 us -> none  [pick(): return lax.dynamic_index_in_dim(array, index, axis, keepdims=False)]
    dynamic_slice x7 -> x0, local copies, waits for them, and re-layouts: 31.2 us -> none  [pick(): return lax.dynamic_index_in_dim(array, index, axis, keepdims=False)]
    another operation x52 -> x3, other arithmetic: 31.6 us -> 2.07 us  [gather(): jnp.stack([jnp.where(first, held[0], held[1]), jnp.where(first, held[1],...]
    dot_general x10 -> x0, local copies, waits for them, and re-layouts: 24.6 us -> none  [transposed(): lax.dot_general(matrix, vector, (((0,), (0,)), ((), ())), precision=lax.P...]
  transfers between devices with their start and end apart: 122 -> 80, of which waited for: 46 -> 39; matrix products, arithmetic and copies ran while one was open for 43% -> 4% of each run, Pallas kernels for 5% -> 26%
where the time goes in v3:
time: 525 us; the launch traced here: 518 us
  waiting for transfers between devices  226 us (43%)
  Pallas kernels  155 us (30%)
  starting transfers between devices  103 us (20%)
  local copies, waits for them, and re-layouts  17 us (3%)
  other arithmetic  14.7 us (3%)
    ppermute x72, waiting for transfers between devices, send(): return lax.ppermute(array, AXES, group.pairs[step - 1])  164 us
    pallas_call x62, Pallas kernels, __call__(): pl.pallas_call(lambda *refs: kernel(*refs[:count + 1], *refs[count + 2:])...  87.7 us
    ppermute x72, starting transfers between devices, send(): return lax.ppermute(array, AXES, group.pairs[step - 1])  80 us
    ppermute x8, waiting for transfers between devices, exchange(): return lax.ppermute(array, AXES, listed)  62 us
    pallas_call x4, Pallas kernels, base(): pl.pallas_call(base_kernel, grid_spec=pltpu.PrefetchScalarGridSpec(num_sc...  45.4 us
    ppermute x8, starting transfers between devices, exchange(): return lax.ppermute(array, AXES, listed)  22.9 us
    pallas_call x2, Pallas kernels, root(): pl.pallas_call(root_kernel, grid_spec=pltpu.PrefetchScalarGridSpec(num_sc...  22.3 us
    unnamed x78, local copies, waits for them, and re-layouts  11.7 us
  transfers between devices with their start and end apart: 80, of which 39 were waited for; matrix products, arithmetic and copies ran while one was open for 4% of the time, Pallas kernels for 26%

profile of v3, /device:TPU:0, one launch (start us, length us, event | category | flops | bytes accessed | tf_op | source)
XLA Modules:
  0.0 518.1 jit_solution(16746330036796290284)
XLA Ops:
  2.1 10.4 %shard_map.182 = (f32[1152,128]{1,0:T(8,128)}, f32[1152,128]{1,0:T(8,128)}, f32[1152,128]{1,0:T(8,128)}, f32[1152,128]{1,0:T(8,128)}) custom-call(s32[11]{0:T(128)} %pad_add_fusion.4.refs_0_.refs_5_.me, f32[768,1536]{1,0:T(8,128)} %refs_1_.22, f32[384,768]{1,0:T(8,128)} %refs_2_.22, f32[1536,512]{1,0:T(8,128)} %refs_3_.4, f32[768,512]{1,0:T(8,128)} %refs_4_.4, ...), custom_call_target="tpu_custom_call" | custom-call | flops 1 | bytes 1 | tf_op jit(solution)/shard_map/pallas_call | solution.py:245
  13.0 10.1 %shard_map.183 = (f32[1152,128]{1,0:T(8,128)}, f32[1152,128]{1,0:T(8,128)}, f32[1152,128]{1,0:T(8,128)}, f32[1152,128]{1,0:T(8,128)}) custom-call(s32[11]{0:T(128)} %pad_add_fusion.4.refs_0_.refs_5_.me, f32[640,1280]{1,0:T(8,128)} %refs_1_.23, f32[512,1024]{1,0:T(8,128)} %refs_2_.23, f32[1280,512]{1,0:T(8,128)} %refs_3_.5, f32[1024,512]{1,0:T(8,128)} %refs_4_.5, ...), custom_call_target="tpu_custom_call" | custom-call | flops 1 | bytes 1 | tf_op jit(solution)/shard_map/pallas_call | solution.py:245
  31.4 11.4 %shard_map.188.last.upper = f32[1024,256]{1,0:T(8,128)S(1)} custom-call(s32[11]{0:T(128)S(1)} %copy-done.21, f32[2048,4096]{1,0:T(8,128)} %right.3, f32[4096,512]{1,0:T(8,128)S(1)} %copy-done, f32[4096,512]{1,0:T(8,128)S(1)} %copy-done, f32[1152,128]{1,0:T(8,128)S(1)} %shard_map.187.last.refs_1_), custom_call_target="tpu_custom_call" | custom-call | flops 1 | bytes 1 | tf_op jit(solution)/shard_map/pallas_call | solution.py:364
  42.8 11.2 %shard_map.189.refs_3_.lower = f32[1024,256]{1,0:T(8,128)S(1)} custom-call(s32[11]{0:T(128)S(1)} %copy-done.21, f32[2048,4096]{1,0:T(8,128)} %right.3, f32[4096,512]{1,0:T(8,128)S(1)} %copy-done, f32[4096,512]{1,0:T(8,128)S(1)} %copy-done, f32[1024,256]{1,0:T(8,128)S(1)} %shard_map.188.last.upper), custom_call_target="tpu_custom_call" | custom-call | flops 1 | bytes 1 | tf_op jit(solution)/shard_map/pallas_call | solution.py:364
  65.3 11.2 %shard_map.193.refs_3_.upper = f32[1024,256]{1,0:T(8,128)S(1)} custom-call(s32[11]{0:T(128)S(1)} %copy-done.21, f32[2048,4096]{1,0:T(8,128)} %right.3, f32[4096,512]{1,0:T(8,128)S(1)} %copy-done, f32[4096,512]{1,0:T(8,128)S(1)} %copy-done, f32[4,128,256]{2,1,0:T(8,128)S(1)} %get-tuple-element.85.last.refs_1_), custom_call_target="tpu_custom_call" | custom-call | flops 1 | bytes 1 | tf_op jit(solution)/shard_map/pallas_call | solution.py:364
  83.6 11.6 %shard_map.195.refs_5_.lower = f32[1024,256]{1,0:T(8,128)S(1)} custom-call(s32[11]{0:T(128)S(1)} %copy-done.21, f32[2048,4096]{1,0:T(8,128)} %right.3, f32[4096,512]{1,0:T(8,128)S(1)} %copy-done, f32[4096,512]{1,0:T(8,128)S(1)} %copy-done, f32[128,256]{1,0:T(8,128)S(1)} %get-tuple-element.87.last.refs_1_), custom_call_target="tpu_custom_call" | custom-call | flops 1 | bytes 1 | tf_op jit(solution)/shard_map/pallas_call | solution.py:364
  116.0 21.9 %collective-permute-done.20.refs_2_ = f32[4,128,256]{2,1,0:T(8,128)S(1)} collective-permute-done((f32[4,128,256]{2,1,0:T(8,128)S(1)}, f32[4,128,256]{2,1,0:T(8,128)S(1)}, u32[]{:S(2)}, u32[]{:S(2)}) %collective-permute-start.20) | collective-permute-done | bytes 524320 | tf_op jit(solution)/shard_map/ppermute | solution.py:561
  153.2 12.2 %collective-permute-done.21.refs_1_ = f32[8,128,256]{2,1,0:T(8,128)} collective-permute-done((f32[8,128,256]{2,1,0:T(8,128)}, f32[8,128,256]{2,1,0:T(8,128)}, u32[]{:S(2)}, u32[]{:S(2)}) %collective-permute-start.21) | collective-permute-done | bytes 1048608 | tf_op jit(solution)/shard_map/ppermute | solution.py:561
  177.2 5.3 %collective-permute-done.25.refs_3_ = f32[128,256]{1,0:T(8,128)} collective-permute-done((f32[128,256]{1,0:T(8,128)}, f32[128,256]{1,0:T(8,128)}, u32[]{:S(2)}, u32[]{:S(2)}) %collective-permute-start.25) | collective-permute-done | bytes 131104 | tf_op jit(solution)/shard_map/ppermute | solution.py:561
  199.0 11.9 %shard_map.205 = (f32[2048,128]{1,0:T(8,128)S(1)}, f32[2048,128]{1,0:T(8,128)S(1)}) custom-call(s32[4,32]{1,0:T(4,128)S(1)} %get-tuple-element.166.list_ref, f32[2048,4096]{1,0:T(8,128)} %right.3, f32[2048,4096]{1,0:T(8,128)} %right.3, f32[1024,256]{1,0:T(8,128)S(1)} %copy-done.16, f32[1024,256]{1,0:T(8,128)S(1)} %copy-done.10, ...), custom_call_target="tpu_custom_call" | custom-call | flops 1 | bytes 1 | tf_op jit(solution)/shard_map/pallas_call | solution.py:433
  216.7 21.8 %collective-permute-done.34.refs_1_ = f32[8,128,256]{2,1,0:T(8,128)S(1)} collective-permute-done((f32[8,128,256]{2,1,0:T(8,128)S(1)}, f32[8,128,256]{2,1,0:T(8,128)S(1)}, u32[]{:S(2)}, u32[]{:S(2)}) %collective-permute-start.34) | collective-permute-done | bytes 1048608 | tf_op jit(solution)/shard_map/ppermute | solution.py:561
  241.1 10.4 %shard_map.209 = (f32[2048,128]{1,0:T(8,128)S(1)}, f32[2048,128]{1,0:T(8,128)S(1)}) custom-call(s32[4,32]{1,0:T(4,128)S(1)} %get-tuple-element.165.list_ref, f32[2048,4096]{1,0:T(8,128)} %right.3, f32[2048,4096]{1,0:T(8,128)} %right.3, f32[1024,256]{1,0:T(8,128)S(1)} %copy-done.12, f32[1024,256]{1,0:T(8,128)S(1)} %copy-done.14, ...), custom_call_target="tpu_custom_call" | custom-call | flops 1 | bytes 1 | tf_op jit(solution)/shard_map/pallas_call | solution.py:433
  256.0 13.0 %collective-permute-done.37.refs_2_ = f32[4,128,256]{2,1,0:T(8,128)S(1)} collective-permute-done((f32[4,128,256]{2,1,0:T(8,128)S(1)}, f32[4,128,256]{2,1,0:T(8,128)S(1)}, u32[]{:S(2)}, u32[]{:S(2)}) %collective-permute-start.37) | collective-permute-done | bytes 524320 | tf_op jit(solution)/shard_map/ppermute | solution.py:561
  269.7 10.6 %collective-permute-done.42.refs_2_ = f32[2048,128]{1,0:T(8,128)S(1)} collective-permute-done((f32[2048,128]{1,0:T(8,128)S(1)}, f32[2048,128]{1,0:T(8,128)S(1)}, u32[]{:S(2)}, u32[]{:S(2)}) %collective-permute-start.42) | collective-permute-done | bytes 1048608 | tf_op jit(solution)/shard_map/ppermute | solution.py:561
  281.0 6.2 %collective-permute-start.39 = (f32[128,256]{1,0:T(8,128)S(1)}, f32[128,256]{1,0:T(8,128)S(1)}, u32[]{:S(2)}, u32[]{:S(2)}) collective-permute-start(f32[128,256]{1,0:T(8,128)S(1)} %get-tuple-element.104), channel_id=1, source_target_pairs={{0,2},{1,3},{2,4},{3,5},{4,6},{5,7},{6,0},{7,1},{8,10},{9,11},{10,... | collective-permute-start | bytes 393224 | tf_op jit(solution)/shard_map/ppermute | solution.py:561
  291.0 5.2 %collective-permute-done.40.refs_3_ = f32[128,256]{1,0:T(8,128)S(1)} collective-permute-done((f32[128,256]{1,0:T(8,128)S(1)}, f32[128,256]{1,0:T(8,128)S(1)}, u32[]{:S(2)}, u32[]{:S(2)}) %collective-permute-start.40) | collective-permute-done | bytes 131104 | tf_op jit(solution)/shard_map/ppermute | solution.py:561
  313.5 5.4 %collective-permute-done.48.refs_2_ = f32[4,128,256]{2,1,0:T(8,128)S(1)} collective-permute-done((f32[4,128,256]{2,1,0:T(8,128)S(1)}, f32[4,128,256]{2,1,0:T(8,128)S(1)}, u32[]{:S(2)}, u32[]{:S(2)}) %collective-permute-start.48) | collective-permute-done | bytes 524320 | tf_op jit(solution)/shard_map/ppermute | solution.py:561
  322.7 5.8 %collective-permute-done.47.refs_4_ = f32[4,128,256]{2,1,0:T(8,128)S(1)} collective-permute-done((f32[4,128,256]{2,1,0:T(8,128)S(1)}, f32[4,128,256]{2,1,0:T(8,128)S(1)}, u32[]{:S(2)}, u32[]{:S(2)}) %collective-permute-start.47) | collective-permute-done | bytes 524320 | tf_op jit(solution)/shard_map/ppermute | solution.py:561
  389.0 12.9 %collective-permute-done.59.refs_2_ = f32[4,288,256]{2,1,0:T(8,128)S(1)} collective-permute-done((f32[4,288,256]{2,1,0:T(8,128)}, f32[4,288,256]{2,1,0:T(8,128)S(1)}, u32[]{:S(2)}, u32[]{:S(2)}) %collective-permute-start.59) | collective-permute-done | bytes 1179680 | tf_op jit(solution)/shard_map/ppermute | solution.py:561
  408.4 9.3 %collective-permute-done.65.refs_2_ = f32[2,288,256]{2,1,0:T(8,128)S(1)} collective-permute-done((f32[2,288,256]{2,1,0:T(8,128)S(1)}, f32[2,288,256]{2,1,0:T(8,128)S(1)}, u32[]{:S(2)}, u32[]{:S(2)}) %collective-permute-start.65) | collective-permute-done | bytes 589856 | tf_op jit(solution)/shard_map/ppermute | solution.py:725
  438.2 10.3 %collective-permute-done.67.refs_2_ = f32[288,256]{1,0:T(8,128)S(1)} collective-permute-done((f32[288,256]{1,0:T(8,128)S(1)}, f32[288,256]{1,0:T(8,128)S(1)}, u32[]{:S(2)}, u32[]{:S(2)}) %collective-permute-start.67) | collective-permute-done | bytes 294944 | tf_op jit(solution)/shard_map/ppermute | solution.py:725
  458.8 15.0 %collective-permute-done.75.refs_2_ = f32[288,256]{1,0:T(8,128)S(1)} collective-permute-done((f32[288,256]{1,0:T(8,128)S(1)}, f32[288,256]{1,0:T(8,128)S(1)}, u32[]{:S(2)}, u32[]{:S(2)}) %collective-permute-start.75) | collective-permute-done | bytes 294944 | tf_op jit(solution)/shard_map/ppermute | solution.py:725
  482.5 16.6 %collective-permute-done.76.refs_2_ = f32[288,256]{1,0:T(8,128)S(1)} collective-permute-done((f32[288,256]{1,0:T(8,128)S(1)}, f32[288,256]{1,0:T(8,128)S(1)}, u32[]{:S(2)}, u32[]{:S(2)}) %collective-permute-start.76) | collective-permute-done | bytes 294944 | tf_op jit(solution)/shard_map/ppermute | solution.py:725
  505.1 10.3 %collective-permute-done.79.refs_3_ = f32[288,256]{1,0:T(8,128)S(1)} collective-permute-done((f32[288,256]{1,0:T(8,128)S(1)}, f32[288,256]{1,0:T(8,128)S(1)}, u32[]{:S(2)}, u32[]{:S(2)}) %collective-permute-start.79) | collective-permute-done | bytes 294944 | tf_op jit(solution)/shard_map/ppermute | solution.py:725
  (317 shorter events, 245.6 us)
Async XLA Ops:
  25.4 28.6 %collective-permute-start.1 = (f32[1152,128]{1,0:T(8,128)S(1)}, f32[1152,128]{1,0:T(8,128)S(1)}, u32[]{:S(2)}, u32[]{:S(2)}) collective-permute-start(f32[1152,128]{1,0:T(8,128)S(1)} %shard_map.184.refs_3_.refs_1_), channel_id=1, source_target_pairs={{0,16},{1,17},{2,18},{3,19},{4,20},{5,21},{6,22},{7,23},{8,24},{9,... | collective-permute-start | bytes 1769480 | tf_op jit(solution)/shard_map/ppermute | solution.py:561
  29.0 26.1 %collective-permute-start.6 = (f32[1152,128]{1,0:T(8,128)S(1)}, f32[1152,128]{1,0:T(8,128)S(1)}, u32[]{:S(2)}, u32[]{:S(2)}) collective-permute-start(f32[1152,128]{1,0:T(8,128)S(1)} %shard_map.185.refs_3_.refs_1_), channel_id=1, source_target_pairs={{0,16},{1,17},{2,18},{3,19},{4,20},{5,21},{6,22},{7,23},{8,24},{9,... | collective-permute-start | bytes 1769480 | tf_op jit(solution)/shard_map/ppermute | solution.py:561
  63.2 33.2 %collective-permute-start.15 = (f32[1152,128]{1,0:T(8,128)S(1)}, f32[1152,128]{1,0:T(8,128)S(1)}, u32[]{:S(2)}, u32[]{:S(2)}) collective-permute-start(f32[1152,128]{1,0:T(8,128)S(1)} %shard_map.186.refs_3_.refs_1_), channel_id=1, source_target_pairs={{0,16},{1,17},{2,18},{3,19},{4,20},{5,21},{6,22},{7,23},{8,24},{9,... | collective-permute-start | bytes 1769480 | tf_op jit(solution)/shard_map/ppermute | solution.py:561
  64.7 32.4 %collective-permute-start.17 = (f32[1152,128]{1,0:T(8,128)S(1)}, f32[1152,128]{1,0:T(8,128)S(1)}, u32[]{:S(2)}, u32[]{:S(2)}) collective-permute-start(f32[1152,128]{1,0:T(8,128)S(1)} %shard_map.187.last.refs_1_), channel_id=1, source_target_pairs={{0,16},{1,17},{2,18},{3,19},{4,20},{5,21},{6,22},{7,23},{8,24},{9,... | collective-permute-start | bytes 1769480 | tf_op jit(solution)/shard_map/ppermute | solution.py:561
  113.8 26.6 %collective-permute-start.19 = (f32[4,128,256]{2,1,0:T(8,128)S(1)}, f32[4,128,256]{2,1,0:T(8,128)S(1)}, u32[]{:S(2)}, u32[]{:S(2)}) collective-permute-start(f32[4,128,256]{2,1,0:T(8,128)S(1)} %shard_map.200.refs_3_.refs_1_), channel_id=1, source_target_pairs={{0,1},{1,0},{2,3},{3,2},{4,5},{5,4},{6,7},{7,6},{8,9},{9,8},{10,11... | collective-permute-start | bytes 1572872 | tf_op jit(solution)/shard_map/ppermute | solution.py:561
  114.9 23.0 %collective-permute-start.20 = (f32[4,128,256]{2,1,0:T(8,128)S(1)}, f32[4,128,256]{2,1,0:T(8,128)S(1)}, u32[]{:S(2)}, u32[]{:S(2)}) collective-permute-start(f32[4,128,256]{2,1,0:T(8,128)S(1)} %get-tuple-element.92), channel_id=1, source_target_pairs={{0,1},{1,0},{2,3},{3,2},{4,5},{5,4},{6,7},{7,6},{8,9},{9,8},{10,11... | collective-permute-start | bytes 1572872 | tf_op jit(solution)/shard_map/ppermute | solution.py:561
  142.0 23.3 %collective-permute-start.21 = (f32[8,128,256]{2,1,0:T(8,128)}, f32[8,128,256]{2,1,0:T(8,128)}, u32[]{:S(2)}, u32[]{:S(2)}) collective-permute-start(f32[8,128,256]{2,1,0:T(8,128)} %shard_map.202.refs_5_.refs_0_), channel_id=1, source_target_pairs={{0,16},{1,17},{2,18},{3,19},{4,20},{5,21},{6,22},{7,23},{8,24},{9,... | collective-permute-start | bytes 3145736 | tf_op jit(solution)/shard_map/ppermute | solution.py:561
  153.1 45.8 %collective-permute-start.22 = (f32[8,128,256]{2,1,0:T(8,128)}, f32[8,128,256]{2,1,0:T(8,128)}, u32[]{:S(2)}, u32[]{:S(2)}) collective-permute-start(f32[8,128,256]{2,1,0:T(8,128)} %shard_map.202.refs_5_.refs_0_), channel_id=1, source_target_pairs={{0,8},{1,9},{2,10},{3,11},{4,12},{5,13},{6,14},{7,15},{8,0},{9,1},... | collective-permute-start | bytes 3145736 | tf_op jit(solution)/shard_map/ppermute | solution.py:561
  165.4 33.6 %collective-permute-start.23 = (f32[8,128,256]{2,1,0:T(8,128)}, f32[8,128,256]{2,1,0:T(8,128)}, u32[]{:S(2)}, u32[]{:S(2)}) collective-permute-start(f32[8,128,256]{2,1,0:T(8,128)} %collective-permute-done.21.refs_1_), channel_id=1, source_target_pairs={{0,8},{1,9},{2,10},{3,11},{4,12},{5,13},{6,14},{7,15},{8,0},{9,1},... | collective-permute-start | bytes 3145736 | tf_op jit(solution)/shard_map/ppermute | solution.py:561
  190.5 20.5 %collective-permute-start.29 = (f32[2,128,256]{2,1,0:T(8,128)S(1)}, f32[2,128,256]{2,1,0:T(8,128)S(1)}, u32[]{:S(2)}, u32[]{:S(2)}) collective-permute-start(f32[2,128,256]{2,1,0:T(8,128)S(1)} %shard_map.204.refs_4_.refs_1_), channel_id=1, source_target_pairs={{0,2},{1,3},{2,4},{3,5},{4,6},{5,7},{6,0},{7,1},{8,10},{9,11},{10,... | collective-permute-start | bytes 786440 | tf_op jit(solution)/shard_map/ppermute | solution.py:561
  213.4 25.1 %collective-permute-start.34 = (f32[8,128,256]{2,1,0:T(8,128)S(1)}, f32[8,128,256]{2,1,0:T(8,128)S(1)}, u32[]{:S(2)}, u32[]{:S(2)}) collective-permute-start(f32[8,128,256]{2,1,0:T(8,128)S(1)} %shard_map.206.refs_3_.refs_0_), channel_id=1, source_target_pairs={{0,1},{1,0},{2,3},{3,2},{4,5},{5,4},{6,7},{7,6},{8,9},{9,8},{10,11... | collective-permute-start | bytes 3145736 | tf_op jit(solution)/shard_map/ppermute | solution.py:561
  215.1 24.8 %collective-permute-start.32 = (f32[2048,128]{1,0:T(8,128)S(1)}, f32[2048,128]{1,0:T(8,128)S(1)}, u32[]{:S(2)}, u32[]{:S(2)}) collective-permute-start(f32[2048,128]{1,0:T(8,128)S(1)} %shard_map.207.refs_1_.refs_3_), channel_id=1, source_target_pairs={{0,16},{1,17},{2,18},{3,19},{4,20},{5,21},{6,22},{7,23},{8,24},{9,... | collective-permute-start | bytes 3145736 | tf_op jit(solution)/shard_map/ppermute | solution.py:561
  216.7 24.0 %collective-permute-start.35 = (f32[8,128,256]{2,1,0:T(8,128)S(1)}, f32[8,128,256]{2,1,0:T(8,128)S(1)}, u32[]{:S(2)}, u32[]{:S(2)}) collective-permute-start(f32[8,128,256]{2,1,0:T(8,128)S(1)} %shard_map.206.refs_3_.refs_0_), channel_id=1, source_target_pairs={{0,8},{1,9},{2,10},{3,11},{4,12},{5,13},{6,14},{7,15},{8,0},{9,1},... | collective-permute-start | bytes 3145736 | tf_op jit(solution)/shard_map/ppermute | solution.py:561
  255.0 25.3 %collective-permute-start.42 = (f32[2048,128]{1,0:T(8,128)S(1)}, f32[2048,128]{1,0:T(8,128)S(1)}, u32[]{:S(2)}, u32[]{:S(2)}) collective-permute-start(f32[2048,128]{1,0:T(8,128)S(1)} %shard_map.211.refs_3_.refs_1_), channel_id=1, source_target_pairs={{0,16},{1,17},{2,18},{3,19},{4,20},{5,21},{6,22},{7,23},{8,24},{9,... | collective-permute-start | bytes 3145736 | tf_op jit(solution)/shard_map/ppermute | solution.py:561
  280.9 22.4 %collective-permute-start.46 = (f32[2048,128]{1,0:T(8,128)S(1)}, f32[2048,128]{1,0:T(8,128)S(1)}, u32[]{:S(2)}, u32[]{:S(2)}) collective-permute-start(f32[2048,128]{1,0:T(8,128)S(1)} %shard_map.213.refs_5_.refs_1_.refs_3_), channel_id=1, source_target_pairs={{0,8},{1,9},{2,10},{3,11},{4,12},{5,13},{6,14},{7,15},{8,0},{9,1},... | collective-permute-start | bytes 3145736 | tf_op jit(solution)/shard_map/ppermute | solution.py:561
  334.6 19.7 %collective-permute-start.50 = (f32[1152,128]{1,0:T(8,128)S(1)}, f32[1152,128]{1,0:T(8,128)S(1)}, u32[]{:S(2)}, u32[]{:S(2)}) collective-permute-start(f32[1152,128]{1,0:T(8,128)S(1)} %shard_map.221.refs_3_.refs_2_), channel_id=1, source_target_pairs={{0,16},{1,17},{2,18},{3,19},{4,20},{5,21},{6,22},{7,23},{8,24},{9,... | collective-permute-start | bytes 1769480 | tf_op jit(solution)/shard_map/ppermute | solution.py:561
  367.4 34.6 %collective-permute-start.59 = (f32[4,288,256]{2,1,0:T(8,128)}, f32[4,288,256]{2,1,0:T(8,128)S(1)}, u32[]{:S(2)}, u32[]{:S(2)}) collective-permute-start(f32[4,288,256]{2,1,0:T(8,128)} %get-tuple-element.118), channel_id=1, source_target_pairs={{0,1},{1,0},{2,3},{3,2},{4,5},{5,4},{6,7},{7,6},{8,9},{9,8},{10,11... | collective-permute-start | bytes 3538952 | tf_op jit(solution)/shard_map/ppermute | solution.py:561
  385.7 20.2 %collective-permute-start.66 = (f32[1152,128]{1,0:T(8,128)S(1)}, f32[1152,128]{1,0:T(8,128)S(1)}, u32[]{:S(2)}, u32[]{:S(2)}) collective-permute-start(f32[1152,128]{1,0:T(8,128)S(1)} %shard_map.231.refs_3_.refs_2_), channel_id=1, source_target_pairs={{0,16},{1,17},{2,18},{3,19},{4,20},{5,21},{6,22},{7,23},{8,24},{9,... | collective-permute-start | bytes 1769480 | tf_op jit(solution)/shard_map/ppermute | solution.py:561
  387.5 39.8 %collective-permute-start.71 = (f32[4,288,256]{2,1,0:T(8,128)}, f32[4,288,256]{2,1,0:T(8,128)S(1)}, u32[]{:S(2)}, u32[]{:S(2)}) collective-permute-start(f32[4,288,256]{2,1,0:T(8,128)} %get-tuple-element.129), channel_id=1, source_target_pairs={{0,1},{1,0},{2,3},{3,2},{4,5},{5,4},{6,7},{7,6},{8,9},{9,8},{10,11... | collective-permute-start | bytes 3538952 | tf_op jit(solution)/shard_map/ppermute | solution.py:561
  421.8 30.7 %collective-permute-start.72 = (f32[4,288,256]{2,1,0:T(8,128)S(1)}, f32[4,288,256]{2,1,0:T(8,128)S(1)}, u32[]{:S(2)}, u32[]{:S(2)}) collective-permute-start(f32[4,288,256]{2,1,0:T(8,128)S(1)} %get-tuple-element.132), channel_id=1, source_target_pairs={{0,1},{1,0},{2,3},{3,2},{4,5},{5,4},{6,7},{7,6},{8,9},{9,8},{10,11... | collective-permute-start | bytes 3538952 | tf_op jit(solution)/shard_map/ppermute | solution.py:561
  427.9 21.4 %collective-permute-start.73 = (f32[2,288,256]{2,1,0:T(8,128)S(1)}, f32[2,288,256]{2,1,0:T(8,128)S(1)}, u32[]{:S(2)}, u32[]{:S(2)}) collective-permute-start(f32[2,288,256]{2,1,0:T(8,128)S(1)} %get-tuple-element.130.refs_5_), channel_id=1, source_target_pairs={{0,2},{1,3},{2,0},{3,1},{4,6},{5,7},{6,4},{7,5},{8,10},{9,11},{10,... | collective-permute-start | bytes 1769480 | tf_op jit(solution)/shard_map/ppermute | solution.py:725
  434.9 41.8 %collective-permute-start.77 = (f32[4,288,256]{2,1,0:T(8,128)S(1)}, f32[4,288,256]{2,1,0:T(8,128)S(1)}, u32[]{:S(2)}, u32[]{:S(2)}) collective-permute-start(f32[4,288,256]{2,1,0:T(8,128)S(1)} %get-tuple-element.140), channel_id=1, source_target_pairs={{0,1},{1,0},{2,3},{3,2},{4,5},{5,4},{6,7},{7,6},{8,9},{9,8},{10,11... | collective-permute-start | bytes 3538952 | tf_op jit(solution)/shard_map/ppermute | solution.py:561
  453.2 21.4 %collective-permute-start.74 = (f32[2,288,256]{2,1,0:T(8,128)S(1)}, f32[2,288,256]{2,1,0:T(8,128)S(1)}, u32[]{:S(2)}, u32[]{:S(2)}) collective-permute-start(f32[2,288,256]{2,1,0:T(8,128)S(1)} %get-tuple-element.136.refs_3_), channel_id=1, source_target_pairs={{0,2},{1,3},{2,0},{3,1},{4,6},{5,7},{6,4},{7,5},{8,10},{9,11},{10,... | collective-permute-start | bytes 1769480 | tf_op jit(solution)/shard_map/ppermute | solution.py:725
  477.4 22.4 %collective-permute-start.78 = (f32[2,288,256]{2,1,0:T(8,128)S(1)}, f32[2,288,256]{2,1,0:T(8,128)S(1)}, u32[]{:S(2)}, u32[]{:S(2)}) collective-permute-start(f32[2,288,256]{2,1,0:T(8,128)S(1)} %get-tuple-element.141.refs_3_), channel_id=1, source_target_pairs={{0,2},{1,3},{2,0},{3,1},{4,6},{5,7},{6,4},{7,5},{8,10},{9,11},{10,... | collective-permute-start | bytes 1769480 | tf_op jit(solution)/shard_map/ppermute | solution.py:725
  (94 other events, 856.4 us)

commit v4 on v3

--- a/solution.py
+++ b/solution.py
@@ -10,6 +10,81 @@
 BLOCK = 128
 AXES = ("row", "col")
 COST = pl.CostEstimate(flops=1, bytes_accessed=1, transcendentals=0)
+
+ORDER = (
+    ("begin", 0),
+    ("begin", 1),
+    ("cross", 0, 0),
+    ("cross", 0, 1),
+    ("cross", 1, 0),
+    ("cross", 1, 1),
+    ("base", 0, 0),
+    ("base", 0, 1),
+    ("end", 0, 0),
+    ("end", 0, 1),
+    ("couple", 0),
+    ("base", 1, 0),
+    ("sum_y", 0),
+    ("base", 1, 1),
+    ("sum_z", 0),
+    ("end", 1, 0),
+    ("end", 1, 1),
+    ("couple", 1),
+    ("sum_y", 1),
+    ("gather_z", 0),
+    ("gather_y", 0),
+    ("sum_z", 1),
+    ("gather_z", 1),
+    ("hold_far", 0),
+    ("root", 0),
+    ("cross_root", 0),
+    ("gather_y", 1),
+    ("end_root", 0),
+    ("pick", 0),
+    ("pick_y", 0),
+    ("hold_far", 1),
+    ("root", 1),
+    ("pick_z", 0),
+    ("cross_root", 1),
+    ("pick_g", 0),
+    ("end_root", 1),
+    ("pick", 1),
+    ("correct", 0, 0),
+    ("correct", 0, 1),
+    ("correct_x", 0, 0),
+    ("correct_x", 0, 1),
+    ("pick_y", 1),
+    ("pick_z", 1),
+    ("reduce", 0, 0),
+    ("final", 0, 0),
+    ("whole",),
+    ("pick_g", 1),
+    ("final_y", 0, 0),
+    ("reduce", 0, 1),
+    ("final", 0, 1),
+    ("correct", 1, 0),
+    ("correct", 1, 1),
+    ("correct_x", 1, 0),
+    ("correct_x", 1, 1),
+    ("final_z", 0, 0),
+    ("reduce", 1, 0),
+    ("final", 1, 0),
+    ("final_y", 0, 1),
+    ("reduce", 1, 1),
+    ("final", 1, 1),
+    ("final_last", 0, 0),
+    ("final_z", 0, 1),
+    ("final_y", 1, 0),
+    ("final_last", 0, 1),
+    ("final_y", 1, 2),
+    ("final_y", 1, 3),
+    ("final_z", 1, 0),
+    ("final_z", 1, 2),
+    ("final_last", 1, 0),
+    ("final_z", 1, 3),
+    ("finish", 0),
+    ("finish", 1),
+)
 
 
 def product(matrix, vector):
@@ -256,6 +331,18 @@
         self.last = results[0]
         return results
 
+    def hold(self, array):
+        result = pl.pallas_call(
+            lambda held, last, out: None,
+            in_specs=[pl.BlockSpec(memory_space=pl.ANY)] * 2,
+            out_specs=pl.BlockSpec(memory_space=pl.ANY),
+            out_shape=shape(*array.shape),
+            input_output_aliases={0: 0},
+            cost_estimate=COST,
+        )(array, self.last)
+        self.last = result
+        return result
+
     def merge(self, inputs, signs=None):
         signs = signs or (1,) * len(inputs)
 
@@ -335,7 +422,7 @@
         span = slice(start, start + rows)
         held = jnp.concatenate([own[span], other[span]], axis=1)
         value = dot(split(weight[...]), split(held))
-        place = lax.rem(child + count - z, count)
+        place = child
 
         @pl.when(y == 0)
         def _():
@@ -384,16 +471,16 @@
 
 
 def root_kernel(list_ref, left, right, upper, lower, *refs):
-    sources, (own, other, moved) = refs[:-4], refs[-3:]
+    sources, (own, other_up, other_low, moved) = refs[:-5], refs[-4:]
     step = pl.program_id(0)
     width = own.shape[1]
     rows = own.shape[0]
 
     @pl.when(step == 0)
     def _():
-        for start, ref in ((0, upper), (rows // 2, lower)):
+        for start, ref, other in ((0, upper, other_up), (rows // 2, lower, other_low)):
             own[start : start + rows // 2] = ref[:, :width]
-            other[start : start + rows // 2] = ref[:, width:]
+            other[...] = ref[:, width:]
 
     @pl.when(2 * step < list_ref[3, 0])
     def _():
@@ -423,7 +510,9 @@
             weight = split(jnp.concatenate([left[span], right[span]], axis=1))
             value = dot(weight, held)
             own[span] -= value[:, :width]
-            other[span] -= value[:, width:]
+            other = other_up if start < rows // 2 else other_low
+            there = start % (rows // 2)
+            other[there : there + tile] -= value[:, width:]
 
 
 def root(sequence, listed, weight, starts, sources):
@@ -441,10 +530,10 @@
             ]
             + [whole] * (2 + len(sources))
             + [pl.BlockSpec(memory_space=pl.ANY)],
-            out_specs=[whole] * 2,
+            out_specs=[whole] * 3,
             scratch_shapes=[pltpu.VMEM((2 * BLOCK, 2 * width), jnp.float32)],
         ),
-        out_shape=[shape(rows, width)] * 2,
+        out_shape=[shape(rows, width)] + [shape(rows // 2, width)] * 2,
         cost_estimate=COST,
         compiler_params=pltpu.CompilerParams(vmem_limit_bytes=40 * 2**20),
     )(listed, weight, weight, *starts, *sources, sequence.last)
@@ -459,7 +548,7 @@
     children = keep.shape[0]
     for out, block in ((send, 1 - y), (keep, y)):
         for child in range(children):
-            place = lax.rem(child + children - z, children)
+            place = child
             source = me[3 + 2 * child + block]
             inside = jnp.logical_and(source >= 0, source < count)
 
@@ -481,21 +570,21 @@
     start = 0
     for child, weight in zip(pair, (first, second)):
         rows = weight.shape[1]
-        place = lax.rem(z + children - child, children)
-        rows_ref[pl.ds(pl.multiple_of(y * BLOCK, BLOCK), BLOCK)] = near[place]
-        rows_ref[pl.ds(pl.multiple_of((1 - y) * BLOCK, BLOCK), BLOCK)] = far[place]
+        rows_ref[pl.ds(pl.multiple_of(y * BLOCK, BLOCK), BLOCK)] = near[child]
+        rows_ref[pl.ds(pl.multiple_of((1 - y) * BLOCK, BLOCK), BLOCK)] = far[child]
         value = dot(split(weight[...]), split(rows_ref[...]), True)
         own[start : start + rows] = value[:, :width]
         other[start : start + rows] = value[:, width:]
         start += rows
 
 
-def final_kernel(me, first, second, own, other, keep, send, whole):
+def final_kernel(me, first, second, own, other, *refs):
+    outs, whole = refs[:-1], refs[-1]
     y, z = me[1], me[2]
-    count = keep.shape[0]
+    count = outs[0].shape[0]
     width = own.shape[1]
     start, place = 0, 0
-    for weight in (first, second):
+    for weight, (keep, send) in ((first, outs[:2]), (second, outs[-2:])):
         rows, columns = weight.shape
         size = columns // (2 * count)
         span = slice(start, start + rows)
@@ -508,7 +597,13 @@
                 taken = pl.ds(pl.multiple_of((2 * owner + side) * size, 8), size)
                 out[jnp.bitwise_xor(owner, z), place : place + size] = whole[taken]
         start += rows
-        place += size
+        place += size if len(outs) == 2 else 0
+
+
+def join_add_kernel(me, base_ref, upper, lower, out):
+    rows = upper.shape[0]
+    out[:rows] = base_ref[:rows] + upper[...]
+    out[rows:] = base_ref[rows:] + lower[...]
 
 
 def halve_kernel(me, keep, arrived, send, held):
@@ -518,18 +613,19 @@
 
 
 def finish_kernel(terms, me, *refs):
+    held = iter(refs[:-2])
+    outs = refs[-2:]
+    rows = outs[0].shape[0]
     parts = len(terms)
-    held = iter(refs[:-2])
-    first, second = refs[-2:]
-    rows = first.shape[0]
-    width = first.shape[1] // (2 * parts)
-    for part in range(parts):
-        value = total([next(held)[...] for _ in range(terms[part])], (1,) * terms[part])
-        for half in range(2):
-            there = slice((half * parts + part) * width, (half * parts + part + 1) * width)
-            here = slice(half * width, (half + 1) * width)
-            first[:, there] = value[:rows, here]
-            second[:, there] = value[rows:, here]
+    width = outs[0].shape[1] // (2 * parts)
+    for part, counts in enumerate(terms):
+        values = [total([next(held)[...] for _ in range(count)], (1,) * count) for count in counts]
+        if len(values) == 1:
+            values = [values[0][:rows], values[0][rows:]]
+        for out, value in zip(outs, values):
+            for half in range(2):
+                start = (half * parts + part) * width
+                out[:, start : start + width] = value[:, half * width : (half + 1) * width]
 
 
 def whole_kernel(me, *refs):
@@ -560,12 +656,6 @@
     def send(array, group, step=1):
         return lax.ppermute(array, AXES, group.pairs[step - 1])
 
-    def spread(array, group):
-        return [send(array, group, step) for step in range(1, group.size)]
-
-    def deal(arrays, group):
-        return [send(arrays[step], group, step) for step in range(1, group.size)]
-
     mine = lax.dynamic_slice_in_dim(target_blocks, row * per_row, per_row, 1)
     wanted = (mine - lax.axis_index("col") * held).reshape(-1)
     me = jnp.concatenate([jnp.stack([core.place, y.place, z.place]).astype(jnp.int32), wanted])
@@ -576,32 +666,23 @@
     away_x = jnp.where(from_row // 2 == x.place, 0, 1)
     away_core = jnp.where(from_row % 2 == core.place, 0, 1)
     away_y = jnp.where(block % per_row == y.place, 0, 1)
-    place = (z.place + z.size - child) % z.size
     local_block = target_blocks - row * owned
     inside = ((local_block >= 0) & (local_block < owned)).reshape(-1)
     rank = jnp.cumsum(inside.astype(jnp.int32)) - 1
     entries = jnp.arange(inside.shape[0], dtype=jnp.int32)
     chosen = inside[None, :] & (rank[None, :] == entries[:, None])
-    tables = (
-        (local_block, away_core * 2 + away_x + 1, away_y * z.size + place),
-        (local_block, away_core * 2 + away_y + 1, place * x.size + away_x),
+    table = (local_block, away_core * 2 + away_x + 1, away_y * children + child)
+    held_rows = jnp.sum(jnp.where(chosen[None], jnp.stack(table).reshape(3, 1, -1), 0), axis=2)
+    found = jnp.sum(inside.astype(jnp.int32))
+    last = jnp.sum(jnp.where(entries == found - 1, held_rows[0], 0))
+    listed = jnp.stack(
+        [
+            jnp.where(entries < found, held_rows[0], last),
+            held_rows[1] - 1,
+            held_rows[2],
+            jnp.zeros_like(entries) + found,
+        ]
     )
-    found = jnp.sum(inside.astype(jnp.int32))
-    listed = []
-    for table in tables:
-        rows_of = jnp.stack(table).reshape(3, -1)
-        held_rows = jnp.sum(jnp.where(chosen[None], rows_of[:, None, :], 0), axis=2)
-        last = jnp.sum(jnp.where(entries == found - 1, held_rows[0], 0))
-        listed.append(
-            jnp.stack(
-                [
-                    jnp.where(entries < found, held_rows[0], last),
-                    held_rows[1] - 1,
-                    held_rows[2],
-                    jnp.zeros_like(entries) + found,
-                ]
-            )
-        )
 
     run = Sequence(me)
     parts = range(2)
@@ -640,42 +721,38 @@
         keep, sent = run(kernel, list(couplings) + flat, [piece] * 2, limit=40)
         state[part]["keep"], state[part]["arrived"] = keep, send(sent, y)
 
+    def exchange(array, mask):
+        flip = mask * y.size
+        listed = [(r * cols + c, r * cols + (c ^ flip)) for r in range(rows) for c in range(cols)]
+        return lax.ppermute(array, AXES, listed)
+
     def sum_y(part):
-        split_up = run.merge_split([state[part]["keep"], state[part]["arrived"]])
-        state[part]["terms"] = [split_up[0]] + deal(split_up, z)
+        value = run.merge([state[part]["keep"], state[part]["arrived"]])
+        state[part]["terms"] = [value, exchange(value, 1)]
 
     def sum_z(part):
         value = run.merge(state[part]["terms"])
-        state[part]["pieces"] = [value] + spread(value, z)
+        state[part]["terms"] = [value, exchange(value, 2)]
 
     def gather_z(part):
-        near = run.stack(state[part]["pieces"])
+        near = run.merge(state[part]["terms"])
         state[part]["near"], state[part]["far"] = near, send(near, y)
 
     def gather_y(part):
         near = run.join([state[part]["near"], state[part]["far"]])
-        far = send(near, x)
-        state[part]["blocks"] = [near, far, send(near, core), send(far, core)]
-
-    def gather_x(part):
-        value = run.merge(state[part]["terms"])
-        state[part]["pieces"] = [value, send(value, x)]
-
-    def spread_z(part):
-        both = run.stack(state[part]["pieces"])
-        state[part]["pieces"] = [both] + spread(both, z)
-
-    def join_z(part):
-        near = run.join(state[part]["pieces"])
-        far = send(near, y)
-        state[part]["blocks"] = [near, far, send(near, core), send(far, core)]
+        state[part]["blocks"] = [near, send(near, x), send(near, core)]
+
+    def hold_far(part):
+        near, far, near_there = state[part]["blocks"]
+        far = run.hold(far)
+        state[part]["blocks"] = [near, far, near_there, send(far, core)]
 
     def solve_root(part):
-        own, other = root(run, listed[part], inverse_root, state[part]["base"], state[part]["blocks"])
-        state[part]["root"] = own, send(other, core)
+        own, upper, lower = root(run, listed, inverse_root, [state[part]["base"][0], state[part]["base"][1]], state[part]["blocks"])
+        state[part]["root"] = own, send(upper, core), send(lower, core)
 
     def cross_root(part):
-        own = run.merge(list(state[part]["root"]))
+        own = run(join_add_kernel, list(state[part]["root"]), [shape(*state[part]["root"][0].shape)])[0]
         state[part]["root"] = own, send(own, x)
 
     def end_root(part):
@@ -707,22 +784,23 @@
         own = run.merge([first] + list(state[part][group]), (1, -1, -1))
         state[part][group] = own, send(own, core)
 
+    def split_of(part, group):
+        return (2, 3) if (part, group) == (1, 1) else (group,)
+
     def final(part, group):
         weights = [inverses[k] for k in pairs[group]]
-        size = sum(weight.shape[1] for weight in weights) // cols
-        keep, sent = run(
+        sizes = [weight.shape[1] // cols for weight in weights]
+        keys = split_of(part, group)
+        sizes = sizes if len(keys) == 2 else [sum(sizes)]
+        outs = run(
             final_kernel,
             weights + list(state[part][group]),
-            [shape(z.size, size, 2 * width)] * 2,
+            [shape(z.size, size, 2 * width) for size in sizes for _ in range(2)],
             [pltpu.VMEM((max(weight.shape[1] for weight in weights), 2 * width), jnp.float32)],
             limit=40,
         )
-        state[part][group] = keep, send(sent, y)
-
-    def exchange(array, mask):
-        flip = mask * y.size
-        listed = [(r * cols + c, r * cols + (c ^ flip)) for r in range(rows) for c in range(cols)]
-        return lax.ppermute(array, AXES, listed)
+        for key, keep, sent in zip(keys, outs[::2], outs[1::2]):
+            state[part][key] = keep, send(sent, y)
 
     def final_y(part, group):
         keep, arrived = state[part][group]
@@ -737,8 +815,9 @@
     def finish(group):
         sizes = [inverses[k].shape[1] // cols for k in pairs[group]]
         outs = [shape(size, 4 * width) for size in sizes]
-        terms = [len(state[part][group]) for part in parts]
-        inputs = [a for part in parts for a in state[part][group]]
+        pieces = [[state[part][key] for key in split_of(part, group)] for part in parts]
+        terms = [[len(piece) for piece in held] for held in pieces]
+        inputs = [a for held in pieces for piece in held for a in piece]
         return run(functools.partial(finish_kernel, terms), inputs, outs)
 
     def final_last(part, group):
@@ -746,87 +825,78 @@
 
     def by_child(part):
         arrays = [None] * children
-        for (a, b), (own, other) in zip(pairs, forward[part]):
+        for group, (a, b) in enumerate(pairs):
+            own, other = forward[part][group]
             arrays[a] = own, other, 0
             arrays[b] = own, other, couplings[a].shape[1]
         return arrays
 
+    forward = [[None, None] for _ in parts]
+
+    def begin(group, chosen=(0, 1)):
+        for part, piece in zip(chosen, forward_start(pairs[group], chosen)):
+            forward[part][group] = piece
+
+    def begin_part(part, group):
+        begin(group, (part,))
+
+    def cross(part, group):
+        forward[part][group] = forward_cross(*forward[part][group])
+
+    def end(part, group):
+        forward[part][group] = forward_end(*forward[part][group])
+
+    def couple_all(part):
+        couple(part, by_child(part))
+
     def start_root(part, piece):
         held = base(run, part, piece, width, inverse_root, loads_root)
-        state[part].setdefault("base", []).append(held)
-
-    def forward_begin(chosen):
-        begun = [forward_start(pair, chosen) for pair in pairs]
-        return [[forward_cross(*pieces[k]) for pieces in begun] for k in range(len(chosen))]
-
-    crossed = forward_begin((0, 1))
-    start_root(0, 0)
-    start_root(0, 1)
-    forward = [None, None]
-    forward[0] = [forward_end(*piece) for piece in crossed[0]]
-    couple(0, by_child(0))
-    start_root(1, 0)
-    sum_y(0)
-    start_root(1, 1)
-    sum_z(0)
-    forward[1] = [forward_end(*piece) for piece in crossed[1]]
-    couple(1, by_child(1))
-    gather_z(0)
-    sum_y(1)
-    gather_y(0)
-    gather_x(1)
-    spread_z(1)
-    solve_root(0)
-    join_z(1)
-    cross_root(0)
-    end_root(0)
-    solve_root(1)
-    pick_root(0)
-    cross_root(1)
-    sum_y(0)
-    end_root(1)
-    sum_z(0)
-    pick_root(1)
-    gather_z(0)
-    sum_y(1)
-    (solved_root,) = run(
-        whole_kernel,
-        [a for part in parts for a in state[part]["root"]],
-        [shape(inverse_root.shape[0], 4 * width)],
+        state[part].setdefault("base", {})[piece] = held
+
+    solved = [None] * 4
+
+    def finish_pair(group):
+        a, b = pairs[group]
+        solved[a], solved[b] = finish(group)
+
+    whole_root = []
+
+    def whole():
+        held = [a for part in parts for a in state[part]["root"]]
+        whole_root.extend(run(whole_kernel, held, [shape(inverse_root.shape[0], 4 * width)]))
+
+    named = dict(
+        begin=begin,
+        begin_part=begin_part,
+        cross=cross,
+        end=end,
+        base=start_root,
+        couple=couple_all,
+        sum_y=sum_y,
+        sum_z=sum_z,
+        gather_z=gather_z,
+        gather_y=gather_y,
+        hold_far=hold_far,
+        root=solve_root,
+        cross_root=cross_root,
+        end_root=end_root,
+        pick=pick_root,
+        pick_y=sum_y,
+        pick_z=sum_z,
+        pick_g=gather_z,
+        whole=whole,
+        correct=correct,
+        correct_x=correct_cross,
+        reduce=reduce,
+        final=final,
+        final_y=final_y,
+        final_z=final_z,
+        final_last=final_last,
+        finish=finish_pair,
     )
-    correct(0, 0)
-    correct(0, 1)
-    correct_cross(0, 0)
-    correct_cross(0, 1)
-    sum_z(1)
-    reduce(0, 0)
-    gather_z(1)
-    final(0, 0)
-    reduce(0, 1)
-    correct(1, 0)
-    correct(1, 1)
-    final(0, 1)
-    correct_cross(1, 0)
-    correct_cross(1, 1)
-    final_y(0, 0)
-    reduce(1, 0)
-    final_z(0, 0)
-    final(1, 0)
-    reduce(1, 1)
-    final_y(0, 1)
-    final(1, 1)
-    final_last(0, 0)
-    final_z(0, 1)
-    final_y(1, 0)
-    final_last(0, 1)
-    final_z(1, 0)
-    final_y(1, 1)
-    final_last(1, 0)
-    final_z(1, 1)
-    solved = [None] * 4
-    for group, (a, b) in enumerate(pairs):
-        solved[a], solved[b] = finish(group)
-    return tuple(solved) + (solved_root,)
+    for name, *which in ORDER:
+        named[name](*which)
+    return tuple(solved) + (whole_root[0],)
 
 
 def local(rows, cols, *arguments):

time: 525 us -> 517 us (0.985)
  waiting for transfers between devices: 226 us -> 280 us
  starting transfers between devices: 103 us -> 52.4 us
  other arithmetic: 14.7 us -> 4.33 us
    ppermute x8 -> x18, waiting for transfers between devices: 62 us -> 160 us  [exchange(): return lax.ppermute(array, AXES, listed)]
    ppermute x72 -> x51, starting transfers between devices: 80 us -> 32.7 us  [send(): return lax.ppermute(array, AXES, group.pairs[step - 1])]
    ppermute x72 -> x51, waiting for transfers between devices: 164 us -> 120 us  [send(): return lax.ppermute(array, AXES, group.pairs[step - 1])]
    unnamed x78 -> x79, local copies, waits for them, and re-layouts: 11.7 us -> 16 us
    ppermute x8 -> x18, starting transfers between devices: 22.9 us -> 19.7 us  [exchange(): return lax.ppermute(array, AXES, listed)]
    pallas_call x62 -> x64, Pallas kernels: 87.7 us -> 86.4 us  [__call__(): pl.pallas_call(lambda *refs: kernel(*refs[:count + 1], *refs[count + 2:])...]
  transfers between devices with their start and end apart: 80 -> 69, of which waited for: 39 -> 42; matrix products, arithmetic and copies ran while one was open for 4% -> 1% of each run, Pallas kernels for 26% -> 22%
where the time goes in v4:
time: 517 us; the launch traced here: 508 us
  waiting for transfers between devices  280 us (54%)
  Pallas kernels  152 us (29%)
  starting transfers between devices  52.4 us (10%)
  local copies, waits for them, and re-layouts  17.3 us (3%)
    ppermute x18, waiting for transfers between devices, exchange(): return lax.ppermute(array, AXES, listed)  160 us
    ppermute x51, waiting for transfers between devices, send(): return lax.ppermute(array, AXES, group.pairs[step - 1])  120 us
    pallas_call x64, Pallas kernels, __call__(): pl.pallas_call(lambda *refs: kernel(*refs[:count + 1], *refs[count + 2:])...  86.4 us
    pallas_call x4, Pallas kernels, base(): pl.pallas_call(base_kernel, grid_spec=pltpu.PrefetchScalarGridSpec(num_sc...  45.3 us
    ppermute x51, starting transfers between devices, send(): return lax.ppermute(array, AXES, group.pairs[step - 1])  32.7 us
    pallas_call x2, Pallas kernels, root(): pl.pallas_call(root_kernel, grid_spec=pltpu.PrefetchScalarGridSpec(num_sc...  20 us
    ppermute x18, starting transfers between devices, exchange(): return lax.ppermute(array, AXES, listed)  19.7 us
    unnamed x79, local copies, waits for them, and re-layouts  16 us
  transfers between devices with their start and end apart: 69, of which 42 were waited for; matrix products, arithmetic and copies ran while one was open for 1% of the time, Pallas kernels for 22%

profile of v4, /device:TPU:0, one launch (start us, length us, event | category | flops | bytes accessed | tf_op | source)
XLA Modules:
  0.0 508.4 jit_solution(14588205414468701512)
XLA Ops:
  2.1 10.5 %shard_map.182 = (f32[1152,128]{1,0:T(8,128)}, f32[1152,128]{1,0:T(8,128)}, f32[1152,128]{1,0:T(8,128)}, f32[1152,128]{1,0:T(8,128)}) custom-call(s32[11]{0:T(128)} %pad_add_fusion.2.refs_0_.refs_5_.me, f32[768,1536]{1,0:T(8,128)} %refs_1_.22, f32[384,768]{1,0:T(8,128)} %refs_2_.22, f32[1536,512]{1,0:T(8,128)} %refs_3_.4, f32[768,512]{1,0:T(8,128)} %refs_4_.4, ...), custom_call_target="tpu_custom_call" | custom-call | flops 1 | bytes 1 | tf_op jit(solution)/shard_map/pallas_call | solution.py:320
  13.0 10.1 %shard_map.183 = (f32[1152,128]{1,0:T(8,128)}, f32[1152,128]{1,0:T(8,128)}, f32[1152,128]{1,0:T(8,128)}, f32[1152,128]{1,0:T(8,128)}) custom-call(s32[11]{0:T(128)} %pad_add_fusion.2.refs_0_.refs_5_.me, f32[640,1280]{1,0:T(8,128)} %refs_1_.23, f32[512,1024]{1,0:T(8,128)} %refs_2_.23, f32[1280,512]{1,0:T(8,128)} %refs_3_.5, f32[1024,512]{1,0:T(8,128)} %refs_4_.5, ...), custom_call_target="tpu_custom_call" | custom-call | flops 1 | bytes 1 | tf_op jit(solution)/shard_map/pallas_call | solution.py:320
  31.4 11.4 %shard_map.188.last.upper = f32[1024,256]{1,0:T(8,128)S(1)} custom-call(s32[11]{0:T(128)S(1)} %copy-done.29, f32[2048,4096]{1,0:T(8,128)} %right.3, f32[4096,512]{1,0:T(8,128)S(1)} %copy-done, f32[4096,512]{1,0:T(8,128)S(1)} %copy-done, f32[1152,128]{1,0:T(8,128)S(1)} %shard_map.187.last.refs_1_), custom_call_target="tpu_custom_call" | custom-call | flops 1 | bytes 1 | tf_op jit(solution)/shard_map/pallas_call | solution.py:451
  42.8 11.2 %shard_map.189.refs_3_.lower = f32[1024,256]{1,0:T(8,128)S(1)} custom-call(s32[11]{0:T(128)S(1)} %copy-done.29, f32[2048,4096]{1,0:T(8,128)} %right.3, f32[4096,512]{1,0:T(8,128)S(1)} %copy-done, f32[4096,512]{1,0:T(8,128)S(1)} %copy-done, f32[1024,256]{1,0:T(8,128)S(1)} %shard_map.188.last.upper), custom_call_target="tpu_custom_call" | custom-call | flops 1 | bytes 1 | tf_op jit(solution)/shard_map/pallas_call | solution.py:451
  65.9 11.6 %shard_map.193.refs_3_.upper = f32[1024,256]{1,0:T(8,128)S(1)} custom-call(s32[11]{0:T(128)S(1)} %copy-done.29, f32[2048,4096]{1,0:T(8,128)} %right.3, f32[4096,512]{1,0:T(8,128)S(1)} %copy-done, f32[4096,512]{1,0:T(8,128)S(1)} %copy-done, f32[4,128,256]{2,1,0:T(8,128)S(1)} %get-tuple-element.77.last.refs_1_), custom_call_target="tpu_custom_call" | custom-call | flops 1 | bytes 1 | tf_op jit(solution)/shard_map/pallas_call | solution.py:451
  80.7 11.2 %shard_map.195.refs_3_.lower = f32[1024,256]{1,0:T(8,128)S(1)} custom-call(s32[11]{0:T(128)S(1)} %copy-done.29, f32[2048,4096]{1,0:T(8,128)} %right.3, f32[4096,512]{1,0:T(8,128)S(1)} %copy-done, f32[4096,512]{1,0:T(8,128)S(1)} %copy-done, f32[4,128,256]{2,1,0:T(8,128)S(1)} %shard_map.194.last.refs_1_), custom_call_target="tpu_custom_call" | custom-call | flops 1 | bytes 1 | tf_op jit(solution)/shard_map/pallas_call | solution.py:451
  103.3 10.9 %collective-permute-done.15.refs_2_ = f32[4,128,256]{2,1,0:T(8,128)S(1)} collective-permute-done((f32[4,128,256]{2,1,0:T(8,128)S(1)}, f32[4,128,256]{2,1,0:T(8,128)S(1)}, u32[]{:S(2)}, u32[]{:S(2)}) %collective-permute-start.15) | collective-permute-done | bytes 524320 | tf_op jit(solution)/shard_map/ppermute | solution.py:657
  114.8 11.8 %collective-permute-done.10.refs_2_ = f32[4,128,256]{2,1,0:T(8,128)S(1)} collective-permute-done((f32[4,128,256]{2,1,0:T(8,128)S(1)}, f32[4,128,256]{2,1,0:T(8,128)S(1)}, u32[]{:S(2)}, u32[]{:S(2)}) %collective-permute-start.10) | collective-permute-done | bytes 524320 | tf_op jit(solution)/shard_map/ppermute | solution.py:727
  129.4 10.6 %collective-permute-done.16.refs_2_ = f32[4,128,256]{2,1,0:T(8,128)S(1)} collective-permute-done((f32[4,128,256]{2,1,0:T(8,128)S(1)}, f32[4,128,256]{2,1,0:T(8,128)S(1)}, u32[]{:S(2)}, u32[]{:S(2)}) %collective-permute-start.16) | collective-permute-done | bytes 524320 | tf_op jit(solution)/shard_map/ppermute | solution.py:657
  146.4 22.3 %collective-permute-done.19.refs_2_ = f32[4,128,256]{2,1,0:T(8,128)} collective-permute-done((f32[4,128,256]{2,1,0:T(8,128)}, f32[4,128,256]{2,1,0:T(8,128)}, u32[]{:S(2)}, u32[]{:S(2)}) %collective-permute-start.19) | collective-permute-done | bytes 524320 | tf_op jit(solution)/shard_map/ppermute | solution.py:727
  180.0 9.8 %shard_map.206 = (f32[2048,128]{1,0:T(8,128)S(1)}, f32[1024,128]{1,0:T(8,128)S(1)}, f32[1024,128]{1,0:T(8,128)S(1)}) custom-call(s32[4,32]{1,0:T(4,128)S(1)} %pad_add_fusion.list_ref, f32[2048,4096]{1,0:T(8,128)} %right.3, f32[2048,4096]{1,0:T(8,128)} %right.3, f32[1024,256]{1,0:T(8,128)S(1)} %copy-done.14, f32[1024,256]{1,0:T(8,128)S(1)} %copy-done.12, ...), custom_call_target="tpu_custom_call" | custom-call | flops 1 | bytes 1 | tf_op jit(solution)/shard_map/pallas_call | solution.py:522
  195.1 12.8 %collective-permute-done.25.refs_2_ = f32[4,128,256]{2,1,0:T(8,128)S(1)} collective-permute-done((f32[4,128,256]{2,1,0:T(8,128)S(1)}, f32[4,128,256]{2,1,0:T(8,128)S(1)}, u32[]{:S(2)}, u32[]{:S(2)}) %collective-permute-start.25) | collective-permute-done | bytes 524320 | tf_op jit(solution)/shard_map/ppermute | solution.py:657
  209.5 9.3 %collective-permute-done.24.refs_2_ = f32[2048,128]{1,0:T(8,128)S(1)} collective-permute-done((f32[2048,128]{1,0:T(8,128)S(1)}, f32[2048,128]{1,0:T(8,128)S(1)}, u32[]{:S(2)}, u32[]{:S(2)}) %collective-permute-start.24) | collective-permute-done | bytes 1048608 | tf_op jit(solution)/shard_map/ppermute | solution.py:657
  224.6 12.6 %collective-permute-done.27.refs_2_ = f32[4,128,256]{2,1,0:T(8,128)S(1)} collective-permute-done((f32[4,128,256]{2,1,0:T(8,128)S(1)}, f32[4,128,256]{2,1,0:T(8,128)S(1)}, u32[]{:S(2)}, u32[]{:S(2)}) %collective-permute-start.27) | collective-permute-done | bytes 524320 | tf_op jit(solution)/shard_map/ppermute | solution.py:657
  250.8 10.2 %shard_map.213 = (f32[2048,128]{1,0:T(8,128)S(1)}, f32[1024,128]{1,0:T(8,128)S(1)}, f32[1024,128]{1,0:T(8,128)S(1)}) custom-call(s32[4,32]{1,0:T(4,128)S(1)} %pad_add_fusion.list_ref, f32[2048,4096]{1,0:T(8,128)} %right.3, f32[2048,4096]{1,0:T(8,128)} %right.3, f32[1024,256]{1,0:T(8,128)S(1)} %copy-done.16, f32[1024,256]{1,0:T(8,128)S(1)} %copy-done.18, ...), custom_call_target="tpu_custom_call" | custom-call | flops 1 | bytes 1 | tf_op jit(solution)/shard_map/pallas_call | solution.py:522
  265.8 24.9 %collective-permute-done.32.refs_2_ = f32[4,128,256]{2,1,0:T(8,128)S(1)} collective-permute-done((f32[4,128,256]{2,1,0:T(8,128)S(1)}, f32[4,128,256]{2,1,0:T(8,128)S(1)}, u32[]{:S(2)}, u32[]{:S(2)}) %collective-permute-start.32) | collective-permute-done | bytes 524320 | tf_op jit(solution)/shard_map/ppermute | solution.py:727
  295.6 10.8 %collective-permute-done.35.refs_4_ = f32[4,128,256]{2,1,0:T(8,128)S(1)} collective-permute-done((f32[4,128,256]{2,1,0:T(8,128)S(1)}, f32[4,128,256]{2,1,0:T(8,128)S(1)}, u32[]{:S(2)}, u32[]{:S(2)}) %collective-permute-start.35) | collective-permute-done | bytes 524320 | tf_op jit(solution)/shard_map/ppermute | solution.py:657
  313.8 9.6 %collective-permute-done.40.refs_2_ = f32[4,128,256]{2,1,0:T(8,128)S(1)} collective-permute-done((f32[4,128,256]{2,1,0:T(8,128)S(1)}, f32[4,128,256]{2,1,0:T(8,128)S(1)}, u32[]{:S(2)}, u32[]{:S(2)}) %collective-permute-start.40) | collective-permute-done | bytes 524320 | tf_op jit(solution)/shard_map/ppermute | solution.py:657
  324.1 13.1 %collective-permute-done.42.refs_2_ = f32[4,128,256]{2,1,0:T(8,128)S(1)} collective-permute-done((f32[4,128,256]{2,1,0:T(8,128)S(1)}, f32[4,128,256]{2,1,0:T(8,128)S(1)}, u32[]{:S(2)}, u32[]{:S(2)}) %collective-permute-start.42) | collective-permute-done | bytes 524320 | tf_op jit(solution)/shard_map/ppermute | solution.py:727
  350.4 21.9 %collective-permute-done.45.refs_2_ = f32[4,128,256]{2,1,0:T(8,128)S(1)} collective-permute-done((f32[4,128,256]{2,1,0:T(8,128)S(1)}, f32[4,128,256]{2,1,0:T(8,128)S(1)}, u32[]{:S(2)}, u32[]{:S(2)}) %collective-permute-start.45) | collective-permute-done | bytes 524320 | tf_op jit(solution)/shard_map/ppermute | solution.py:727
  396.5 12.8 %collective-permute-done.46.refs_2_ = f32[2,288,256]{2,1,0:T(8,128)S(1)} collective-permute-done((f32[2,288,256]{2,1,0:T(8,128)S(1)}, f32[2,288,256]{2,1,0:T(8,128)S(1)}, u32[]{:S(2)}, u32[]{:S(2)}) %collective-permute-start.46) | collective-permute-done | bytes 589856 | tf_op jit(solution)/shard_map/ppermute | solution.py:727
  434.4 14.1 %collective-permute-done.52.refs_2_ = f32[288,256]{1,0:T(8,128)S(1)} collective-permute-done((f32[288,256]{1,0:T(8,128)S(1)}, f32[288,256]{1,0:T(8,128)S(1)}, u32[]{:S(2)}, u32[]{:S(2)}) %collective-permute-start.52) | collective-permute-done | bytes 294944 | tf_op jit(solution)/shard_map/ppermute | solution.py:727
  454.6 17.1 %collective-permute-done.63.refs_2_ = f32[288,256]{1,0:T(8,128)S(1)} collective-permute-done((f32[288,256]{1,0:T(8,128)S(1)}, f32[288,256]{1,0:T(8,128)S(1)}, u32[]{:S(2)}, u32[]{:S(2)}) %collective-permute-start.63) | collective-permute-done | bytes 294944 | tf_op jit(solution)/shard_map/ppermute | solution.py:727
  479.7 11.1 %collective-permute-done.65.refs_2_ = f32[2,160,256]{2,1,0:T(8,128)S(1)} collective-permute-done((f32[2,160,256]{2,1,0:T(8,128)S(1)}, f32[2,160,256]{2,1,0:T(8,128)S(1)}, u32[]{:S(2)}, u32[]{:S(2)}) %collective-permute-start.65) | collective-permute-done | bytes 327712 | tf_op jit(solution)/shard_map/ppermute | solution.py:727
  (295 shorter events, 194.2 us)
Async XLA Ops:
  25.5 28.6 %collective-permute-start.1 = (f32[1152,128]{1,0:T(8,128)S(1)}, f32[1152,128]{1,0:T(8,128)S(1)}, u32[]{:S(2)}, u32[]{:S(2)}) collective-permute-start(f32[1152,128]{1,0:T(8,128)S(1)} %shard_map.184.refs_3_.refs_1_), channel_id=1, source_target_pairs={{0,16},{1,17},{2,18},{3,19},{4,20},{5,21},{6,22},{7,23},{8,24},{9,... | collective-permute-start | bytes 1769480 | tf_op jit(solution)/shard_map/ppermute | solution.py:657
  29.0 26.0 %collective-permute-start.6 = (f32[1152,128]{1,0:T(8,128)S(1)}, f32[1152,128]{1,0:T(8,128)S(1)}, u32[]{:S(2)}, u32[]{:S(2)}) collective-permute-start(f32[1152,128]{1,0:T(8,128)S(1)} %shard_map.185.refs_3_.refs_1_), channel_id=1, source_target_pairs={{0,16},{1,17},{2,18},{3,19},{4,20},{5,21},{6,22},{7,23},{8,24},{9,... | collective-permute-start | bytes 1769480 | tf_op jit(solution)/shard_map/ppermute | solution.py:657
  63.9 28.9 %collective-permute-start.11 = (f32[1152,128]{1,0:T(8,128)S(1)}, f32[1152,128]{1,0:T(8,128)S(1)}, u32[]{:S(2)}, u32[]{:S(2)}) collective-permute-start(f32[1152,128]{1,0:T(8,128)S(1)} %shard_map.186.refs_3_.refs_1_), channel_id=1, source_target_pairs={{0,16},{1,17},{2,18},{3,19},{4,20},{5,21},{6,22},{7,23},{8,24},{9,... | collective-permute-start | bytes 1769480 | tf_op jit(solution)/shard_map/ppermute | solution.py:657
  65.4 28.1 %collective-permute-start.13 = (f32[1152,128]{1,0:T(8,128)S(1)}, f32[1152,128]{1,0:T(8,128)S(1)}, u32[]{:S(2)}, u32[]{:S(2)}) collective-permute-start(f32[1152,128]{1,0:T(8,128)S(1)} %shard_map.187.last.refs_1_), channel_id=1, source_target_pairs={{0,16},{1,17},{2,18},{3,19},{4,20},{5,21},{6,22},{7,23},{8,24},{9,... | collective-permute-start | bytes 1769480 | tf_op jit(solution)/shard_map/ppermute | solution.py:657
  100.7 25.8 %collective-permute-start.10 = (f32[4,128,256]{2,1,0:T(8,128)S(1)}, f32[4,128,256]{2,1,0:T(8,128)S(1)}, u32[]{:S(2)}, u32[]{:S(2)}) collective-permute-start(f32[4,128,256]{2,1,0:T(8,128)S(1)} %shard_map.196.refs_3_.refs_1_), channel_id=1, source_target_pairs={{0,4},{1,5},{2,6},{3,7},{4,0},{5,1},{6,2},{7,3},{8,12},{9,13},{10,... | collective-permute-start | bytes 1572872 | tf_op jit(solution)/shard_map/ppermute | solution.py:727
  141.7 29.3 %collective-permute-start.17 = (f32[8,128,256]{2,1,0:T(8,128)}, f32[8,128,256]{2,1,0:T(8,128)S(1)}, u32[]{:S(2)}, u32[]{:S(2)}) collective-permute-start(f32[8,128,256]{2,1,0:T(8,128)} %shard_map.202.refs_3_.refs_0_), channel_id=1, source_target_pairs={{0,16},{1,17},{2,18},{3,19},{4,20},{5,21},{6,22},{7,23},{8,24},{9,... | collective-permute-start | bytes 3145736 | tf_op jit(solution)/shard_map/ppermute | solution.py:657
  144.6 24.2 %collective-permute-start.19 = (f32[4,128,256]{2,1,0:T(8,128)}, f32[4,128,256]{2,1,0:T(8,128)}, u32[]{:S(2)}, u32[]{:S(2)}) collective-permute-start(f32[4,128,256]{2,1,0:T(8,128)} %shard_map.203.refs_1_.refs_3_), channel_id=1, source_target_pairs={{0,4},{1,5},{2,6},{3,7},{4,0},{5,1},{6,2},{7,3},{8,12},{9,13},{10,... | collective-permute-start | bytes 1572872 | tf_op jit(solution)/shard_map/ppermute | solution.py:727
  146.4 30.0 %collective-permute-start.20 = (f32[8,128,256]{2,1,0:T(8,128)}, f32[8,128,256]{2,1,0:T(8,128)}, u32[]{:S(2)}, u32[]{:S(2)}) collective-permute-start(f32[8,128,256]{2,1,0:T(8,128)} %shard_map.202.refs_3_.refs_0_), channel_id=1, source_target_pairs={{0,8},{1,9},{2,10},{3,11},{4,12},{5,13},{6,14},{7,15},{8,0},{9,1},... | collective-permute-start | bytes 3145736 | tf_op jit(solution)/shard_map/ppermute | solution.py:657
  193.4 25.5 %collective-permute-start.24 = (f32[2048,128]{1,0:T(8,128)S(1)}, f32[2048,128]{1,0:T(8,128)S(1)}, u32[]{:S(2)}, u32[]{:S(2)}) collective-permute-start(f32[2048,128]{1,0:T(8,128)S(1)} %shard_map.207.refs_3_.refs_1_), channel_id=1, source_target_pairs={{0,16},{1,17},{2,18},{3,19},{4,20},{5,21},{6,22},{7,23},{8,24},{9,... | collective-permute-start | bytes 3145736 | tf_op jit(solution)/shard_map/ppermute | solution.py:657
  219.6 25.9 %collective-permute-start.29 = (f32[8,128,256]{2,1,0:T(8,128)}, f32[8,128,256]{2,1,0:T(8,128)}, u32[]{:S(2)}, u32[]{:S(2)}) collective-permute-start(f32[8,128,256]{2,1,0:T(8,128)} %shard_map.208.refs_3_.refs_0_), channel_id=1, source_target_pairs={{0,16},{1,17},{2,18},{3,19},{4,20},{5,21},{6,22},{7,23},{8,24},{9,... | collective-permute-start | bytes 3145736 | tf_op jit(solution)/shard_map/ppermute | solution.py:657
  224.6 21.6 %collective-permute-start.30 = (f32[8,128,256]{2,1,0:T(8,128)}, f32[8,128,256]{2,1,0:T(8,128)}, u32[]{:S(2)}, u32[]{:S(2)}) collective-permute-start(f32[8,128,256]{2,1,0:T(8,128)} %shard_map.208.refs_3_.refs_0_), channel_id=1, source_target_pairs={{0,8},{1,9},{2,10},{3,11},{4,12},{5,13},{6,14},{7,15},{8,0},{9,1},... | collective-permute-start | bytes 3145736 | tf_op jit(solution)/shard_map/ppermute | solution.py:657
  264.4 26.9 %collective-permute-start.36 = (f32[2048,128]{1,0:T(8,128)S(1)}, f32[2048,128]{1,0:T(8,128)S(1)}, u32[]{:S(2)}, u32[]{:S(2)}) collective-permute-start(f32[2048,128]{1,0:T(8,128)S(1)} %shard_map.215.refs_3_.refs_1_), channel_id=1, source_target_pairs={{0,16},{1,17},{2,18},{3,19},{4,20},{5,21},{6,22},{7,23},{8,24},{9,... | collective-permute-start | bytes 3145736 | tf_op jit(solution)/shard_map/ppermute | solution.py:657
  264.5 26.2 %collective-permute-start.32 = (f32[4,128,256]{2,1,0:T(8,128)S(1)}, f32[4,128,256]{2,1,0:T(8,128)S(1)}, u32[]{:S(2)}, u32[]{:S(2)}) collective-permute-start(f32[4,128,256]{2,1,0:T(8,128)S(1)} %shard_map.214.refs_4_.refs_1_), channel_id=1, source_target_pairs={{0,4},{1,5},{2,6},{3,7},{4,0},{5,1},{6,2},{7,3},{8,12},{9,13},{10,... | collective-permute-start | bytes 1572872 | tf_op jit(solution)/shard_map/ppermute | solution.py:727
  311.5 26.3 %collective-permute-start.39 = (f32[1152,128]{1,0:T(8,128)S(1)}, f32[1152,128]{1,0:T(8,128)S(1)}, u32[]{:S(2)}, u32[]{:S(2)}) collective-permute-start(f32[1152,128]{1,0:T(8,128)S(1)} %shard_map.221.refs_3_.refs_2_), channel_id=1, source_target_pairs={{0,16},{1,17},{2,18},{3,19},{4,20},{5,21},{6,22},{7,23},{8,24},{9,... | collective-permute-start | bytes 1769480 | tf_op jit(solution)/shard_map/ppermute | solution.py:657
  344.0 31.1 %collective-permute-start.44 = (f32[4,288,256]{2,1,0:T(8,128)S(1)}, f32[4,288,256]{2,1,0:T(8,128)S(1)}, u32[]{:S(2)}, u32[]{:S(2)}) collective-permute-start(f32[4,288,256]{2,1,0:T(8,128)S(1)} %get-tuple-element.96), channel_id=1, source_target_pairs={{0,1},{1,0},{2,3},{3,2},{4,5},{5,4},{6,7},{7,6},{8,9},{9,8},{10,11... | collective-permute-start | bytes 3538952 | tf_op jit(solution)/shard_map/ppermute | solution.py:657
  345.4 30.4 %collective-permute-start.48 = (f32[1152,128]{1,0:T(8,128)S(1)}, f32[1152,128]{1,0:T(8,128)S(1)}, u32[]{:S(2)}, u32[]{:S(2)}) collective-permute-start(f32[1152,128]{1,0:T(8,128)S(1)} %shard_map.222.refs_3_.refs_2_), channel_id=1, source_target_pairs={{0,16},{1,17},{2,18},{3,19},{4,20},{5,21},{6,22},{7,23},{8,24},{9,... | collective-permute-start | bytes 1769480 | tf_op jit(solution)/shard_map/ppermute | solution.py:657
  347.1 25.3 %collective-permute-start.45 = (f32[4,128,256]{2,1,0:T(8,128)S(1)}, f32[4,128,256]{2,1,0:T(8,128)S(1)}, u32[]{:S(2)}, u32[]{:S(2)}) collective-permute-start(f32[4,128,256]{2,1,0:T(8,128)S(1)} %shard_map.224.refs_4_.refs_1_), channel_id=1, source_target_pairs={{0,4},{1,5},{2,6},{3,7},{4,0},{5,1},{6,2},{7,3},{8,12},{9,13},{10,... | collective-permute-start | bytes 1572872 | tf_op jit(solution)/shard_map/ppermute | solution.py:727
  395.3 28.9 %collective-permute-start.54 = (f32[4,288,256]{2,1,0:T(8,128)S(1)}, f32[4,288,256]{2,1,0:T(8,128)S(1)}, u32[]{:S(2)}, u32[]{:S(2)}) collective-permute-start(f32[4,288,256]{2,1,0:T(8,128)S(1)} %get-tuple-element.106), channel_id=1, source_target_pairs={{0,1},{1,0},{2,3},{3,2},{4,5},{5,4},{6,7},{7,6},{8,9},{9,8},{10,11... | collective-permute-start | bytes 3538952 | tf_op jit(solution)/shard_map/ppermute | solution.py:657
  417.7 32.4 %collective-permute-start.58 = (f32[4,288,256]{2,1,0:T(8,128)}, f32[4,288,256]{2,1,0:T(8,128)S(1)}, u32[]{:S(2)}, u32[]{:S(2)}) collective-permute-start(f32[4,288,256]{2,1,0:T(8,128)} %get-tuple-element.110), channel_id=1, source_target_pairs={{0,1},{1,0},{2,3},{3,2},{4,5},{5,4},{6,7},{7,6},{8,9},{9,8},{10,11... | collective-permute-start | bytes 3538952 | tf_op jit(solution)/shard_map/ppermute | solution.py:657
  427.4 22.1 %collective-permute-start.59 = (f32[2,288,256]{2,1,0:T(8,128)S(1)}, f32[2,288,256]{2,1,0:T(8,128)S(1)}, u32[]{:S(2)}, u32[]{:S(2)}) collective-permute-start(f32[2,288,256]{2,1,0:T(8,128)S(1)} %get-tuple-element.108.refs_4_), channel_id=1, source_target_pairs={{0,2},{1,3},{2,0},{3,1},{4,6},{5,7},{6,4},{7,5},{8,10},{9,11},{10,... | collective-permute-start | bytes 1769480 | tf_op jit(solution)/shard_map/ppermute | solution.py:727
  432.9 39.3 %collective-permute-start.62 = (f32[4,160,256]{2,1,0:T(8,128)S(1)}, f32[4,160,256]{2,1,0:T(8,128)S(1)}, u32[]{:S(2)}, u32[]{:S(2)}) collective-permute-start(f32[4,160,256]{2,1,0:T(8,128)S(1)} %get-tuple-element.117), channel_id=1, source_target_pairs={{0,1},{1,0},{2,3},{3,2},{4,5},{5,4},{6,7},{7,6},{8,9},{9,8},{10,11... | collective-permute-start | bytes 1966088 | tf_op jit(solution)/shard_map/ppermute | solution.py:657
  450.8 26.2 %collective-permute-start.60 = (f32[2,288,256]{2,1,0:T(8,128)S(1)}, f32[2,288,256]{2,1,0:T(8,128)S(1)}, u32[]{:S(2)}, u32[]{:S(2)}) collective-permute-start(f32[2,288,256]{2,1,0:T(8,128)S(1)} %get-tuple-element.114.refs_3_), channel_id=1, source_target_pairs={{0,2},{1,3},{2,0},{3,1},{4,6},{5,7},{6,4},{7,5},{8,10},{9,11},{10,... | collective-permute-start | bytes 1769480 | tf_op jit(solution)/shard_map/ppermute | solution.py:727
  452.9 23.4 %collective-permute-start.61 = (f32[4,128,256]{2,1,0:T(8,128)S(1)}, f32[4,128,256]{2,1,0:T(8,128)S(1)}, u32[]{:S(2)}, u32[]{:S(2)}) collective-permute-start(f32[4,128,256]{2,1,0:T(8,128)S(1)} %get-tuple-element.116), channel_id=1, source_target_pairs={{0,1},{1,0},{2,3},{3,2},{4,5},{5,4},{6,7},{7,6},{8,9},{9,8},{10,11... | collective-permute-start | bytes 1572872 | tf_op jit(solution)/shard_map/ppermute | solution.py:657
  477.7 19.8 %collective-permute-start.66 = (f32[2,128,256]{2,1,0:T(8,128)S(1)}, f32[2,128,256]{2,1,0:T(8,128)S(1)}, u32[]{:S(2)}, u32[]{:S(2)}) collective-permute-start(f32[2,128,256]{2,1,0:T(8,128)S(1)} %get-tuple-element.120.refs_3_), channel_id=1, source_target_pairs={{0,2},{1,3},{2,0},{3,1},{4,6},{5,7},{6,4},{7,5},{8,10},{9,11},{10,... | collective-permute-start | bytes 786440 | tf_op jit(solution)/shard_map/ppermute | solution.py:727
  (84 other events, 632.9 us)

commit v5 on v4

--- a/solution.py
+++ b/solution.py
@@ -54,14 +54,14 @@
     ("correct_x", 0, 0),
     ("correct_x", 0, 1),
     ("pick_y", 1),
-    ("pick_z", 1),
     ("reduce", 0, 0),
     ("final", 0, 0),
+    ("pick_z", 1),
     ("whole",),
     ("pick_g", 1),
-    ("final_y", 0, 0),
     ("reduce", 0, 1),
     ("final", 0, 1),
+    ("final_y", 0, 0),
     ("correct", 1, 0),
     ("correct", 1, 1),
     ("correct_x", 1, 0),

time: 517 us -> 511 us (0.988)
  waiting for transfers between devices: 280 us -> 270 us
    ppermute x18, waiting for transfers between devices: 160 us -> 152 us  [exchange(): return lax.ppermute(array, AXES, listed)]
    unnamed x79 -> x83, local copies, waits for them, and re-layouts: 16 us -> 15.8 us
  transfers between devices with their start and end apart: 69 -> 69, of which waited for: 42 -> 44; matrix products, arithmetic and copies ran while one was open for 1% -> 1% of each run, Pallas kernels for 22% -> 23%
where the time goes in v5:
time: 511 us; the launch traced here: 504 us
  waiting for transfers between devices  270 us (53%)
  Pallas kernels  153 us (30%)
  starting transfers between devices  57.3 us (11%)
  local copies, waits for them, and re-layouts  17 us (3%)
    ppermute x18, waiting for transfers between devices, exchange(): return lax.ppermute(array, AXES, listed)  152 us
    ppermute x51, waiting for transfers between devices, send(): return lax.ppermute(array, AXES, group.pairs[step - 1])  118 us
    pallas_call x64, Pallas kernels, __call__(): pl.pallas_call(lambda *refs: kernel(*refs[:count + 1], *refs[count + 2:])...  87.5 us
    pallas_call x4, Pallas kernels, base(): pl.pallas_call(base_kernel, grid_spec=pltpu.PrefetchScalarGridSpec(num_sc...  45.3 us
    ppermute x51, starting transfers between devices, send(): return lax.ppermute(array, AXES, group.pairs[step - 1])  33 us
    ppermute x18, starting transfers between devices, exchange(): return lax.ppermute(array, AXES, listed)  24.3 us
    pallas_call x2, Pallas kernels, root(): pl.pallas_call(root_kernel, grid_spec=pltpu.PrefetchScalarGridSpec(num_sc...  20.1 us
    unnamed x83, local copies, waits for them, and re-layouts  15.8 us
  transfers between devices with their start and end apart: 69, of which 44 were waited for; matrix products, arithmetic and copies ran while one was open for 1% of the time, Pallas kernels for 23%

profile of v5, /device:TPU:0, one launch (start us, length us, event | category | flops | bytes accessed | tf_op | source)
XLA Modules:
  0.0 504.0 jit_solution(10089499959903714280)
XLA Ops:
  2.1 10.5 %shard_map.182 = (f32[1152,128]{1,0:T(8,128)}, f32[1152,128]{1,0:T(8,128)}, f32[1152,128]{1,0:T(8,128)}, f32[1152,128]{1,0:T(8,128)}) custom-call(s32[11]{0:T(128)} %pad_add_fusion.2.refs_0_.refs_5_.me, f32[768,1536]{1,0:T(8,128)} %refs_1_.22, f32[384,768]{1,0:T(8,128)} %refs_2_.22, f32[1536,512]{1,0:T(8,128)} %refs_3_.4, f32[768,512]{1,0:T(8,128)} %refs_4_.4, ...), custom_call_target="tpu_custom_call" | custom-call | flops 1 | bytes 1 | tf_op jit(solution)/shard_map/pallas_call | solution.py:320
  13.0 10.2 %shard_map.183 = (f32[1152,128]{1,0:T(8,128)}, f32[1152,128]{1,0:T(8,128)}, f32[1152,128]{1,0:T(8,128)}, f32[1152,128]{1,0:T(8,128)}) custom-call(s32[11]{0:T(128)} %pad_add_fusion.2.refs_0_.refs_5_.me, f32[640,1280]{1,0:T(8,128)} %refs_1_.23, f32[512,1024]{1,0:T(8,128)} %refs_2_.23, f32[1280,512]{1,0:T(8,128)} %refs_3_.5, f32[1024,512]{1,0:T(8,128)} %refs_4_.5, ...), custom_call_target="tpu_custom_call" | custom-call | flops 1 | bytes 1 | tf_op jit(solution)/shard_map/pallas_call | solution.py:320
  31.4 11.4 %shard_map.188.last.upper = f32[1024,256]{1,0:T(8,128)S(1)} custom-call(s32[11]{0:T(128)S(1)} %copy-done.29, f32[2048,4096]{1,0:T(8,128)} %right.3, f32[4096,512]{1,0:T(8,128)S(1)} %copy-done, f32[4096,512]{1,0:T(8,128)S(1)} %copy-done, f32[1152,128]{1,0:T(8,128)S(1)} %shard_map.187.last.refs_1_), custom_call_target="tpu_custom_call" | custom-call | flops 1 | bytes 1 | tf_op jit(solution)/shard_map/pallas_call | solution.py:451
  42.8 11.2 %shard_map.189.refs_3_.lower = f32[1024,256]{1,0:T(8,128)S(1)} custom-call(s32[11]{0:T(128)S(1)} %copy-done.29, f32[2048,4096]{1,0:T(8,128)} %right.3, f32[4096,512]{1,0:T(8,128)S(1)} %copy-done, f32[4096,512]{1,0:T(8,128)S(1)} %copy-done, f32[1024,256]{1,0:T(8,128)S(1)} %shard_map.188.last.upper), custom_call_target="tpu_custom_call" | custom-call | flops 1 | bytes 1 | tf_op jit(solution)/shard_map/pallas_call | solution.py:451
  65.9 11.6 %shard_map.193.refs_3_.upper = f32[1024,256]{1,0:T(8,128)S(1)} custom-call(s32[11]{0:T(128)S(1)} %copy-done.29, f32[2048,4096]{1,0:T(8,128)} %right.3, f32[4096,512]{1,0:T(8,128)S(1)} %copy-done, f32[4096,512]{1,0:T(8,128)S(1)} %copy-done, f32[4,128,256]{2,1,0:T(8,128)S(1)} %get-tuple-element.77.last.refs_1_), custom_call_target="tpu_custom_call" | custom-call | flops 1 | bytes 1 | tf_op jit(solution)/shard_map/pallas_call | solution.py:451
  80.7 11.2 %shard_map.195.refs_3_.lower = f32[1024,256]{1,0:T(8,128)S(1)} custom-call(s32[11]{0:T(128)S(1)} %copy-done.29, f32[2048,4096]{1,0:T(8,128)} %right.3, f32[4096,512]{1,0:T(8,128)S(1)} %copy-done, f32[4096,512]{1,0:T(8,128)S(1)} %copy-done, f32[4,128,256]{2,1,0:T(8,128)S(1)} %shard_map.194.last.refs_1_), custom_call_target="tpu_custom_call" | custom-call | flops 1 | bytes 1 | tf_op jit(solution)/shard_map/pallas_call | solution.py:451
  103.3 10.9 %collective-permute-done.15.refs_2_ = f32[4,128,256]{2,1,0:T(8,128)S(1)} collective-permute-done((f32[4,128,256]{2,1,0:T(8,128)S(1)}, f32[4,128,256]{2,1,0:T(8,128)S(1)}, u32[]{:S(2)}, u32[]{:S(2)}) %collective-permute-start.15) | collective-permute-done | bytes 524320 | tf_op jit(solution)/shard_map/ppermute | solution.py:657
  114.8 11.7 %collective-permute-done.10.refs_2_ = f32[4,128,256]{2,1,0:T(8,128)S(1)} collective-permute-done((f32[4,128,256]{2,1,0:T(8,128)S(1)}, f32[4,128,256]{2,1,0:T(8,128)S(1)}, u32[]{:S(2)}, u32[]{:S(2)}) %collective-permute-start.10) | collective-permute-done | bytes 524320 | tf_op jit(solution)/shard_map/ppermute | solution.py:727
  129.4 10.6 %collective-permute-done.16.refs_2_ = f32[4,128,256]{2,1,0:T(8,128)S(1)} collective-permute-done((f32[4,128,256]{2,1,0:T(8,128)S(1)}, f32[4,128,256]{2,1,0:T(8,128)S(1)}, u32[]{:S(2)}, u32[]{:S(2)}) %collective-permute-start.16) | collective-permute-done | bytes 524320 | tf_op jit(solution)/shard_map/ppermute | solution.py:657
  146.4 22.3 %collective-permute-done.19.refs_2_ = f32[4,128,256]{2,1,0:T(8,128)} collective-permute-done((f32[4,128,256]{2,1,0:T(8,128)}, f32[4,128,256]{2,1,0:T(8,128)}, u32[]{:S(2)}, u32[]{:S(2)}) %collective-permute-start.19) | collective-permute-done | bytes 524320 | tf_op jit(solution)/shard_map/ppermute | solution.py:727
  180.0 9.8 %shard_map.206 = (f32[2048,128]{1,0:T(8,128)S(1)}, f32[1024,128]{1,0:T(8,128)S(1)}, f32[1024,128]{1,0:T(8,128)S(1)}) custom-call(s32[4,32]{1,0:T(4,128)S(1)} %pad_add_fusion.list_ref, f32[2048,4096]{1,0:T(8,128)} %right.3, f32[2048,4096]{1,0:T(8,128)} %right.3, f32[1024,256]{1,0:T(8,128)S(1)} %copy-done.14, f32[1024,256]{1,0:T(8,128)S(1)} %copy-done.12, ...), custom_call_target="tpu_custom_call" | custom-call | flops 1 | bytes 1 | tf_op jit(solution)/shard_map/pallas_call | solution.py:522
  195.2 13.4 %collective-permute-done.25.refs_2_ = f32[4,128,256]{2,1,0:T(8,128)S(1)} collective-permute-done((f32[4,128,256]{2,1,0:T(8,128)S(1)}, f32[4,128,256]{2,1,0:T(8,128)S(1)}, u32[]{:S(2)}, u32[]{:S(2)}) %collective-permute-start.25) | collective-permute-done | bytes 524320 | tf_op jit(solution)/shard_map/ppermute | solution.py:657
  210.2 8.3 %collective-permute-done.24.refs_2_ = f32[2048,128]{1,0:T(8,128)S(1)} collective-permute-done((f32[2048,128]{1,0:T(8,128)S(1)}, f32[2048,128]{1,0:T(8,128)S(1)}, u32[]{:S(2)}, u32[]{:S(2)}) %collective-permute-start.24) | collective-permute-done | bytes 1048608 | tf_op jit(solution)/shard_map/ppermute | solution.py:657
  224.2 12.6 %collective-permute-done.27.refs_2_ = f32[4,128,256]{2,1,0:T(8,128)S(1)} collective-permute-done((f32[4,128,256]{2,1,0:T(8,128)S(1)}, f32[4,128,256]{2,1,0:T(8,128)S(1)}, u32[]{:S(2)}, u32[]{:S(2)}) %collective-permute-start.27) | collective-permute-done | bytes 524320 | tf_op jit(solution)/shard_map/ppermute | solution.py:657
  250.4 10.3 %shard_map.213 = (f32[2048,128]{1,0:T(8,128)S(1)}, f32[1024,128]{1,0:T(8,128)S(1)}, f32[1024,128]{1,0:T(8,128)S(1)}) custom-call(s32[4,32]{1,0:T(4,128)S(1)} %pad_add_fusion.list_ref, f32[2048,4096]{1,0:T(8,128)} %right.3, f32[2048,4096]{1,0:T(8,128)} %right.3, f32[1024,256]{1,0:T(8,128)S(1)} %copy-done.16, f32[1024,256]{1,0:T(8,128)S(1)} %copy-done.18, ...), custom_call_target="tpu_custom_call" | custom-call | flops 1 | bytes 1 | tf_op jit(solution)/shard_map/pallas_call | solution.py:522
  266.7 24.7 %collective-permute-done.32.refs_2_ = f32[4,128,256]{2,1,0:T(8,128)S(1)} collective-permute-done((f32[4,128,256]{2,1,0:T(8,128)S(1)}, f32[4,128,256]{2,1,0:T(8,128)S(1)}, u32[]{:S(2)}, u32[]{:S(2)}) %collective-permute-start.32) | collective-permute-done | bytes 524320 | tf_op jit(solution)/shard_map/ppermute | solution.py:727
  296.3 10.8 %collective-permute-done.35.refs_4_ = f32[4,128,256]{2,1,0:T(8,128)S(1)} collective-permute-done((f32[4,128,256]{2,1,0:T(8,128)S(1)}, f32[4,128,256]{2,1,0:T(8,128)S(1)}, u32[]{:S(2)}, u32[]{:S(2)}) %collective-permute-start.35) | collective-permute-done | bytes 524320 | tf_op jit(solution)/shard_map/ppermute | solution.py:657
  313.7 11.7 %collective-permute-done.40.refs_2_ = f32[4,128,256]{2,1,0:T(8,128)S(1)} collective-permute-done((f32[4,128,256]{2,1,0:T(8,128)S(1)}, f32[4,128,256]{2,1,0:T(8,128)S(1)}, u32[]{:S(2)}, u32[]{:S(2)}) %collective-permute-start.40) | collective-permute-done | bytes 524320 | tf_op jit(solution)/shard_map/ppermute | solution.py:657
  346.4 21.4 %collective-permute-done.46.refs_2_ = f32[4,128,256]{2,1,0:T(8,128)S(1)} collective-permute-done((f32[4,128,256]{2,1,0:T(8,128)S(1)}, f32[4,128,256]{2,1,0:T(8,128)S(1)}, u32[]{:S(2)}, u32[]{:S(2)}) %collective-permute-start.46) | collective-permute-done | bytes 524320 | tf_op jit(solution)/shard_map/ppermute | solution.py:727
  378.6 7.1 %collective-permute-done.49.refs_4_ = f32[4,128,256]{2,1,0:T(8,128)S(1)} collective-permute-done((f32[4,128,256]{2,1,0:T(8,128)S(1)}, f32[4,128,256]{2,1,0:T(8,128)S(1)}, u32[]{:S(2)}, u32[]{:S(2)}) %collective-permute-start.49) | collective-permute-done | bytes 524320 | tf_op jit(solution)/shard_map/ppermute | solution.py:657
  392.3 11.8 %collective-permute-done.48.refs_2_ = f32[2,288,256]{2,1,0:T(8,128)S(1)} collective-permute-done((f32[2,288,256]{2,1,0:T(8,128)S(1)}, f32[2,288,256]{2,1,0:T(8,128)S(1)}, u32[]{:S(2)}, u32[]{:S(2)}) %collective-permute-start.48) | collective-permute-done | bytes 589856 | tf_op jit(solution)/shard_map/ppermute | solution.py:727
  429.1 14.2 %collective-permute-done.52.refs_2_ = f32[288,256]{1,0:T(8,128)S(1)} collective-permute-done((f32[288,256]{1,0:T(8,128)S(1)}, f32[288,256]{1,0:T(8,128)S(1)}, u32[]{:S(2)}, u32[]{:S(2)}) %collective-permute-start.52) | collective-permute-done | bytes 294944 | tf_op jit(solution)/shard_map/ppermute | solution.py:727
  449.7 17.6 %collective-permute-done.63.refs_2_ = f32[288,256]{1,0:T(8,128)S(1)} collective-permute-done((f32[288,256]{1,0:T(8,128)S(1)}, f32[288,256]{1,0:T(8,128)S(1)}, u32[]{:S(2)}, u32[]{:S(2)}) %collective-permute-start.63) | collective-permute-done | bytes 294944 | tf_op jit(solution)/shard_map/ppermute | solution.py:727
  475.2 11.1 %collective-permute-done.65.refs_2_ = f32[2,160,256]{2,1,0:T(8,128)S(1)} collective-permute-done((f32[2,160,256]{2,1,0:T(8,128)S(1)}, f32[2,160,256]{2,1,0:T(8,128)S(1)}, u32[]{:S(2)}, u32[]{:S(2)}) %collective-permute-start.65) | collective-permute-done | bytes 327712 | tf_op jit(solution)/shard_map/ppermute | solution.py:727
  (299 shorter events, 194.9 us)
Async XLA Ops:
  25.5 28.6 %collective-permute-start.1 = (f32[1152,128]{1,0:T(8,128)S(1)}, f32[1152,128]{1,0:T(8,128)S(1)}, u32[]{:S(2)}, u32[]{:S(2)}) collective-permute-start(f32[1152,128]{1,0:T(8,128)S(1)} %shard_map.184.refs_3_.refs_1_), channel_id=1, source_target_pairs={{0,16},{1,17},{2,18},{3,19},{4,20},{5,21},{6,22},{7,23},{8,24},{9,... | collective-permute-start | bytes 1769480 | tf_op jit(solution)/shard_map/ppermute | solution.py:657
  29.0 26.0 %collective-permute-start.6 = (f32[1152,128]{1,0:T(8,128)S(1)}, f32[1152,128]{1,0:T(8,128)S(1)}, u32[]{:S(2)}, u32[]{:S(2)}) collective-permute-start(f32[1152,128]{1,0:T(8,128)S(1)} %shard_map.185.refs_3_.refs_1_), channel_id=1, source_target_pairs={{0,16},{1,17},{2,18},{3,19},{4,20},{5,21},{6,22},{7,23},{8,24},{9,... | collective-permute-start | bytes 1769480 | tf_op jit(solution)/shard_map/ppermute | solution.py:657
  63.9 28.9 %collective-permute-start.11 = (f32[1152,128]{1,0:T(8,128)S(1)}, f32[1152,128]{1,0:T(8,128)S(1)}, u32[]{:S(2)}, u32[]{:S(2)}) collective-permute-start(f32[1152,128]{1,0:T(8,128)S(1)} %shard_map.186.refs_3_.refs_1_), channel_id=1, source_target_pairs={{0,16},{1,17},{2,18},{3,19},{4,20},{5,21},{6,22},{7,23},{8,24},{9,... | collective-permute-start | bytes 1769480 | tf_op jit(solution)/shard_map/ppermute | solution.py:657
  65.4 28.1 %collective-permute-start.13 = (f32[1152,128]{1,0:T(8,128)S(1)}, f32[1152,128]{1,0:T(8,128)S(1)}, u32[]{:S(2)}, u32[]{:S(2)}) collective-permute-start(f32[1152,128]{1,0:T(8,128)S(1)} %shard_map.187.last.refs_1_), channel_id=1, source_target_pairs={{0,16},{1,17},{2,18},{3,19},{4,20},{5,21},{6,22},{7,23},{8,24},{9,... | collective-permute-start | bytes 1769480 | tf_op jit(solution)/shard_map/ppermute | solution.py:657
  100.7 25.8 %collective-permute-start.10 = (f32[4,128,256]{2,1,0:T(8,128)S(1)}, f32[4,128,256]{2,1,0:T(8,128)S(1)}, u32[]{:S(2)}, u32[]{:S(2)}) collective-permute-start(f32[4,128,256]{2,1,0:T(8,128)S(1)} %shard_map.196.refs_3_.refs_1_), channel_id=1, source_target_pairs={{0,4},{1,5},{2,6},{3,7},{4,0},{5,1},{6,2},{7,3},{8,12},{9,13},{10,... | collective-permute-start | bytes 1572872 | tf_op jit(solution)/shard_map/ppermute | solution.py:727
  141.6 29.3 %collective-permute-start.17 = (f32[8,128,256]{2,1,0:T(8,128)}, f32[8,128,256]{2,1,0:T(8,128)S(1)}, u32[]{:S(2)}, u32[]{:S(2)}) collective-permute-start(f32[8,128,256]{2,1,0:T(8,128)} %shard_map.202.refs_3_.refs_0_), channel_id=1, source_target_pairs={{0,16},{1,17},{2,18},{3,19},{4,20},{5,21},{6,22},{7,23},{8,24},{9,... | collective-permute-start | bytes 3145736 | tf_op jit(solution)/shard_map/ppermute | solution.py:657
  144.5 24.2 %collective-permute-start.19 = (f32[4,128,256]{2,1,0:T(8,128)}, f32[4,128,256]{2,1,0:T(8,128)}, u32[]{:S(2)}, u32[]{:S(2)}) collective-permute-start(f32[4,128,256]{2,1,0:T(8,128)} %shard_map.203.refs_1_.refs_3_), channel_id=1, source_target_pairs={{0,4},{1,5},{2,6},{3,7},{4,0},{5,1},{6,2},{7,3},{8,12},{9,13},{10,... | collective-permute-start | bytes 1572872 | tf_op jit(solution)/shard_map/ppermute | solution.py:727
  146.4 30.0 %collective-permute-start.20 = (f32[8,128,256]{2,1,0:T(8,128)}, f32[8,128,256]{2,1,0:T(8,128)}, u32[]{:S(2)}, u32[]{:S(2)}) collective-permute-start(f32[8,128,256]{2,1,0:T(8,128)} %shard_map.202.refs_3_.refs_0_), channel_id=1, source_target_pairs={{0,8},{1,9},{2,10},{3,11},{4,12},{5,13},{6,14},{7,15},{8,0},{9,1},... | collective-permute-start | bytes 3145736 | tf_op jit(solution)/shard_map/ppermute | solution.py:657
  193.2 25.3 %collective-permute-start.24 = (f32[2048,128]{1,0:T(8,128)S(1)}, f32[2048,128]{1,0:T(8,128)S(1)}, u32[]{:S(2)}, u32[]{:S(2)}) collective-permute-start(f32[2048,128]{1,0:T(8,128)S(1)} %shard_map.207.refs_3_.refs_1_), channel_id=1, source_target_pairs={{0,16},{1,17},{2,18},{3,19},{4,20},{5,21},{6,22},{7,23},{8,24},{9,... | collective-permute-start | bytes 3145736 | tf_op jit(solution)/shard_map/ppermute | solution.py:657
  219.2 25.9 %collective-permute-start.29 = (f32[8,128,256]{2,1,0:T(8,128)}, f32[8,128,256]{2,1,0:T(8,128)}, u32[]{:S(2)}, u32[]{:S(2)}) collective-permute-start(f32[8,128,256]{2,1,0:T(8,128)} %shard_map.208.refs_3_.refs_0_), channel_id=1, source_target_pairs={{0,16},{1,17},{2,18},{3,19},{4,20},{5,21},{6,22},{7,23},{8,24},{9,... | collective-permute-start | bytes 3145736 | tf_op jit(solution)/shard_map/ppermute | solution.py:657
  224.2 21.7 %collective-permute-start.30 = (f32[8,128,256]{2,1,0:T(8,128)}, f32[8,128,256]{2,1,0:T(8,128)}, u32[]{:S(2)}, u32[]{:S(2)}) collective-permute-start(f32[8,128,256]{2,1,0:T(8,128)} %shard_map.208.refs_3_.refs_0_), channel_id=1, source_target_pairs={{0,8},{1,9},{2,10},{3,11},{4,12},{5,13},{6,14},{7,15},{8,0},{9,1},... | collective-permute-start | bytes 3145736 | tf_op jit(solution)/shard_map/ppermute | solution.py:657
  264.1 27.8 %collective-permute-start.36 = (f32[2048,128]{1,0:T(8,128)S(1)}, f32[2048,128]{1,0:T(8,128)S(1)}, u32[]{:S(2)}, u32[]{:S(2)}) collective-permute-start(f32[2048,128]{1,0:T(8,128)S(1)} %shard_map.215.refs_3_.refs_1_), channel_id=1, source_target_pairs={{0,16},{1,17},{2,18},{3,19},{4,20},{5,21},{6,22},{7,23},{8,24},{9,... | collective-permute-start | bytes 3145736 | tf_op jit(solution)/shard_map/ppermute | solution.py:657
  265.3 26.0 %collective-permute-start.32 = (f32[4,128,256]{2,1,0:T(8,128)S(1)}, f32[4,128,256]{2,1,0:T(8,128)S(1)}, u32[]{:S(2)}, u32[]{:S(2)}) collective-permute-start(f32[4,128,256]{2,1,0:T(8,128)S(1)} %shard_map.214.refs_4_.refs_1_), channel_id=1, source_target_pairs={{0,4},{1,5},{2,6},{3,7},{4,0},{5,1},{6,2},{7,3},{8,12},{9,13},{10,... | collective-permute-start | bytes 1572872 | tf_op jit(solution)/shard_map/ppermute | solution.py:727
  327.3 43.4 %collective-permute-start.44 = (f32[1152,128]{1,0:T(8,128)S(1)}, f32[1152,128]{1,0:T(8,128)S(1)}, u32[]{:S(2)}, u32[]{:S(2)}) collective-permute-start(f32[1152,128]{1,0:T(8,128)S(1)} %shard_map.222.refs_3_.refs_2_), channel_id=1, source_target_pairs={{0,16},{1,17},{2,18},{3,19},{4,20},{5,21},{6,22},{7,23},{8,24},{9,... | collective-permute-start | bytes 1769480 | tf_op jit(solution)/shard_map/ppermute | solution.py:657
  333.7 43.1 %collective-permute-start.43 = (f32[4,288,256]{2,1,0:T(8,128)}, f32[4,288,256]{2,1,0:T(8,128)}, u32[]{:S(2)}, u32[]{:S(2)}) collective-permute-start(f32[4,288,256]{2,1,0:T(8,128)} %get-tuple-element.96), channel_id=1, source_target_pairs={{0,1},{1,0},{2,3},{3,2},{4,5},{5,4},{6,7},{7,6},{8,9},{9,8},{10,11... | collective-permute-start | bytes 3538952 | tf_op jit(solution)/shard_map/ppermute | solution.py:657
  342.1 25.7 %collective-permute-start.46 = (f32[4,128,256]{2,1,0:T(8,128)S(1)}, f32[4,128,256]{2,1,0:T(8,128)S(1)}, u32[]{:S(2)}, u32[]{:S(2)}) collective-permute-start(f32[4,128,256]{2,1,0:T(8,128)S(1)} %shard_map.226.refs_5_.refs_1_), channel_id=1, source_target_pairs={{0,4},{1,5},{2,6},{3,7},{4,0},{5,1},{6,2},{7,3},{8,12},{9,13},{10,... | collective-permute-start | bytes 1572872 | tf_op jit(solution)/shard_map/ppermute | solution.py:727
  390.7 28.9 %collective-permute-start.54 = (f32[4,288,256]{2,1,0:T(8,128)S(1)}, f32[4,288,256]{2,1,0:T(8,128)S(1)}, u32[]{:S(2)}, u32[]{:S(2)}) collective-permute-start(f32[4,288,256]{2,1,0:T(8,128)S(1)} %copy-done.36), channel_id=1, source_target_pairs={{0,1},{1,0},{2,3},{3,2},{4,5},{5,4},{6,7},{7,6},{8,9},{9,8},{10,11... | collective-permute-start | bytes 3538952 | tf_op jit(solution)/shard_map/ppermute | solution.py:657
  411.5 33.4 %collective-permute-start.58 = (f32[4,288,256]{2,1,0:T(8,128)S(1)}, f32[4,288,256]{2,1,0:T(8,128)S(1)}, u32[]{:S(2)}, u32[]{:S(2)}) collective-permute-start(f32[4,288,256]{2,1,0:T(8,128)S(1)} %get-tuple-element.110), channel_id=1, source_target_pairs={{0,1},{1,0},{2,3},{3,2},{4,5},{5,4},{6,7},{7,6},{8,9},{9,8},{10,11... | collective-permute-start | bytes 3538952 | tf_op jit(solution)/shard_map/ppermute | solution.py:657
  422.2 22.1 %collective-permute-start.59 = (f32[2,288,256]{2,1,0:T(8,128)S(1)}, f32[2,288,256]{2,1,0:T(8,128)S(1)}, u32[]{:S(2)}, u32[]{:S(2)}) collective-permute-start(f32[2,288,256]{2,1,0:T(8,128)S(1)} %get-tuple-element.108.refs_4_), channel_id=1, source_target_pairs={{0,2},{1,3},{2,0},{3,1},{4,6},{5,7},{6,4},{7,5},{8,10},{9,11},{10,... | collective-permute-start | bytes 1769480 | tf_op jit(solution)/shard_map/ppermute | solution.py:727
  423.8 19.5 %collective-permute-start.52 = (f32[288,256]{1,0:T(8,128)S(1)}, f32[288,256]{1,0:T(8,128)S(1)}, u32[]{:S(2)}, u32[]{:S(2)}) collective-permute-start(f32[288,256]{1,0:T(8,128)S(1)} %get-tuple-element.105), channel_id=1, source_target_pairs={{0,4},{1,5},{2,6},{3,7},{4,0},{5,1},{6,2},{7,3},{8,12},{9,13},{10,... | collective-permute-start | bytes 884744 | tf_op jit(solution)/shard_map/ppermute | solution.py:727
  428.5 39.3 %collective-permute-start.62 = (f32[4,160,256]{2,1,0:T(8,128)S(1)}, f32[4,160,256]{2,1,0:T(8,128)S(1)}, u32[]{:S(2)}, u32[]{:S(2)}) collective-permute-start(f32[4,160,256]{2,1,0:T(8,128)S(1)} %get-tuple-element.117), channel_id=1, source_target_pairs={{0,1},{1,0},{2,3},{3,2},{4,5},{5,4},{6,7},{7,6},{8,9},{9,8},{10,11... | collective-permute-start | bytes 1966088 | tf_op jit(solution)/shard_map/ppermute | solution.py:657
  445.6 26.2 %collective-permute-start.60 = (f32[2,288,256]{2,1,0:T(8,128)S(1)}, f32[2,288,256]{2,1,0:T(8,128)S(1)}, u32[]{:S(2)}, u32[]{:S(2)}) collective-permute-start(f32[2,288,256]{2,1,0:T(8,128)S(1)} %get-tuple-element.114.refs_3_), channel_id=1, source_target_pairs={{0,2},{1,3},{2,0},{3,1},{4,6},{5,7},{6,4},{7,5},{8,10},{9,11},{10,... | collective-permute-start | bytes 1769480 | tf_op jit(solution)/shard_map/ppermute | solution.py:727
  448.5 22.6 %collective-permute-start.61 = (f32[4,128,256]{2,1,0:T(8,128)S(1)}, f32[4,128,256]{2,1,0:T(8,128)S(1)}, u32[]{:S(2)}, u32[]{:S(2)}) collective-permute-start(f32[4,128,256]{2,1,0:T(8,128)S(1)} %get-tuple-element.116), channel_id=1, source_target_pairs={{0,1},{1,0},{2,3},{3,2},{4,5},{5,4},{6,7},{7,6},{8,9},{9,8},{10,11... | collective-permute-start | bytes 1572872 | tf_op jit(solution)/shard_map/ppermute | solution.py:657
  473.2 18.2 %collective-permute-start.66 = (f32[2,128,256]{2,1,0:T(8,128)S(1)}, f32[2,128,256]{2,1,0:T(8,128)S(1)}, u32[]{:S(2)}, u32[]{:S(2)}) collective-permute-start(f32[2,128,256]{2,1,0:T(8,128)S(1)} %get-tuple-element.120.refs_3_), channel_id=1, source_target_pairs={{0,2},{1,3},{2,0},{3,1},{4,6},{5,7},{6,4},{7,5},{8,10},{9,11},{10,... | collective-permute-start | bytes 786440 | tf_op jit(solution)/shard_map/ppermute | solution.py:727
  (86 other events, 632.9 us)
